TPU v7x, 512 devices: a whole 4x8x8 slice. The times are simulated.
512 devices in a mesh: wide: 64 (over y, z_lo, x), tp: 8 (over z_hi, core).
Axes of the slice: x: 4, y: 8, z: 8 (z_hi: 4, z_lo: 2; z = z_hi * 2 + z_lo), core: 2. Of those that a mesh axis runs over, the one named last changes fastest.
Arguments:
- query: bfloat16 [256, 2048], P('wide', 'tp'), may hold values from -120 to 120
- key_cache: bfloat16 [256, 128, 1024], P('wide', None, 'tp'), may hold values from -6 to 6
- value_cache: bfloat16 [256, 128, 1024], P('wide', None, 'tp'), may hold values from -6 to 6
- new_key: bfloat16 [256, 1024], P('wide', 'tp'), may hold values from -6 to 6
- new_value: bfloat16 [256, 1024], P('wide', 'tp'), may hold values from -6 to 6
- cache_lengths: int32 [256], P('wide'), may hold values from 1 to 128
- out_weight: bfloat16 [2048, 4096], P('tp'), may hold values from -0.125 to 0.125
- delta_index: int32 [64], P('wide'), may hold values from 0 to 63
- delta_values: bfloat16 [64, 1024, 128], P('wide', 'tp'), may hold values from -0.5 to 0.5
- fin_route: int32 [4096, 1], P('wide'), may hold values from 0 to 63; in each aligned block of 64 rows (0 to 63, 64 to 127, ...) at most 2 rows name the same one
- fin_lengths: int32 [4096], P('wide'), may hold values from 1 to 8
- fin_rows: bfloat16 [4096, 8, 8192], P('wide', None, 'tp'), may hold values from -6 to 6
- reward_query: bfloat16 [8192, 512], P('tp'), may hold values from -0.0625 to 0.0625
- rubric_keys: bfloat16 [64, 1024, 128], P('wide'), may hold values from -240 to 240
- rubric_values: bfloat16 [64, 1024, 128], P('wide'), may hold values from -6 to 6
- score_weight: bfloat16 [512], replicated, may hold values from -3 to 3
Outputs:
- decoded: bfloat16 [256, 4096], P('wide', 'tp')
- rewards: float32 [4096], P('wide')
Inputs may be any that keep to these rules, and one draw needn't show every extreme that they name: `fin_route`: in the rows of one wide index no reward group is named more than 2 times.
All inputs are finite; a program needn't handle non-finite values.
Results may differ from a plain program's by a relative error of at most 0.0095.
Values may be sent and summed in bfloat16 or wider, within the bound.
No kernel may reach another device: no remote copies, remote signals or barrier semaphores. Data moves between devices by JAX's collectives and lax.ppermute only.
A program may use at most 64 MiB of HBM per device.

v0:
```python
import math

import jax
import jax.numpy as jnp
from jax import lax
from jax.sharding import PartitionSpec as P

HD = 128
BLK = 128
RD = 8192
RHEADS = 4


def attend_local(query, key_cache, value_cache, new_key, new_value, cache_lengths):
    seq_count = query.shape[0]
    head_count = query.shape[1] // HD
    kv_count = key_cache.shape[2] // HD
    group_size = head_count // kv_count
    positions = key_cache.shape[1]
    queries = query.reshape(seq_count, kv_count, group_size, HD)
    cached_keys = key_cache.reshape(seq_count, positions, kv_count, HD)
    cached_values = value_cache.reshape(seq_count, positions, kv_count, HD)
    fresh_keys = new_key.reshape(seq_count, kv_count, HD)
    fresh_values = new_value.reshape(seq_count, kv_count, HD)
    scale_factor = 1.0 / math.sqrt(HD)
    scores = (
        jnp.einsum("skgd,slkd->skgl", queries, cached_keys, preferred_element_type=jnp.float32)
        * scale_factor
    )
    own_score = (
        jnp.einsum("skgd,skd->skg", queries, fresh_keys, preferred_element_type=jnp.float32)
        * scale_factor
    )
    valid = jnp.arange(positions)[None, :] < cache_lengths[:, None]
    scores = jnp.where(valid[:, None, None, :], scores, -jnp.inf)
    highest = jnp.maximum(jnp.max(scores, axis=-1), own_score)
    weights = jnp.exp(scores - highest[..., None])
    own_weight = jnp.exp(own_score - highest)
    denominator = jnp.sum(weights, axis=-1) + own_weight
    probs = (weights / denominator[..., None]).astype(jnp.bfloat16)
    own_prob = (own_weight / denominator).astype(jnp.bfloat16)
    mixed = jnp.einsum("skgl,slkd->skgd", probs, cached_values, preferred_element_type=jnp.float32)
    mixed = mixed + jnp.einsum(
        "skg,skd->skgd", own_prob, fresh_values, preferred_element_type=jnp.float32
    )
    return mixed.astype(jnp.bfloat16).reshape(seq_count, head_count * HD)


def finish_scores(projected, squares, lengths_float, keys_float, values_local, scorer):
    slot_rows = projected.shape[0]
    row_len = projected.shape[1]
    normed = projected * lax.rsqrt(squares / RD + 1e-05)[..., None]
    heads = normed.reshape(slot_rows, row_len, RHEADS, HD)
    scores = jnp.einsum(
        "nthd,pd->nthp", heads, keys_float, precision=lax.Precision.HIGHEST
    ) / math.sqrt(HD)
    highest = jnp.max(scores, axis=-1, keepdims=True)
    weights = jnp.exp(scores - highest)
    probs = (weights / jnp.sum(weights, axis=-1, keepdims=True)).astype(jnp.bfloat16)
    context = jnp.einsum("nthp,pd->nthd", probs, values_local, preferred_element_type=jnp.float32)
    context = context.reshape(slot_rows, row_len, RHEADS * HD)
    token_score = jnp.sum(jax.nn.silu(context) * scorer, axis=-1)
    mask = jnp.arange(row_len)[None, :].astype(jnp.float32) < lengths_float[:, None]
    return jnp.sum(jnp.where(mask, token_score, 0.0), axis=-1) / jnp.maximum(lengths_float, 1.0)


def per_device(
    query,
    key_cache,
    value_cache,
    new_key,
    new_value,
    cache_lengths,
    out_weight,
    delta_index,
    delta_values,
    fin_route,
    fin_lengths,
    fin_rows,
    reward_query,
    rubric_keys,
    rubric_values,
    score_weight,
):
    attn = attend_local(query, key_cache, value_cache, new_key, new_value, cache_lengths)
    seq_count = attn.shape[0]
    row_blocks = attn.shape[1] // BLK
    col_blocks = out_weight.shape[1] // BLK
    wide_count = lax.axis_size("wide")
    block_ids = lax.all_gather(delta_index, "wide", axis=0, tiled=True)
    local_rows = attn.reshape(seq_count, row_blocks, BLK)
    row_pick = (block_ids[:, None] // col_blocks == jnp.arange(row_blocks)[None, :]).astype(
        jnp.bfloat16
    )
    col_pick = (block_ids[:, None] % col_blocks == jnp.arange(col_blocks)[None, :]).astype(
        jnp.float32
    )
    chosen = jnp.einsum(
        "kr,srd->ksd", row_pick, local_rows, preferred_element_type=jnp.float32
    ).astype(jnp.bfloat16)
    products = jnp.einsum(
        "ksd,kde->kse",
        chosen,
        lax.all_gather(delta_values, "wide", axis=0, tiled=True),
        preferred_element_type=jnp.float32,
    )
    extra = jnp.einsum("kc,kse->sce", col_pick, products, precision=lax.Precision.HIGHEST)
    partial_out = jnp.dot(attn, out_weight, preferred_element_type=jnp.float32) + extra.reshape(
        seq_count, col_blocks * BLK
    )
    decoded = lax.psum_scatter(partial_out, "tp", scatter_dimension=1, tiled=True).astype(
        jnp.bfloat16
    )
    finished = fin_rows.shape[0]
    row_len = fin_rows.shape[1]
    features = fin_rows.shape[2]
    capacity = max(2, 3 * finished // (2 * wide_count))
    slot_count = wide_count * capacity
    target = fin_route[:, 0]
    order = jnp.arange(finished)
    same_group = target[:, None] == target[None, :]
    earlier = order[:, None] > order[None, :]
    ranking = jnp.sum(jnp.logical_and(same_group, earlier).astype(jnp.int32), axis=1)
    slot_index = target * capacity + ranking
    placement = jnp.arange(slot_count)[:, None] == slot_index[None, :]
    send_rows = jnp.dot(
        placement.astype(jnp.bfloat16),
        fin_rows.reshape(finished, row_len * features),
        preferred_element_type=jnp.float32,
    )
    send_rows = send_rows.astype(jnp.bfloat16).reshape(wide_count, capacity, row_len, features)
    send_lengths = jnp.dot(
        placement.astype(jnp.float32),
        fin_lengths.astype(jnp.float32),
        precision=lax.Precision.HIGHEST,
    )
    send_lengths = send_lengths.astype(jnp.bfloat16).reshape(wide_count, capacity)
    rows_in, lengths_in = (
        lax.all_to_all(send_rows, "wide", split_axis=0, concat_axis=0, tiled=True),
        lax.all_to_all(send_lengths, "wide", split_axis=0, concat_axis=0, tiled=True),
    )
    projected = jnp.einsum(
        "wcrf,fq->wcrq", rows_in, reward_query, preferred_element_type=jnp.float32
    )
    squares = jnp.sum(jnp.square(rows_in.astype(jnp.float32)), axis=-1)
    scorer = score_weight.astype(jnp.float32)
    keys_float = rubric_keys[0].astype(jnp.float32)
    values_local = rubric_values[0]
    projected, squares = lax.psum((projected, squares), "tp")

    def grade_block(item):
        block_proj, block_squares, block_lengths = item
        return finish_scores(
            block_proj, block_squares, block_lengths, keys_float, values_local, scorer
        )

    graded = lax.map(grade_block, (projected, squares, lengths_in.astype(jnp.float32)))
    returned = lax.all_to_all(graded, "wide", split_axis=0, concat_axis=0, tiled=True)
    rewards = jnp.sum(placement.astype(jnp.float32) * returned.reshape(slot_count)[:, None], axis=0)
    return (decoded, rewards)


def solution(mesh):
    in_specs = (
        P("wide", "tp"),
        P("wide", None, "tp"),
        P("wide", None, "tp"),
        P("wide", "tp"),
        P("wide", "tp"),
        P("wide"),
        P("tp", None),
        P("wide"),
        P("wide", "tp", None),
        P("wide", None),
        P("wide"),
        P("wide", None, "tp"),
        P("tp", None),
        P("wide", None, None),
        P("wide", None, None),
        P(),
    )
    out_specs = (P("wide", "tp"), P("wide"))
    return jax.shard_map(
        per_device, mesh=mesh, in_specs=in_specs, out_specs=out_specs, check_vma=False
    )
```

profile of v0, /device:TPU:1, one launch (start us, length us, event | category | flops | bytes accessed | tf_op | source)
XLA Modules:
  0.0 705.5 jit_solution(9121764070540982603)
XLA Ops:
  9.7 1.8 copy.58
  12.3 2.8 copy.59
  15.1 13.3 %all-to-all-start.1 = ((bf16[64,2,8,1024]{3,2,1,0:T(8,128)(2,1)}), bf16[64,2,8,1024]{3,2,1,0:T(8,128)(2,1)}, u32[]{:S(2)}, u32[]{:S(2)}) async-start(bf16[64,2,8,1024]{3,2,1,0:T(8,128)(2,1)} %bitcast.99), calls=%async_computation.1 | async-start | bytes 4194304 | tf_op jit(solution)/shard_map/all_to_all | solution.py:139
  32.9 50.5 %all-reduce = s32[64]{0:T(128)S(1)} all-reduce(s32[64]{0:T(128)S(1)} %dynamic-update-slice), channel_id=1, replica_groups=mesh['wide'=64,'tp'=8] {'wide'}, use_global_device_ids=true, to_apply=%add | all-reduce | flops 64 | bytes 512
  83.9 8.2 %all-to-all-start = ((bf16[64,1,2]{2,1,0:T(2,128)(2,1)}), bf16[64,1,2]{2,1,0:T(2,128)(2,1)S(1)}, u32[]{:S(2)}, u32[]{:S(2)}) async-start(bf16[64,1,2]{2,1,0:T(2,128)(2,1)} %all_to_all.20), calls=%async_computation | async-start | bytes 65536 | tf_op jit(solution)/shard_map/all_to_all | solution.py:140
  92.2 4.4 fusion.17
  98.1 3.4 all-to-all-done
  101.6 198.6 %all-gather.2.cloned.1.call-done = bf16[64,128,128]{2,1,0:T(8,128)(2,1)} async-done(((bf16[1,128,128]{2,1,0:T(8,128)(2,1)}), bf16[64,128,128]{2,1,0:T(8,128)(2,1)}) %all-gather.2.cloned.1.call-update) | async-done | bytes 2097168 | tf_op jit(solution)/shard_map/all_gather | solution.py:104
  300.2 2.2 fusion.20
  303.0 1.9 copy.54
  304.9 2.1 multiply_reduce_fusion.1
  307.1 66.4 %psum.15 = f32[64,2,8]{2,1,0:T(2,128)S(1)} all-reduce(f32[64,2,8]{2,1,0:T(2,128)S(1)} %multiply_reduce_fusion.1), channel_id=1, replica_groups=mesh['wide'=64,'tp'=8] {'tp'}, use_global_device_ids=true, to_apply=%region_6.7 | all-reduce | flops 1024 | bytes 8192 | tf_op jit(solution)/shard_map/psum | solution.py:149
  373.5 305.6 %while.10 = (s32[]{:T(128)}, f32[64,2]{1,0:T(8,128)}, f32[64,2]{1,0:T(8,128)S(1)}, f32[64,2,8,512]{3,2,1,0:T(8,128)}, f32[64,2,8]{2,1,0:T(2,128)S(1)}, /*index=5...) while((s32[]{:T(128)}, f32[64,2]{1,0:T(8,128)}, ...), condition=%wide.region_12.13_spmd, body=%wide.region_7.12_spmd.sunk | while | flops 117826640 | bytes 1870921 | solution.py:157
  416.6 1.5 convolution_multiply_fusion.3
  454.7 1.5 convolution_multiply_fusion.3
  469.1 1.5 convolution_multiply_fusion.3
  473.8 1.5 convolution_multiply_fusion.3
  478.6 1.5 convolution_multiply_fusion.3
  483.4 1.5 convolution_multiply_fusion.3
  488.2 1.5 convolution_multiply_fusion.3
  531.2 1.5 convolution_multiply_fusion.3
  679.2 7.5 %all-to-all-start.2 = ((f32[64,1,2]{2,1,0:T(1,128)}), f32[64,1,2]{2,1,0:T(1,128)S(1)}, u32[]{:S(2)}, u32[]{:S(2)}) async-start(f32[64,1,2]{2,1,0:T(1,128)} %bitcast.32), calls=%async_computation.2 | async-start | bytes 65536 | tf_op jit(solution)/shard_map/all_to_all | solution.py:158
  686.8 1.7 copy.55
  688.4 7.6 %all-to-all-done.2 = f32[64,1,2]{2,1,0:T(1,128)S(1)} async-done(((f32[64,1,2]{2,1,0:T(1,128)}), f32[64,1,2]{2,1,0:T(1,128)S(1)}, u32[]{:S(2)}, u32[]{:S(2)}) %all-to-all-start.2) | async-done | bytes 544 | tf_op jit(solution)/shard_map/all_to_all | solution.py:158
  (630 shorter events, 303.4 us)
Async XLA Ops:
  8.0 294.6 %copy-start = (bf16[256,4096]{1,0:T(8,128)(2,1)S(1)}, bf16[256,4096]{1,0:T(8,128)(2,1)}, u32[]{:S(2)}) copy-start(bf16[256,4096]{1,0:T(8,128)(2,1)} %param.24) | copy-start | bytes 6291460
  15.1 14.8 %copy-start.3 = (bf16[4,256]{1,0:T(4,128)(2,1)S(1)}, bf16[4,256]{1,0:T(4,128)(2,1)}, u32[]{:S(2)}) copy-start(bf16[4,256]{1,0:T(4,128)(2,1)} %param.18) | copy-start | bytes 6148
  15.1 14.8 %copy-start.9 = (s32[64]{0:T(128)S(1)}, s32[64]{0:T(128)}, u32[]{:S(2)}) copy-start(s32[64]{0:T(128)} %param.28) | copy-start | bytes 772
  15.1 68.4 %copy-start.10 = (s32[4]{0:T(128)S(1)}, s32[4]{0:T(128)}, u32[]{:S(2)}) copy-start(s32[4]{0:T(128)} %param.23) | copy-start | bytes 52
  15.1 68.4 %copy-start.8 = (bf16[4,128]{1,0:T(4,128)(2,1)S(1)}, bf16[4,128]{1,0:T(4,128)(2,1)}, u32[]{:S(2)}) copy-start(bf16[4,128]{1,0:T(4,128)(2,1)} %param.21) | copy-start | bytes 3076
  15.1 68.6 %copy-start.2 = (bf16[4,128,128]{2,1,0:T(8,128)(2,1)S(1)}, bf16[4,128,128]{2,1,0:T(8,128)(2,1)}, u32[]{:S(2)}) copy-start(bf16[4,128,128]{2,1,0:T(8,128)(2,1)} %param.19) | copy-start | bytes 393220
  15.1 68.8 %all-to-all-start.1 = ((bf16[64,2,8,1024]{3,2,1,0:T(8,128)(2,1)}), bf16[64,2,8,1024]{3,2,1,0:T(8,128)(2,1)}, u32[]{:S(2)}, u32[]{:S(2)}) async-start(bf16[64,2,8,1024]{3,2,1,0:T(8,128)(2,1)} %bitcast.99), calls=%async_computation.1 | async-start | bytes 4194304 | tf_op jit(solution)/shard_map/all_to_all | solution.py:139
  28.5 271.7 %all-gather.2.cloned.1.call-start = ((), (), s32[]{:S(2)}) async-start(), calls=%async_computation.4 | async-start | bytes 2129920 | tf_op jit(solution)/shard_map/all_gather | solution.py:104
  83.9 17.5 %all-to-all-start = ((bf16[64,1,2]{2,1,0:T(2,128)(2,1)}), bf16[64,1,2]{2,1,0:T(2,128)(2,1)S(1)}, u32[]{:S(2)}, u32[]{:S(2)}) async-start(bf16[64,1,2]{2,1,0:T(2,128)(2,1)} %all_to_all.20), calls=%async_computation | async-start | bytes 65536 | tf_op jit(solution)/shard_map/all_to_all | solution.py:140
  92.1 281.4 %all-reduce.3.cloned.1.call-start = ((), (), s32[]{:S(2)}) async-start(), calls=%async_computation.5 | async-start | bytes 4194304 | tf_op jit(solution)/shard_map/psum | solution.py:149
  96.6 0.7 copy-start.4
  96.6 0.9 copy-start.7
  96.6 1.1 copy-start.1
  96.6 1.4 copy-start.5
  96.7 590.1 %reduce-scatter.4.cloned.1.call-start = ((), (), s32[]{:S(2)}) async-start(), calls=%async_computation.6 | async-start | bytes 2359296
  304.9 68.6 %copy-start.6 = (bf16[1,1024,128]{2,1,0:T(8,128)(2,1)S(1)}, bf16[1,1024,128]{2,1,0:T(8,128)(2,1)}, u32[]{:S(2)}) copy-start(bf16[1,1024,128]{2,1,0:T(8,128)(2,1)} %param.32) | copy-start | bytes 786436
  679.2 16.8 %all-to-all-start.2 = ((f32[64,1,2]{2,1,0:T(1,128)}), f32[64,1,2]{2,1,0:T(1,128)S(1)}, u32[]{:S(2)}, u32[]{:S(2)}) async-start(f32[64,1,2]{2,1,0:T(1,128)} %bitcast.32), calls=%async_computation.2 | async-start | bytes 65536 | tf_op jit(solution)/shard_map/all_to_all | solution.py:158
Sparse Core Ops, SparseCore 0:
  31.4 268.7 all-gather.1
Sparse Core Ops, SparseCore 1:
  96.7 97.6 all-reduce.2
  373.6 43.6 reduce-scatter.3
where the time goes:
time: 715 us; the launch traced here: 706 us
  waiting for transfers between devices  210 us (29%)
  matrix products  124 us (17%)
  blocking collectives  117 us (16%)
  other arithmetic  111 us (16%)
  local copies, waits for them, and re-layouts  95.5 us (13%)
  starting transfers between devices  29.2 us (4%)
  between operations  16.3 us (2%)
    all_gather x1, waiting for transfers between devices, per_device(): lax.all_gather(delta_values, 'wide', axis=0, tiled=True)  199 us
    dot_general x64, matrix products, finish_scores(): jnp.einsum('nthd,pd->nthp', heads, keys_float, precision=lax.Precision.HI...  93.5 us
    sub x64, other arithmetic, finish_scores(): weights = jnp.exp(scores - highest)  92.4 us
    dynamic_update_slice x64, local copies, waits for them, and re-layouts, per_device(): lax.map(grade_block, (projected, squares, lengths_in.astype(jnp.float32)))  82.6 us
    psum x1, blocking collectives, per_device(): projected, squares = lax.psum((projected, squares), 'tp')  66.4 us
    unnamed x1, blocking collectives  50.5 us
    dot_general x64, matrix products, finish_scores(): jnp.einsum('nthp,pd->nthd', probs, values_local, preferred_element_type=j...  21.8 us
  transfers between devices with their start and end apart: 6, of which 3 were waited for; matrix products, arithmetic and copies ran while one was open for 45% of the time, Pallas kernels for 0%

commit v1 on v0

v1 whole, which is shorter than its diff:
```python
import functools
import math

import jax
import jax.numpy as jnp
from jax import lax
from jax.experimental import pallas as pl
from jax.experimental.pallas import tpu as pltpu
from jax.sharding import PartitionSpec as P

HD = 128
RD = 8192
CAP = 2
F32 = jnp.float32
BF16 = jnp.bfloat16


def split3(x):
    high = x.astype(BF16)
    rest = x - high.astype(F32)
    mid = rest.astype(BF16)
    low = (rest - mid.astype(F32)).astype(BF16)
    return high, mid, low


def mm(a, b):
    return jnp.dot(a, b, preferred_element_type=F32)


def mm_t(a, b):
    return lax.dot_general(a, b, (((1,), (1,)), ((), ())), preferred_element_type=F32)


def rows_at(first, count, stride):
    return pl.ds(first, count, stride=stride)


def whole(shape):
    return pl.BlockSpec(shape, lambda *_: (0,) * len(shape))


def project_kernel(row_len, per_token, rows_ref, wq_ref, out_ref, acc_ref, sq_ref):
    step = pl.program_id(0)
    rows = rows_ref[...]
    chunk = rows.shape[0] // row_len
    heads = wq_ref.shape[1] // HD
    seqs = (per_token - 8) // heads
    many = rows.shape[0]
    product = mm(rows, wq_ref[...])
    for h in range(heads):
        acc_ref[h * many : (h + 1) * many, :] = product[:, h * HD : (h + 1) * HD]
    wide_rows = rows.astype(F32)
    sums = jnp.sum(wide_rows * wide_rows, axis=1, keepdims=True)
    sq_ref[...] = jnp.broadcast_to(sums, sq_ref.shape)

    @pl.when(step == 0)
    def _():
        for t in range(row_len):
            out_ref[t * per_token + heads * seqs : (t + 1) * per_token, :] = jnp.zeros((8, HD), F32)

    base = pl.multiple_of(step * chunk, chunk)
    here = lax.broadcasted_iota(jnp.int32, (chunk, HD), 0) + step * chunk
    lane = lax.broadcasted_iota(jnp.int32, (chunk, HD), 1)
    for t in range(row_len):
        for h in range(heads):
            out_ref[pl.ds(t * per_token + h * seqs + base, chunk), :] = acc_ref[
                rows_at(h * many + t, chunk, row_len), :
            ]
        picked = jnp.where(here == lane, sq_ref[rows_at(t, chunk, row_len), :], 0.0)
        tail = slice(t * per_token + heads * seqs, (t + 1) * per_token)
        out_ref[tail, :] += jnp.sum(picked, axis=0, keepdims=True)


def decode_kernel(
    lens_ref, q_ref, k_ref, v_ref, nk_ref, nv_ref, w_ref, route_ref, attn_ref, out_ref, place_ref
):
    seqs = q_ref.shape[0]
    rows = 2 * seqs
    scale = 1.0 / math.sqrt(HD)
    q = q_ref[...].astype(F32)
    queries = jnp.concatenate([q[:, :HD], q[:, HD:]], axis=0)
    nk = nk_ref[...].astype(F32)
    nv = nv_ref[...].astype(F32)
    own_key = jnp.concatenate([nk, nk], axis=0)
    own_value = jnp.concatenate([nv, nv], axis=0)
    row = lax.broadcasted_iota(jnp.int32, (rows, HD), 0) % seqs
    place_in = lax.broadcasted_iota(jnp.int32, (rows, HD), 1)
    queries16 = queries.astype(BF16)
    scores = jnp.zeros((rows, HD), F32)
    length = jnp.zeros((rows, HD), jnp.int32)
    for s in range(seqs):
        scores = jnp.where(row == s, mm_t(queries16, k_ref[s]), scores)
        length = jnp.where(row == s, lens_ref[s], length)
    scores = jnp.where(place_in < length, scores * scale, -jnp.inf)
    own_score = jnp.sum(queries * own_key, axis=1, keepdims=True) * scale
    highest = jnp.maximum(jnp.max(scores, axis=1, keepdims=True), own_score)
    weights = jnp.exp(scores - highest)
    own_weight = jnp.exp(own_score - highest)
    denominator = jnp.sum(weights, axis=1, keepdims=True) + own_weight
    probs = (weights / denominator).astype(BF16)
    own_prob = (own_weight / denominator).astype(BF16).astype(F32)
    mixed = jnp.zeros((rows, HD), F32)
    for s in range(seqs):
        mixed = jnp.where(row == s, mm(probs, v_ref[s]), mixed)
    attn = (mixed + own_prob * own_value).astype(BF16).astype(F32)
    attn_ref[...] = attn
    turned = jnp.concatenate([attn[seqs:], attn[:seqs]], axis=0)
    both = jnp.concatenate([attn, turned], axis=1).astype(BF16)
    blocks = w_ref.shape[1] // HD
    for first in range(0, blocks, 4):
        part = mm(both, w_ref[:, first * HD : (first + 4) * HD])
        for c in range(4):
            out_ref[(first + c) * rows : (first + c + 1) * rows, :] = part[:, c * HD : (c + 1) * HD]
    slots = place_ref.shape[0]
    groups = slots // CAP
    down = lax.broadcasted_iota(jnp.int32, (HD, HD), 0)
    across = lax.broadcasted_iota(jnp.int32, (HD, HD), 1)
    target = jnp.broadcast_to(route_ref[...], (HD, HD))
    target_down = jnp.sum(jnp.where(down == across, target, 0.0), axis=1, keepdims=True)
    earlier = jnp.where(jnp.logical_and(target == target_down, down < across), 1.0, 0.0)
    rank = jnp.sum(earlier, axis=0, keepdims=True)
    slot = lax.broadcasted_iota(jnp.int32, (slots, HD), 0)
    group = (slot % groups).astype(F32)
    order = (slot // groups).astype(F32)
    held = jnp.logical_and(route_ref[...] == group, rank == order)
    place_ref[...] = jnp.where(held, 1.0, 0.0).astype(BF16)


def place_kernel(sources, per_token, heads, x_ref, attn_ref, place_ref, out_ref):
    seqs = (per_token - 8) // heads
    groups = place_ref.shape[0] // CAP
    each = out_ref.shape[0] // groups
    total = x_ref[0:per_token, :]
    for k in range(1, sources):
        total = total + x_ref[k * per_token : (k + 1) * per_token, :]
    squares = total[heads * seqs : heads * seqs + 1, :]
    inverse = lax.rsqrt(squares / RD + 1e-05)
    down = lax.broadcasted_iota(jnp.int32, (seqs, HD), 0)
    across = lax.broadcasted_iota(jnp.int32, (seqs, HD), 1)
    factor = jnp.sum(jnp.where(down == across, inverse, 0.0), axis=1, keepdims=True)
    normed = jnp.concatenate(
        [total[h * seqs : (h + 1) * seqs, :] * factor for h in range(heads)], axis=1
    )
    if seqs < HD:
        normed = jnp.concatenate([normed, jnp.zeros((HD - seqs, heads * HD), F32)], axis=0)
    place = place_ref[...]
    high, mid, low = split3(normed)
    placed = (mm(place, low) + mm(place, mid)) + mm(place, high)
    for r in range(CAP):
        for h in range(heads):
            out_ref[rows_at(r * heads + h, groups, each), :] = placed[
                r * groups : (r + 1) * groups, h * HD : (h + 1) * HD
            ]
    attn = attn_ref[...]
    for g in range(groups):
        out_ref[g * each + CAP * heads : (g + 1) * each, :] = attn


def score_kernel(heads, index_ref, x_ref, keys_ref, values_ref, weight_ref, delta_ref, out_ref):
    tile = CAP * heads
    senders = x_ref.shape[0]
    keys = keys_ref[...]
    keys3 = jnp.concatenate([keys, keys, keys], axis=1)
    values = values_ref[...]
    delta = delta_ref[...]
    weight = weight_ref[...].astype(F32)
    weight = jnp.concatenate([weight] * CAP, axis=0)[None]
    scale = 1.0 / math.sqrt(HD)
    block = index_ref[0]
    columns = 32
    row_block = block // columns
    column = (block % columns).astype(F32)
    at_once = min(16, senders)
    row = lax.broadcasted_iota(jnp.int32, (at_once, tile, HD), 1)
    lane = lax.broadcasted_iota(jnp.int32, (at_once, tile, HD), 2)
    for first in range(0, senders, at_once):
        x = x_ref[first : first + at_once]
        pieces = split3(x[:, :tile, :].reshape(at_once * tile, HD))
        scores = mm_t(jnp.concatenate(pieces, axis=1), keys3) * scale
        highest = jnp.max(scores, axis=1, keepdims=True)
        weights = jnp.exp(scores - highest)
        probs = (weights * (1.0 / jnp.sum(weights, axis=1, keepdims=True))).astype(BF16)
        context = mm(probs, values)
        gated = context / (1.0 + jnp.exp(-context))
        terms = gated.reshape(at_once, tile, HD) * weight
        by_head = jnp.sum(terms, axis=2, keepdims=True)
        attn = x[:, tile:, :].reshape(at_once * tile, HD).astype(BF16)
        product = mm(attn, delta).reshape(at_once, tile, HD)
        seqs = tile // 2
        turned = jnp.concatenate([product[:, seqs:], product[:, :seqs]], axis=1)
        result = jnp.where(row_block == 0, product, turned)
        result = jnp.where(row < seqs, result, 0.0)
        for r in range(CAP):
            mine = jnp.logical_and(row >= r * heads, row < (r + 1) * heads)
            score = jnp.sum(jnp.where(mine, by_head, 0.0), axis=1, keepdims=True)
            result = jnp.where(jnp.logical_and(row == seqs, lane == r), score, result)
        result = jnp.where(jnp.logical_and(row == seqs, lane == CAP), column, result)
        out_ref[first : first + at_once] = result


def merge_kernel(tile, x_ref, partial_ref, place_ref, out_ref):
    senders = x_ref.shape[0] // tile
    blocks = partial_ref.shape[0] // tile
    seqs = tile // 2
    extra = x_ref[rows_at(seqs, senders, tile), :]
    column = extra[:, CAP : CAP + 1]
    pieces = split3(
        jnp.concatenate([x_ref[rows_at(s, senders, tile), :] for s in range(seqs)], axis=1)
    )
    down = lax.broadcasted_iota(jnp.int32, (senders, senders), 0)
    across = lax.broadcasted_iota(jnp.int32, (senders, senders), 1)
    column_across = jnp.sum(
        jnp.where(down == across, jnp.broadcast_to(column, (senders, senders)), 0.0),
        axis=0,
        keepdims=True,
    )
    wanted = lax.broadcasted_iota(jnp.int32, (blocks, senders), 0).astype(F32)
    pick = jnp.where(wanted == column_across, 1.0, 0.0).astype(BF16)
    high, mid, low = pieces
    added = (mm(pick, low) + mm(pick, mid)) + mm(pick, high)
    out_ref[...] = partial_ref[...]
    for s in range(seqs):
        where = rows_at(s, blocks, tile)
        out_ref[where, :] = partial_ref[where, :] + added[:, s * HD : (s + 1) * HD]
    place = place_ref[...].astype(F32)
    score = jnp.concatenate([extra[:, r : r + 1] for r in range(CAP)], axis=0)
    back = jnp.sum(place * score, axis=0, keepdims=True)
    shards = 8
    out_ref[rows_at(seqs, shards, blocks // shards * tile), :] = jnp.broadcast_to(
        back, (shards, HD)
    )


def final_kernel(tile, x_ref, length_ref, decoded_ref, rewards_ref):
    seqs = tile // 2
    total = x_ref[0]
    for k in range(1, x_ref.shape[0]):
        total = total + x_ref[k]
    for c in range(total.shape[0] // tile):
        decoded_ref[:, c * HD : (c + 1) * HD] = total[c * tile : c * tile + seqs, :].astype(BF16)
    length = length_ref[...]
    count = rewards_ref.shape[1]
    reward = jnp.zeros((1, HD), F32)
    for k in range(x_ref.shape[0]):
        reward = reward + jnp.where(length > k, x_ref[k, seqs : seqs + 1, :], 0.0)
    rewards_ref[...] = (reward / length)[:, :count]


def per_device(
    query,
    key_cache,
    value_cache,
    new_key,
    new_value,
    cache_lengths,
    out_weight,
    delta_index,
    delta_values,
    fin_route,
    fin_lengths,
    fin_rows,
    reward_query,
    rubric_keys,
    rubric_values,
    score_weight,
):
    wide_count = lax.axis_size("wide")
    tp_count = lax.axis_size("tp")
    finished, row_len, features = fin_rows.shape
    heads = reward_query.shape[1] // HD
    seq_count = query.shape[0]
    tile = 2 * seq_count
    blocks = out_weight.shape[1] // HD
    slots = CAP * wide_count
    per_token = heads * finished + 8
    smem = pl.BlockSpec(memory_space=pltpu.SMEM)
    chunks = 4 if finished % 32 == 0 else 1

    rows = fin_rows.reshape(finished * row_len, features)
    chunk_rows = finished * row_len // chunks
    partial_tokens = pl.pallas_call(
        functools.partial(project_kernel, row_len, per_token),
        grid=(chunks,),
        in_specs=[
            pl.BlockSpec((chunk_rows, features), lambda m: (m, 0)),
            whole(reward_query.shape),
        ],
        out_specs=whole((row_len * per_token, HD)),
        out_shape=jax.ShapeDtypeStruct((row_len * per_token, HD), F32),
        scratch_shapes=[
            pltpu.VMEM((heads * chunk_rows, HD), F32),
            pltpu.VMEM((chunk_rows, HD), F32),
        ],
        name="project",
    )(rows, reward_query)
    summed_tokens = lax.all_to_all(
        partial_tokens.reshape(tp_count, per_token, HD), "tp", split_axis=0, concat_axis=0, tiled=True
    ).reshape(tp_count * per_token, HD)

    pad = ((0, 0), (0, HD - finished))
    route = jnp.pad(fin_route.reshape(1, finished).astype(F32), pad, constant_values=-1.0)
    lengths = jnp.pad(fin_lengths.reshape(1, finished).astype(F32), pad, constant_values=1.0)
    attn, partial_out, place = pl.pallas_call(
        decode_kernel,
        in_specs=[smem]
        + [
            whole(a.shape)
            for a in (query, key_cache, value_cache, new_key, new_value, out_weight, route)
        ],
        out_specs=[whole((tile, HD)), whole((blocks * tile, HD)), whole((slots, HD))],
        out_shape=[
            jax.ShapeDtypeStruct((tile, HD), F32),
            jax.ShapeDtypeStruct((blocks * tile, HD), F32),
            jax.ShapeDtypeStruct((slots, HD), BF16),
        ],
        grid=(1,),
        name="decode",
    )(
        cache_lengths,
        query,
        key_cache,
        value_cache,
        new_key,
        new_value,
        out_weight,
        route,
    )

    each = CAP * heads + tile
    outgoing = pl.pallas_call(
        functools.partial(place_kernel, tp_count, per_token, heads),
        in_specs=[
            whole((tp_count * per_token, HD)),
            whole((tile, HD)),
            whole((slots, HD)),
        ],
        out_specs=whole((wide_count * each, HD)),
        out_shape=jax.ShapeDtypeStruct((wide_count * each, HD), F32),
        grid=(1,),
        name="place",
    )(summed_tokens, attn, place)
    received = lax.all_to_all(
        outgoing.reshape(wide_count, each, HD), "wide", split_axis=0, concat_axis=0, tiled=True
    )

    answers = pl.pallas_call(
        functools.partial(score_kernel, heads),
        in_specs=[
            smem,
            whole((wide_count, each, HD)),
            whole(rubric_keys.shape[1:]),
            whole(rubric_values.shape[1:]),
            whole((heads, HD)),
            whole(delta_values.shape[1:]),
        ],
        out_specs=whole((wide_count, tile, HD)),
        out_shape=jax.ShapeDtypeStruct((wide_count, tile, HD), F32),
        grid=(1,),
        name="score",
    )(
        delta_index,
        received,
        rubric_keys[0],
        rubric_values[0],
        score_weight.reshape(heads, HD),
        delta_values[0],
    )
    returned = lax.all_to_all(answers, "wide", split_axis=0, concat_axis=0, tiled=True)

    merged = pl.pallas_call(
        functools.partial(merge_kernel, tile),
        in_specs=[
            whole((wide_count * tile, HD)),
            whole((blocks * tile, HD)),
            whole((slots, HD)),
        ],
        out_specs=whole((blocks * tile, HD)),
        out_shape=jax.ShapeDtypeStruct((blocks * tile, HD), F32),
        grid=(1,),
        name="merge",
    )(returned.reshape(wide_count * tile, HD), partial_out, place)
    shares = lax.all_to_all(
        merged.reshape(tp_count, blocks // tp_count * tile, HD),
        "tp",
        split_axis=0,
        concat_axis=0,
        tiled=True,
    )

    decoded, rewards = pl.pallas_call(
        functools.partial(final_kernel, tile),
        in_specs=[whole(shares.shape), whole((1, HD))],
        out_specs=[whole((seq_count, blocks // tp_count * HD)), whole((1, finished))],
        out_shape=[
            jax.ShapeDtypeStruct((seq_count, blocks // tp_count * HD), BF16),
            jax.ShapeDtypeStruct((1, finished), F32),
        ],
        grid=(1,),
        name="final",
    )(shares, lengths)
    return decoded, rewards.reshape(finished)


def solution(mesh):
    in_specs = (
        P("wide", "tp"),
        P("wide", None, "tp"),
        P("wide", None, "tp"),
        P("wide", "tp"),
        P("wide", "tp"),
        P("wide"),
        P("tp", None),
        P("wide"),
        P("wide", "tp", None),
        P("wide", None),
        P("wide"),
        P("wide", None, "tp"),
        P("tp", None),
        P("wide", None, None),
        P("wide", None, None),
        P(),
    )
    out_specs = (P("wide", "tp"), P("wide"))
    return jax.shard_map(
        per_device, mesh=mesh, in_specs=in_specs, out_specs=out_specs, check_vma=False
    )
```

time: 715 us -> 119 us (0.17); the launches traced: 706 us -> 119 us
  waiting for transfers between devices: 210 us -> 41.1 us
  matrix products: 124 us -> 0 us
  other arithmetic: 111 us -> 0.01 us
  blocking collectives: 117 us -> 17.7 us
  local copies, waits for them, and re-layouts: 95.5 us -> 3.49 us
  Pallas kernels: 0 us -> 18.3 us
  between operations: 16.3 us -> 1.3 us
  starting transfers between devices: 29.2 us -> 36.7 us
    all_gather x1 -> x0, waiting for transfers between devices: 199 us -> none  [per_device(): lax.all_gather(delta_values, 'wide', axis=0, tiled=True)]
    dot_general x138 -> x0, matrix products: 124 us -> none  [the longest x64 93.5 us: finish_scores(): jnp.einsum('nthd,pd->nthp', heads, keys_float, precision=lax.Precision.HI...]
    sub x64 -> x0, other arithmetic: 92.4 us -> none  [finish_scores(): weights = jnp.exp(scores - highest)]
    dynamic_update_slice x64 -> x0, local copies, waits for them, and re-layouts: 82.6 us -> none  [per_device(): lax.map(grade_block, (projected, squares, lengths_in.astype(jnp.float32)))]
    psum x1 -> x0, blocking collectives: 66.4 us -> none  [per_device(): projected, squares = lax.psum((projected, squares), 'tp')]
    unnamed x1 -> x0, blocking collectives: 50.5 us -> none
    all_to_all x3, waiting for transfers between devices: 11 us -> 41.1 us  [the longest x1 18.4 us: per_device(): lax.all_to_all(partial_tokens.reshape(tp_count, per_token, HD), 'tp', spl...]
    pallas_call x0 -> x6, Pallas kernels: none -> 18.3 us  [the longest x1 4.75 us: per_device(): pl.pallas_call(functools.partial(score_kernel, heads), in_specs=[smem, wh...]
  transfers between devices with their start and end apart: 6 -> 3, of which waited for: 3 -> 3; matrix products, arithmetic and copies ran while one was open for 45% -> 1% of each run, Pallas kernels for 0% -> 3%
where the time goes in v1:
time: 119 us
  waiting for transfers between devices  41.1 us (35%)
  starting transfers between devices  36.7 us (31%)
  Pallas kernels  18.3 us (15%)
  blocking collectives  17.7 us (15%)
  local copies, waits for them, and re-layouts  3.49 us (3%)
  between operations  1.3 us (1%)
    all_to_all x1, waiting for transfers between devices, per_device(): lax.all_to_all(partial_tokens.reshape(tp_count, per_token, HD), 'tp', spl...  18.4 us
    all_to_all x1, starting transfers between devices, per_device(): lax.all_to_all(outgoing.reshape(wide_count, each, HD), 'wide', split_axis...  17.9 us
    all_to_all x1, blocking collectives, per_device(): lax.all_to_all(answers, 'wide', split_axis=0, concat_axis=0, tiled=True)  17.7 us
    all_to_all x1, waiting for transfers between devices, per_device(): lax.all_to_all(outgoing.reshape(wide_count, each, HD), 'wide', split_axis...  15.1 us
    all_to_all x1, starting transfers between devices, per_device(): lax.all_to_all(partial_tokens.reshape(tp_count, per_token, HD), 'tp', spl...  11.9 us
    all_to_all x1, waiting for transfers between devices, per_device(): lax.all_to_all(merged.reshape(tp_count, blocks // tp_count * tile, HD), '...  7.52 us
    all_to_all x1, starting transfers between devices, per_device(): lax.all_to_all(merged.reshape(tp_count, blocks // tp_count * tile, HD), '...  6.81 us
    pallas_call x1, Pallas kernels, per_device(): pl.pallas_call(functools.partial(score_kernel, heads), in_specs=[smem, wh...  4.75 us
  transfers between devices with their start and end apart: 3, of which 3 were waited for; matrix products, arithmetic and copies ran while one was open for 1% of the time, Pallas kernels for 3%

profile of v1, /device:TPU:1, one launch (start us, length us, event | category | flops | bytes accessed | tf_op | source)
XLA Modules:
  0.0 118.5 jit_solution(15472155711329313788)
XLA Ops:
  0.6 4.5 %project.1 = f32[2112,128]{1,0:T(8,128)} custom-call(bf16[512,1024]{1,0:T(8,128)(2,1)} %bitcast.18, bf16[1024,512]{1,0:T(8,128)(2,1)} %wq_ref.1), custom_call_target="tpu_custom_call" | custom-call | tf_op jit(solution)/shard_map/project/pallas_call | solution.py:281
  5.1 0.0 copy-start.3
  5.1 11.9 %all-to-all-start = ((f32[8,264,128]{2,1,0:T(8,128)}), f32[8,264,128]{2,1,0:T(8,128)S(1)}, u32[]{:S(2)}, u32[]{:S(2)}) async-start(f32[8,264,128]{2,1,0:T(8,128)} %bitcast.16), calls=%async_computation | async-start | bytes 2162688 | tf_op jit(solution)/shard_map/all_to_all | solution.py:296
  17.0 0.0 copy-done.3
  17.0 0.5 pad.7.route_ref
  17.6 3.2 %decode.1 = (f32[8,128]{1,0:T(8,128)}, f32[256,128]{1,0:T(8,128)}, bf16[128,128]{1,0:T(8,128)(2,1)}) custom-call(s32[4]{0:T(128)} %lens_ref.1, bf16[4,256]{1,0:T(4,128)(2,1)} %q_ref.1, bf16[4,128,128]{2,1,0:T(8,128)(2,1)} %k_ref.1, bf16[4,128,128]{2,1,0:T(8,128)(2,1)} %v_ref.1, bf16[4,128]{1,0:T(4,128)(2,1)} %nk_ref.1, bf16[4,128]{1,0:T(4,128)(2,1)} %nv_ref.1, ...), custom_call_target="tpu_custom_call" | custom-call | tf_op jit(solution)/shard_map/decode/pallas_call | solution.py:303
  20.8 18.4 %all-to-all-done = f32[8,264,128]{2,1,0:T(8,128)S(1)} async-done(((f32[8,264,128]{2,1,0:T(8,128)}), f32[8,264,128]{2,1,0:T(8,128)S(1)}, u32[]{:S(2)}, u32[]{:S(2)}) %all-to-all-start) | async-done | bytes 1081376 | tf_op jit(solution)/shard_map/all_to_all | solution.py:296
  39.1 0.0 copy-start
  39.1 1.0 copy-done
  40.1 2.5 %place.1 = f32[1024,128]{1,0:T(8,128)} custom-call(f32[2112,128]{1,0:T(8,128)} %bitcast.15, f32[8,128]{1,0:T(8,128)} %get-tuple-element.7.attn_ref, bf16[128,128]{1,0:T(8,128)(2,1)} %get-tuple-element.8.place_ref), custom_call_target="tpu_custom_call" | custom-call | tf_op jit(solution)/shard_map/place/pallas_call | solution.py:330
  42.6 17.9 %all-to-all-start.1 = ((f32[64,16,128]{2,1,0:T(8,128)}), f32[64,16,128]{2,1,0:T(8,128)S(1)}, u32[]{:S(2)}, u32[]{:S(2)}) async-start(f32[64,16,128]{2,1,0:T(8,128)} %bitcast.17), calls=%async_computation.1 | async-start | bytes 1048576 | tf_op jit(solution)/shard_map/all_to_all | solution.py:342
  61.2 15.1 %all-to-all-done.1.x_ref = f32[64,16,128]{2,1,0:T(8,128)S(1)} async-done(((f32[64,16,128]{2,1,0:T(8,128)}), f32[64,16,128]{2,1,0:T(8,128)S(1)}, u32[]{:S(2)}, u32[]{:S(2)}) %all-to-all-start.1) | async-done | bytes 524320 | tf_op jit(solution)/shard_map/all_to_all | solution.py:342
  76.3 0.0 copy-start.1
  76.3 0.8 copy-done.1
  77.1 0.0 copy-start.4
  77.1 4.7 %score.1 = f32[64,8,128]{2,1,0:T(8,128)} custom-call(s32[1]{0:T(128)S(6)} %copy.18.index_ref, f32[64,16,128]{2,1,0:T(8,128)} %copy-done.1, bf16[1024,128]{1,0:T(8,128)(2,1)} %bitcast.21, bf16[1024,128]{1,0:T(8,128)(2,1)} %bitcast.22, bf16[4,128]{1,0:T(4,128)(2,1)} %bitcast.24, bf16[128,128]{1,0:T(8,128)(2,1)} %bitcast.23), custom_call_target="tpu_custom_call" | custom-call | tf_op jit(solution)/shard_map/score/pallas_call | solution.py:346
  81.9 17.7 %all_to_all.20 = f32[64,8,128]{2,1,0:T(8,128)} all-to-all(f32[64,8,128]{2,1,0:T(8,128)} %score.1), channel_id=1, replica_groups=mesh['wide'=64,'tp'=8] {'wide'}, dimensions={0} | all-to-all | bytes 524288 | tf_op jit(solution)/shard_map/all_to_all | solution.py:368
  99.6 1.9 %merge.1 = f32[256,128]{1,0:T(8,128)} custom-call(f32[512,128]{1,0:T(8,128)} %bitcast.19, f32[256,128]{1,0:T(8,128)} %get-tuple-element.9.partial_ref, bf16[128,128]{1,0:T(8,128)(2,1)} %get-tuple-element.8.place_ref), custom_call_target="tpu_custom_call" | custom-call | tf_op jit(solution)/shard_map/merge/pallas_call | solution.py:370
  101.5 6.8 %all-to-all-start.3 = ((f32[8,32,128]{2,1,0:T(8,128)}), f32[8,32,128]{2,1,0:T(8,128)S(1)}, u32[]{:S(2)}, u32[]{:S(2)}) async-start(f32[8,32,128]{2,1,0:T(8,128)} %bitcast.20), calls=%async_computation.3 | async-start | bytes 262144 | tf_op jit(solution)/shard_map/all_to_all | solution.py:382
  108.3 0.0 copy-done.4
  108.3 0.5 pad.8.length_ref
  108.8 7.5 %all-to-all-done.3.x_ref = f32[8,32,128]{2,1,0:T(8,128)S(1)} async-done(((f32[8,32,128]{2,1,0:T(8,128)}), f32[8,32,128]{2,1,0:T(8,128)S(1)}, u32[]{:S(2)}, u32[]{:S(2)}) %all-to-all-start.3) | async-done | bytes 131104 | tf_op jit(solution)/shard_map/all_to_all | solution.py:382
  116.4 0.6 copy-done.2
  117.0 1.5 %final.1 = (bf16[4,512]{1,0:T(4,128)(2,1)}, f32[1,64]{1,0:T(1,128)}) custom-call(f32[8,32,128]{2,1,0:T(8,128)} %copy-done.2, f32[1,128]{1,0:T(1,128)} %pad.8.length_ref), custom_call_target="tpu_custom_call" | custom-call | tf_op jit(solution)/shard_map/final/pallas_call | solution.py:390
  (3 shorter events, 0.0 us)
Async XLA Ops:
  5.1 11.9 %copy-start.3 = (s32[64,1]{0,1:T(1,128)S(1)}, s32[64,1]{0,1:T(1,128)}, u32[]{:S(2)}) copy-start(s32[64,1]{0,1:T(1,128)} %param.25) | copy-start | bytes 772
  5.1 34.0 %all-to-all-start = ((f32[8,264,128]{2,1,0:T(8,128)}), f32[8,264,128]{2,1,0:T(8,128)S(1)}, u32[]{:S(2)}, u32[]{:S(2)}) async-start(f32[8,264,128]{2,1,0:T(8,128)} %bitcast.16), calls=%async_computation | async-start | bytes 2162688 | tf_op jit(solution)/shard_map/all_to_all | solution.py:296
  39.1 1.0 copy-start
  42.6 33.7 %all-to-all-start.1 = ((f32[64,16,128]{2,1,0:T(8,128)}), f32[64,16,128]{2,1,0:T(8,128)S(1)}, u32[]{:S(2)}, u32[]{:S(2)}) async-start(f32[64,16,128]{2,1,0:T(8,128)} %bitcast.17), calls=%async_computation.1 | async-start | bytes 1048576 | tf_op jit(solution)/shard_map/all_to_all | solution.py:342
  76.3 0.8 copy-start.1
  77.1 31.2 %copy-start.4 = (s32[64]{0:T(128)S(1)}, s32[64]{0:T(128)}, u32[]{:S(2)}) copy-start(s32[64]{0:T(128)} %param.26) | copy-start | bytes 772
  101.5 14.9 %all-to-all-start.3 = ((f32[8,32,128]{2,1,0:T(8,128)}), f32[8,32,128]{2,1,0:T(8,128)S(1)}, u32[]{:S(2)}, u32[]{:S(2)}) async-start(f32[8,32,128]{2,1,0:T(8,128)} %bitcast.20), calls=%async_computation.3 | async-start | bytes 262144 | tf_op jit(solution)/shard_map/all_to_all | solution.py:382
  116.4 0.7 copy-start.2

commit v2 on v1

v2 whole, which is shorter than its diff:
```python
import functools
import math

import jax
import jax.numpy as jnp
from jax import lax
from jax.experimental import pallas as pl
from jax.experimental.pallas import tpu as pltpu
from jax.sharding import PartitionSpec as P

HD = 128
RD = 8192
CAP = 2
CORES = 2
PAIR = 2
VMEM_LIMIT = 16 * 2**20
WEIGHT_COPIES = 4
F32 = jnp.float32
BF16 = jnp.bfloat16


def split2(x):
    high = x.astype(BF16)
    return high, (x - high.astype(F32)).astype(BF16)


def split3(x):
    high, mid = split2(x)
    return high, mid, (x - high.astype(F32) - mid.astype(F32)).astype(BF16)


def mm(a, b):
    return jnp.dot(a, b, preferred_element_type=F32)


def mm_t(a, b):
    return lax.dot_general(a, b, (((1,), (1,)), ((), ())), preferred_element_type=F32)


def rows_at(first, count, stride):
    return pl.ds(first, count, stride=stride)


def local_call(kernel, name, operands, outs, scratch=(), scalars=0, fetched=0, pinned=()):
    vmem = pl.BlockSpec(memory_space=pltpu.VMEM)
    smem = pl.BlockSpec(memory_space=pltpu.SMEM)
    hbm = pl.BlockSpec(memory_space=pltpu.HBM)
    kept = len(operands) - fetched
    operands = list(operands)
    for k in range(len(operands)):
        if k >= kept:
            operands[k] = pltpu.with_memory_space_constraint(operands[k], pltpu.HBM)
        elif k in pinned:
            operands[k] = pltpu.with_memory_space_constraint(operands[k], pltpu.VMEM)
    return pl.pallas_call(
        kernel,
        in_specs=[smem] * scalars + [vmem] * (kept - scalars) + [hbm] * fetched,
        out_specs=[vmem] * len(outs),
        out_shape=outs,
        scratch_shapes=list(scratch),
        compiler_params=pltpu.CompilerParams(vmem_limit_bytes=VMEM_LIMIT),
        name=name,
    )(*operands)


def start_copies(pairs, sems):
    copies = [pltpu.make_async_copy(a, b, sems.at[k]) for k, (a, b) in enumerate(pairs)]
    for copy in copies:
        copy.start()
    return copies


def project_kernel(
    row_len, chunks, rows_hbm, wq_hbm, theirs_ref, kept_ref, rows_ref, wq_ref, acc_ref, sq_ref, sems
):
    many = rows_ref.shape[0] // chunks
    depth = wq_ref.shape[0] // WEIGHT_COPIES
    pieces = [(wq_hbm, wq_ref, k * depth, depth) for k in range(WEIGHT_COPIES)]
    pieces += [(rows_hbm, rows_ref, k * many, many) for k in range(chunks)]
    copies = start_copies(
        [(a.at[pl.ds(first, n)], b.at[pl.ds(first, n)]) for a, b, first, n in pieces], sems
    )
    chunk = many // row_len
    width = wq_ref.shape[1] // CORES
    heads = width // HD
    pairs = row_len // PAIR
    each = kept_ref.shape[0] // pairs
    body = each - 8
    seqs = body // (heads * PAIR)
    core = lax.axis_index("tc")
    across = lax.broadcasted_iota(jnp.int32, (chunk, HD), 0)
    lane = lax.broadcasted_iota(jnp.int32, (chunk, HD), 1)
    squares = [jnp.zeros((1, HD), F32) for _ in range(pairs)]
    for copy in copies[:WEIGHT_COPIES]:
        copy.wait()
    for step in range(chunks):
        copies[WEIGHT_COPIES + step].wait()
        rows = rows_ref[step * many : (step + 1) * many, :]
        for turn, (half, out_ref) in enumerate([(1 - core, theirs_ref), (core, kept_ref)]):
            columns = pl.ds(pl.multiple_of(half * width, width), width)
            product = mm(rows, wq_ref[:, columns])
            slab = (step * 2 + turn) * heads * many
            for h in range(heads):
                acc_ref[slab + h * many : slab + (h + 1) * many, :] = product[
                    :, h * HD : (h + 1) * HD
                ]
            for t in range(row_len):
                for h in range(heads):
                    first = (t // PAIR) * each + (h * PAIR + t % PAIR) * seqs + step * chunk
                    out_ref[first : first + chunk, :] = acc_ref[
                        rows_at(slab + h * many + t, chunk, row_len), :
                    ]
        wide_rows = rows.astype(F32)
        sums = jnp.sum(wide_rows * wide_rows, axis=1, keepdims=True)
        sq_ref[step * many : (step + 1) * many, :] = jnp.broadcast_to(sums, (many, HD))
        for t in range(row_len):
            spot = lane == across + ((t % PAIR) * seqs + step * chunk)
            picked = jnp.where(spot, sq_ref[rows_at(step * many + t, chunk, row_len), :], 0.0)
            squares[t // PAIR] += jnp.sum(picked, axis=0, keepdims=True)
    for p in range(pairs):
        tail = jnp.broadcast_to(squares[p], (8, HD))
        for out_ref in (theirs_ref, kept_ref):
            out_ref[p * each + body : (p + 1) * each, :] = tail


def add_kernel(a_ref, b_ref, out_ref):
    out_ref[...] = a_ref[...] + b_ref[...]


def decode_kernel(
    lens_hbm,
    q_hbm,
    nk_hbm,
    nv_hbm,
    route_hbm,
    score_hbm,
    delta_hbm,
    k_hbm,
    v_hbm,
    w_hbm,
    attn_ref,
    out_ref,
    place_ref,
    tile_ref,
    delta_ref,
    lens_ref,
    q_ref,
    nk_ref,
    nv_ref,
    route_ref,
    score_ref,
    k_ref,
    v_ref,
    w_ref,
    sems,
):
    w_cols = w_ref.shape[1] // WEIGHT_COPIES
    copies = start_copies(
        [
            (lens_hbm, lens_ref),
            (q_hbm, q_ref),
            (nk_hbm, nk_ref),
            (nv_hbm, nv_ref),
            (route_hbm, route_ref),
            (score_hbm, score_ref),
            (delta_hbm, delta_ref),
            (k_hbm, k_ref),
            (v_hbm, v_ref),
        ]
        + [
            (w_hbm.at[:, pl.ds(c, w_cols)], w_ref.at[:, pl.ds(c, w_cols)])
            for c in range(0, w_ref.shape[1], w_cols)
        ],
        sems,
    )
    for copy in copies[:-WEIGHT_COPIES]:
        copy.wait()
    seqs = q_ref.shape[0]
    rows = 2 * seqs
    scale = 1.0 / math.sqrt(HD)
    q = q_ref[...].astype(F32)
    queries = jnp.concatenate([q[:, :HD], q[:, HD:]], axis=0)
    nk = nk_ref[...].astype(F32)
    nv = nv_ref[...].astype(F32)
    own_key = jnp.concatenate([nk, nk], axis=0)
    own_value = jnp.concatenate([nv, nv], axis=0)
    row = lax.broadcasted_iota(jnp.int32, (rows, HD), 0) % seqs
    place_in = lax.broadcasted_iota(jnp.int32, (rows, HD), 1)
    queries16 = queries.astype(BF16)
    scores = jnp.zeros((rows, HD), F32)
    length = jnp.zeros((rows, HD), jnp.int32)
    for s in range(seqs):
        scores = jnp.where(row == s, mm_t(queries16, k_ref[s]), scores)
        length = jnp.where(row == s, lens_ref[s], length)
    scores = jnp.where(place_in < length, scores * scale, -jnp.inf)
    own_score = jnp.sum(queries * own_key, axis=1, keepdims=True) * scale
    highest = jnp.maximum(jnp.max(scores, axis=1, keepdims=True), own_score)
    weights = jnp.exp(scores - highest)
    own_weight = jnp.exp(own_score - highest)
    denominator = jnp.sum(weights, axis=1, keepdims=True) + own_weight
    probs = (weights / denominator).astype(BF16)
    own_prob = (own_weight / denominator).astype(BF16).astype(F32)
    mixed = jnp.zeros((rows, HD), F32)
    for s in range(seqs):
        mixed = jnp.where(row == s, mm(probs, v_ref[s]), mixed)
    attn = (mixed + own_prob * own_value).astype(BF16).astype(F32)
    attn_ref[...] = attn
    turned = jnp.concatenate([attn[seqs:], attn[:seqs]], axis=0)
    both = jnp.concatenate([attn, turned], axis=1).astype(BF16)
    blocks = w_ref.shape[1] // HD
    for copy in copies[-WEIGHT_COPIES:]:
        copy.wait()
    for first in range(0, blocks, 4):
        part = mm(both, w_ref[:, first * HD : (first + 4) * HD])
        for c in range(4):
            out_ref[(first + c) * rows : (first + c + 1) * rows, :] = part[:, c * HD : (c + 1) * HD]
    slots = place_ref.shape[0]
    groups = slots // CAP
    down = lax.broadcasted_iota(jnp.int32, (HD, HD), 0)
    across = lax.broadcasted_iota(jnp.int32, (HD, HD), 1)
    target = jnp.broadcast_to(route_ref[...], (HD, HD))
    target_down = jnp.sum(jnp.where(down == across, target, 0.0), axis=1, keepdims=True)
    earlier = jnp.where(jnp.logical_and(target == target_down, down < across), 1.0, 0.0)
    rank = jnp.sum(earlier, axis=0, keepdims=True)
    slot = lax.broadcasted_iota(jnp.int32, (slots, HD), 0)
    group = (slot % groups).astype(F32)
    order = (slot // groups).astype(F32)
    held = jnp.logical_and(route_ref[...] == group, rank == order)
    place_ref[...] = jnp.where(held, 1.0, 0.0).astype(BF16)
    weight = score_ref[...].astype(F32)
    heads = weight.shape[0] // CORES
    weight = jnp.where(lax.axis_index("tc") == 0, weight[:heads], weight[heads:])
    for h in range(heads):
        own = slice(h * rows // heads, (h + 1) * rows // heads)
        tile_ref[own, :] = jnp.broadcast_to(weight[h : h + 1], (rows // heads, HD))


def place_kernel(sources, x_ref, attn_ref, place_ref, out_ref, lay_ref):
    each = x_ref.shape[0] // sources
    body = each - 8
    groups = place_ref.shape[0] // CAP
    tile = out_ref.shape[1] - attn_ref.shape[0]
    lay = tile // 2
    parts = lay // CAP
    heads = parts // PAIR
    seqs = body // parts
    total = x_ref[0:each, :]
    for k in range(1, sources):
        total = total + x_ref[k * each : (k + 1) * each, :]
    inverse = lax.rsqrt(total[body : body + 1, :] / RD + 1e-05) * (math.log2(math.e) / math.sqrt(HD))
    down = lax.broadcasted_iota(jnp.int32, (HD, HD), 0)
    across = lax.broadcasted_iota(jnp.int32, (HD, HD), 1)
    factor = jnp.sum(jnp.where(down == across, inverse, 0.0), axis=1, keepdims=True)
    pieces = []
    for h in range(heads):
        for p in range(PAIR):
            first = (h * PAIR + p) * seqs
            pieces.append(total[first : first + seqs, :] * factor[p * seqs : (p + 1) * seqs, :])
    normed = jnp.concatenate(pieces, axis=1)
    if seqs < HD:
        normed = jnp.concatenate([normed, jnp.zeros((HD - seqs, parts * HD), F32)], axis=0)
    place = place_ref[...]
    for k, term in enumerate(split2(normed)):
        placed = mm(place, term)
        for r in range(CAP):
            for q in range(parts):
                row = k * lay + (q // PAIR) * CAP * PAIR + r * PAIR + q % PAIR
                lay_ref[rows_at(row, groups, tile), :] = placed[
                    r * groups : (r + 1) * groups, q * HD : (q + 1) * HD
                ]
    attn = jnp.broadcast_to(attn_ref[...].astype(BF16)[None], (groups,) + attn_ref.shape)
    out_ref[:, :tile, :] = lay_ref[...].reshape(groups, tile, HD).astype(BF16)
    out_ref[:, tile:, :] = attn


def score_kernel(index_ref, x_ref, keys_ref, values_ref, weight_ref, delta_ref, out_ref):
    tile = out_ref.shape[1]
    seqs = tile // 2
    senders = x_ref.shape[0]
    keys = keys_ref[...]
    keys2 = jnp.concatenate([keys, keys], axis=1)
    values = values_ref[...]
    weight = weight_ref[...][None]
    delta = delta_ref[...]
    block = index_ref[0]
    columns = 32
    row_block = block // columns
    column = (block % columns).astype(F32)
    at_once = min(16, senders)
    row = lax.broadcasted_iota(jnp.int32, (1, tile, HD), 1)
    lane = lax.broadcasted_iota(jnp.int32, (1, tile, HD), 2)
    named = jnp.logical_and(row == seqs, lane == HD - 1)
    for first in range(0, senders, at_once):
        x = x_ref[first : first + at_once].astype(F32)
        flat = [
            x[:, k * tile : (k + 1) * tile, :].reshape(at_once * tile, HD).astype(BF16)
            for k in range(3)
        ]
        scores = mm_t(jnp.concatenate(flat[:2], axis=1), keys2)
        highest = jnp.max(scores, axis=1, keepdims=True)
        weights = jnp.exp2(scores - highest)
        probs = (weights * (1.0 / jnp.sum(weights, axis=1, keepdims=True))).astype(BF16)
        context = mm(probs, values)
        gated = context / (1.0 + jnp.exp(-context))
        terms = gated.reshape(at_once, tile, HD) * weight
        by_head = jnp.broadcast_to(jnp.sum(terms, axis=2, keepdims=True), terms.shape)
        score = by_head + jnp.concatenate([by_head[:, seqs:], by_head[:, :seqs]], axis=1)
        product = mm(flat[2], delta).reshape(at_once, tile, HD)
        turned = jnp.concatenate([product[:, seqs:], product[:, :seqs]], axis=1)
        result = jnp.where(row_block == 0, product, turned)
        result = jnp.where(row < seqs, result, jnp.where(named, column, score))
        out_ref[first : first + at_once] = result


def merge_kernel(tile, x_ref, partial_ref, place_ref, out_ref):
    senders = x_ref.shape[0] // tile
    blocks = partial_ref.shape[0] // tile
    seqs = tile // 2
    column = x_ref[rows_at(seqs, senders, tile), :][:, HD - 1 :]
    pieces = split3(
        jnp.concatenate([x_ref[rows_at(s, senders, tile), :] for s in range(seqs)], axis=1)
    )
    down = lax.broadcasted_iota(jnp.int32, (senders, senders), 0)
    across = lax.broadcasted_iota(jnp.int32, (senders, senders), 1)
    column_across = jnp.sum(
        jnp.where(down == across, jnp.broadcast_to(column, (senders, senders)), 0.0),
        axis=0,
        keepdims=True,
    )
    wanted = lax.broadcasted_iota(jnp.int32, (blocks, senders), 0).astype(F32)
    pick = jnp.where(wanted == column_across, 1.0, 0.0).astype(BF16)
    high, mid, low = pieces
    added = (mm(pick, low) + mm(pick, mid)) + mm(pick, high)
    out_ref[...] = partial_ref[...]
    for s in range(seqs):
        where = rows_at(s, blocks, tile)
        out_ref[where, :] = partial_ref[where, :] + added[:, s * HD : (s + 1) * HD]
    place = place_ref[...].astype(F32)
    shards = 8
    for p in range(PAIR):
        score = jnp.concatenate(
            [x_ref[rows_at(seqs + r * PAIR + p, senders, tile), :] for r in range(CAP)], axis=0
        )[:, :1]
        back = jnp.sum(place * score, axis=0, keepdims=True)
        out_ref[rows_at(seqs + p, shards, blocks // shards * tile), :] = jnp.broadcast_to(
            back, (shards, HD)
        )


def final_kernel(tile, x_ref, length_ref, decoded_ref, rewards_ref):
    seqs = tile // 2
    total = x_ref[0]
    for k in range(1, x_ref.shape[0]):
        total = total + x_ref[k]
    for c in range(total.shape[0] // tile):
        decoded_ref[:, c * HD : (c + 1) * HD] = total[c * tile : c * tile + seqs, :].astype(BF16)
    length = length_ref[...]
    count = rewards_ref.shape[1]
    reward = jnp.zeros((1, HD), F32)
    for k in range(x_ref.shape[0]):
        for p in range(PAIR):
            token = k // CORES * PAIR + p
            row = x_ref[k, seqs + p : seqs + p + 1, :]
            reward = reward + jnp.where(length > token, row, 0.0)
    rewards_ref[...] = (reward / length)[:, :count]


def per_device(
    query,
    key_cache,
    value_cache,
    new_key,
    new_value,
    cache_lengths,
    out_weight,
    delta_index,
    delta_values,
    fin_route,
    fin_lengths,
    fin_rows,
    reward_query,
    rubric_keys,
    rubric_values,
    score_weight,
):
    wide_count = lax.axis_size("wide")
    chips = lax.axis_size("th")
    tp_count = chips * lax.axis_size("tc")
    finished, row_len, features = fin_rows.shape
    heads = reward_query.shape[1] // HD // CORES
    seq_count = query.shape[0]
    tile = 2 * seq_count
    blocks = out_weight.shape[1] // HD
    slots = CAP * wide_count
    parts = PAIR * heads
    message = parts * finished + 8
    chunks = 4 if finished % 32 == 0 else 1
    shape = jax.ShapeDtypeStruct

    rows = fin_rows.reshape(finished * row_len, features)
    partial = shape((chips * message, HD), F32)
    theirs, kept = local_call(
        functools.partial(project_kernel, row_len, chunks),
        "project",
        (rows, reward_query),
        [partial, partial],
        [
            pltpu.VMEM(rows.shape, BF16),
            pltpu.VMEM(reward_query.shape, BF16),
            pltpu.VMEM((CORES * heads * finished * row_len, HD), F32),
            pltpu.VMEM((finished * row_len, HD), F32),
            pltpu.SemaphoreType.DMA((WEIGHT_COPIES + chunks,)),
        ],
        fetched=2,
    )
    got = lax.ppermute(theirs, "tc", [(0, 1), (1, 0)])
    (both,) = local_call(add_kernel, "add", (kept, got), [partial])
    summed_tokens = lax.all_to_all(
        both.reshape(chips, message, HD), "th", split_axis=0, concat_axis=0, tiled=True
    ).reshape(partial.shape)

    pad = ((0, 0), (0, HD - finished))
    route = jnp.pad(fin_route.reshape(1, finished).astype(F32), pad, constant_values=-1.0)
    lengths = jnp.pad(fin_lengths.reshape(1, finished).astype(F32), pad, constant_values=1.0)
    weights = score_weight.reshape(heads * CORES, HD)
    small = (cache_lengths, query, new_key, new_value, route, weights, delta_values[0])
    large = (key_cache, value_cache, out_weight)
    attn, partial_out, place, weight_tile, delta = local_call(
        decode_kernel,
        "decode",
        small + large,
        [
            shape((tile, HD), F32),
            shape((blocks * tile, HD), F32),
            shape((slots, HD), BF16),
            shape((tile, HD), F32),
            shape(delta_values.shape[1:], BF16),
        ],
        [pltpu.SMEM(cache_lengths.shape, jnp.int32)]
        + [pltpu.VMEM(a.shape, a.dtype) for a in small[1:-1] + large]
        + [pltpu.SemaphoreType.DMA((len(small) + 2 + WEIGHT_COPIES,))],
        fetched=len(small) + len(large),
    )

    lay = CAP * parts
    (outgoing,) = local_call(
        functools.partial(place_kernel, chips),
        "place",
        (summed_tokens, attn, place),
        [shape((wide_count, 2 * lay + tile, HD), BF16)],
        [pltpu.VMEM((wide_count * 2 * lay, HD), F32)],
    )
    received = lax.all_to_all(outgoing, "wide", split_axis=0, concat_axis=0, tiled=True)

    (answers,) = local_call(
        score_kernel,
        "score",
        (
            delta_index,
            received,
            rubric_keys[0],
            rubric_values[0],
            weight_tile,
            delta,
        ),
        [shape((wide_count, tile, HD), F32)],
        scalars=1,
    )
    returned = lax.all_to_all(answers, "wide", split_axis=0, concat_axis=0, tiled=True)

    (merged,) = local_call(
        functools.partial(merge_kernel, tile),
        "merge",
        (returned.reshape(wide_count * tile, HD), partial_out, place),
        [shape((blocks * tile, HD), F32)],
    )
    shares = lax.all_to_all(
        merged.reshape(tp_count, blocks // tp_count * tile, HD),
        ("th", "tc"),
        split_axis=0,
        concat_axis=0,
        tiled=True,
    )

    decoded, rewards = local_call(
        functools.partial(final_kernel, tile),
        "final",
        (shares, lengths),
        [shape((seq_count, blocks // tp_count * HD), BF16), shape((1, finished), F32)],
    )
    return decoded, rewards.reshape(finished)


def solution(mesh):
    tp = ("th", "tc")
    wide_count, tp_count = mesh.devices.shape
    split = jax.sharding.Mesh(
        mesh.devices.reshape(wide_count, tp_count // CORES, CORES), ("wide",) + tp
    )
    in_specs = (
        P("wide", tp),
        P("wide", None, tp),
        P("wide", None, tp),
        P("wide", tp),
        P("wide", tp),
        P("wide"),
        P(tp, None),
        P("wide"),
        P("wide", tp, None),
        P("wide", None),
        P("wide"),
        P("wide", None, tp),
        P(tp, None),
        P("wide", None, None),
        P("wide", None, None),
        P(),
    )
    out_specs = (P("wide", tp), P("wide"))
    return jax.shard_map(
        per_device, mesh=split, in_specs=in_specs, out_specs=out_specs, check_vma=False
    )
```

time: 119 us -> 97.5 us (0.82)
  waiting for transfers between devices: 41.1 us -> 31 us
  Pallas kernels: 18.3 us -> 10.9 us
  local copies, waits for them, and re-layouts: 3.49 us -> 0.54 us
    all_to_all x3, waiting for transfers between devices: 41.1 us -> 29.5 us  [the longest x1 12 us: per_device(): lax.all_to_all(outgoing, 'wide', split_axis=0, concat_axis=0, tiled=True)]
    all_to_all x3, starting transfers between devices: 36.7 us -> 26.9 us  [the longest x1 15.4 us: per_device(): lax.all_to_all(outgoing, 'wide', split_axis=0, concat_axis=0, tiled=True)]
    ppermute x0 -> x1, starting transfers between devices: none -> 8.78 us  [per_device(): got = lax.ppermute(theirs, 'tc', [(0, 1), (1, 0)])]
    pallas_call x6 -> x7, Pallas kernels: 18.3 us -> 10.9 us  [local_call(): pl.pallas_call(kernel, in_specs=[smem] * scalars + [vmem] * (kept - scala...]
    unnamed x10 -> x8, local copies, waits for them, and re-layouts: 2.45 us -> 0.02 us
    ppermute x0 -> x1, waiting for transfers between devices: none -> 1.54 us  [per_device(): got = lax.ppermute(theirs, 'tc', [(0, 1), (1, 0)])]
  transfers between devices with their start and end apart: 3 -> 4, of which waited for: 3 -> 4; matrix products, arithmetic and copies ran while one was open for 1% -> 1% of each run, Pallas kernels for 3% -> 2%
where the time goes in v2:
time: 97.5 us; the launch traced here: 97.1 us
  starting transfers between devices  35.7 us (37%)
  waiting for transfers between devices  31 us (32%)
  blocking collectives  17.6 us (18%)
  Pallas kernels  10.9 us (11%)
  between operations  1.36 us (1%)
    all_to_all x1, blocking collectives, per_device(): lax.all_to_all(answers, 'wide', split_axis=0, concat_axis=0, tiled=True)  17.6 us
    all_to_all x1, starting transfers between devices, per_device(): lax.all_to_all(outgoing, 'wide', split_axis=0, concat_axis=0, tiled=True)  15.4 us
    all_to_all x1, waiting for transfers between devices, per_device(): lax.all_to_all(outgoing, 'wide', split_axis=0, concat_axis=0, tiled=True)  12 us
    pallas_call x7, Pallas kernels, local_call(): pl.pallas_call(kernel, in_specs=[smem] * scalars + [vmem] * (kept - scala...  10.9 us
    all_to_all x1, waiting for transfers between devices, per_device(): lax.all_to_all(both.reshape(chips, message, HD), 'th', split_axis=0, conc...  9.46 us
    ppermute x1, starting transfers between devices, per_device(): got = lax.ppermute(theirs, 'tc', [(0, 1), (1, 0)])  8.78 us
    all_to_all x1, waiting for transfers between devices, per_device(): lax.all_to_all(merged.reshape(tp_count, blocks // tp_count * tile, HD), (...  8.03 us
    all_to_all x1, starting transfers between devices, per_device(): lax.all_to_all(merged.reshape(tp_count, blocks // tp_count * tile, HD), (...  6.78 us
  transfers between devices with their start and end apart: 4, of which 4 were waited for; matrix products, arithmetic and copies ran while one was open for 1% of the time, Pallas kernels for 2%

profile of v2, /device:TPU:1, one launch (start us, length us, event | category | flops | bytes accessed | tf_op | source)
XLA Modules:
  0.0 97.1 jit_solution(11335835938818470888)
XLA Ops:
  0.6 0.0 copy-start.2
  0.6 2.8 %project.1 = (f32[1056,128]{1,0:T(8,128)S(1)}, f32[1056,128]{1,0:T(8,128)S(1)}) custom-call(bf16[512,1024]{1,0:T(8,128)(2,1)} %bitcast.18, bf16[1024,512]{1,0:T(8,128)(2,1)} %wq_hbm.1), custom_call_target="tpu_custom_call" | custom-call | tf_op jit(solution)/shard_map/project/pallas_call | solution.py:55
  3.4 8.8 %collective-permute-start = (f32[1056,128]{1,0:T(8,128)S(1)}, f32[1056,128]{1,0:T(8,128)S(1)}, u32[]{:S(2)}, u32[]{:S(2)}) collective-permute-start(f32[1056,128]{1,0:T(8,128)S(1)} %get-tuple-element.12), channel_id=1, source_target_pairs={{0,1},{1,0},{2,3},{3,2},{4,5},{5,4},{6,7},{7,6},{8,9},{9,8},{10,11... | collective-permute-start | bytes 1622024 | tf_op jit(solution)/shard_map/ppermute | solution.py:416
  12.2 1.5 %collective-permute-done.b_ref = f32[1056,128]{1,0:T(8,128)S(1)} collective-permute-done((f32[1056,128]{1,0:T(8,128)S(1)}, f32[1056,128]{1,0:T(8,128)S(1)}, u32[]{:S(2)}, u32[]{:S(2)}) %collective-permute-start) | collective-permute-done | bytes 540704 | tf_op jit(solution)/shard_map/ppermute | solution.py:416
  13.7 0.9 add.5
  14.6 4.6 %all-to-all-start = ((f32[4,264,128]{2,1,0:T(8,128)}), f32[4,264,128]{2,1,0:T(8,128)S(1)}, u32[]{:S(2)}, u32[]{:S(2)}) async-start(f32[4,264,128]{2,1,0:T(8,128)} %bitcast.1), calls=%async_computation | async-start | bytes 1081344 | tf_op jit(solution)/shard_map/all_to_all | solution.py:418
  19.2 0.0 copy-done.2
  19.2 0.0 copy-start
  19.2 0.0 copy-start.1
  19.3 0.5 pad.7.route_hbm
  19.8 2.2 %decode.1 = (f32[8,128]{1,0:T(8,128)S(1)}, f32[256,128]{1,0:T(8,128)S(1)}, bf16[128,128]{1,0:T(8,128)(2,1)S(1)}, f32[8,128]{1,0:T(8,128)S(1)}, bf16[128,128]{1,0:T(8,128)(2,1)S(1)}) custom-call(s32[4]{0:T(128)} %lens_hbm.1, bf16[4,256]{1,0:T(4,128)(2,1)} %q_hbm.1, bf16[4,128]{1,0:T(4,128)(2,1)} %nk_hbm.1, bf16[4,128]{1,0:T(4,128)(2,1)} %nv_hbm.1, ...), custom_call_target="tpu_custom_call" | custom-call | tf_op jit(solution)/shard_map/decode/pallas_call | solution.py:55
  22.0 9.5 %all-to-all-done = f32[4,264,128]{2,1,0:T(8,128)S(1)} async-done(((f32[4,264,128]{2,1,0:T(8,128)}), f32[4,264,128]{2,1,0:T(8,128)S(1)}, u32[]{:S(2)}, u32[]{:S(2)}) %all-to-all-start) | async-done | bytes 540704 | tf_op jit(solution)/shard_map/all_to_all | solution.py:418
  31.5 1.1 %place.1 = bf16[64,24,128]{2,1,0:T(8,128)(2,1)} custom-call(f32[1056,128]{1,0:T(8,128)S(1)} %bitcast.14, f32[8,128]{1,0:T(8,128)S(1)} %get-tuple-element.13.attn_ref, bf16[128,128]{1,0:T(8,128)(2,1)S(1)} %get-tuple-element.14.place_ref), custom_call_target="tpu_custom_call" | custom-call | tf_op jit(solution)/shard_map/place/pallas_call | solution.py:55
  32.6 15.4 %all-to-all-start.1 = ((bf16[64,24,128]{2,1,0:T(8,128)(2,1)}), bf16[64,24,128]{2,1,0:T(8,128)(2,1)S(1)}, u32[]{:S(2)}, u32[]{:S(2)}) async-start(bf16[64,24,128]{2,1,0:T(8,128)(2,1)} %place.1), calls=%async_computation.1 | async-start | bytes 786432 | tf_op jit(solution)/shard_map/all_to_all | solution.py:453
  48.7 12.0 %all-to-all-done.1.x_ref = bf16[64,24,128]{2,1,0:T(8,128)(2,1)S(1)} async-done(((bf16[64,24,128]{2,1,0:T(8,128)(2,1)}), bf16[64,24,128]{2,1,0:T(8,128)(2,1)S(1)}, u32[]{:S(2)}, u32[]{:S(2)}) %all-to-all-start.1) | async-done | bytes 393248 | tf_op jit(solution)/shard_map/all_to_all | solution.py:453
  60.7 0.0 copy-done
  60.7 0.0 copy-done.1
  60.7 2.4 %score.1 = f32[64,8,128]{2,1,0:T(8,128)S(1)} custom-call(s32[1]{0:T(128)S(6)} %copy.18.index_ref, bf16[64,24,128]{2,1,0:T(8,128)(2,1)S(1)} %all-to-all-done.1.x_ref, bf16[1024,128]{1,0:T(8,128)(2,1)S(1)} %bitcast.16, bf16[1024,128]{1,0:T(8,128)(2,1)S(1)} %bitcast.17, f32[8,128]{1,0:T(8,128)S(1)} %get-tuple-element.15.weight_ref, ...), custom_call_target="tpu_custom_call" | custom-call | tf_op jit(solution)/shard_map/score/pallas_call | solution.py:55
  63.1 17.6 %all_to_all.20 = f32[64,8,128]{2,1,0:T(8,128)S(1)} all-to-all(f32[64,8,128]{2,1,0:T(8,128)S(1)} %score.1), channel_id=1, replica_groups=mesh['wide'=64,'th'=4,'tc'=2] {'wide'}, dimensions={0} | all-to-all | bytes 524288 | tf_op jit(solution)/shard_map/all_to_all | solution.py:469
  80.8 0.9 merge.1
  81.7 6.8 %all-to-all-start.3 = ((f32[8,32,128]{2,1,0:T(8,128)}), f32[8,32,128]{2,1,0:T(8,128)S(1)}, u32[]{:S(2)}, u32[]{:S(2)}) async-start(f32[8,32,128]{2,1,0:T(8,128)} %bitcast.9), calls=%async_computation.3 | async-start | bytes 262144 | tf_op jit(solution)/shard_map/all_to_all | solution.py:477
  88.4 0.0 copy-done.3
  88.5 8.0 %all-to-all-done.3.x_ref = f32[8,32,128]{2,1,0:T(8,128)S(1)} async-done(((f32[8,32,128]{2,1,0:T(8,128)}), f32[8,32,128]{2,1,0:T(8,128)S(1)}, u32[]{:S(2)}, u32[]{:S(2)}) %all-to-all-start.3) | async-done | bytes 131104 | tf_op jit(solution)/shard_map/all_to_all | solution.py:477
  96.5 0.6 final.1
  (4 shorter events, 0.0 us)
Async XLA Ops:
  0.6 18.6 %copy-start.2 = (s32[64,1]{0,1:T(1,128)S(1)}, s32[64,1]{0,1:T(1,128)}, u32[]{:S(2)}) copy-start(s32[64,1]{0,1:T(1,128)} %param.25) | copy-start | bytes 772
  3.4 10.3 %collective-permute-start = (f32[1056,128]{1,0:T(8,128)S(1)}, f32[1056,128]{1,0:T(8,128)S(1)}, u32[]{:S(2)}, u32[]{:S(2)}) collective-permute-start(f32[1056,128]{1,0:T(8,128)S(1)} %get-tuple-element.12), channel_id=1, source_target_pairs={{0,1},{1,0},{2,3},{3,2},{4,5},{5,4},{6,7},{7,6},{8,9},{9,8},{10,11... | collective-permute-start | bytes 1622024 | tf_op jit(solution)/shard_map/ppermute | solution.py:416
  14.6 16.9 %all-to-all-start = ((f32[4,264,128]{2,1,0:T(8,128)}), f32[4,264,128]{2,1,0:T(8,128)S(1)}, u32[]{:S(2)}, u32[]{:S(2)}) async-start(f32[4,264,128]{2,1,0:T(8,128)} %bitcast.1), calls=%async_computation | async-start | bytes 1081344 | tf_op jit(solution)/shard_map/all_to_all | solution.py:418
  19.2 41.5 %copy-start = (bf16[1,1024,128]{2,1,0:T(8,128)(2,1)S(1)}, bf16[1,1024,128]{2,1,0:T(8,128)(2,1)}, u32[]{:S(2)}) copy-start(bf16[1,1024,128]{2,1,0:T(8,128)(2,1)} %param.29) | copy-start | bytes 786436
  19.2 41.5 %copy-start.1 = (bf16[1,1024,128]{2,1,0:T(8,128)(2,1)S(1)}, bf16[1,1024,128]{2,1,0:T(8,128)(2,1)}, u32[]{:S(2)}) copy-start(bf16[1,1024,128]{2,1,0:T(8,128)(2,1)} %param.30) | copy-start | bytes 786436
  31.5 56.9 %copy-start.3 = (s32[64]{0:T(128)S(1)}, s32[64]{0:T(128)}, u32[]{:S(2)}) copy-start(s32[64]{0:T(128)} %param.26) | copy-start | bytes 772
  32.6 28.1 %all-to-all-start.1 = ((bf16[64,24,128]{2,1,0:T(8,128)(2,1)}), bf16[64,24,128]{2,1,0:T(8,128)(2,1)S(1)}, u32[]{:S(2)}, u32[]{:S(2)}) async-start(bf16[64,24,128]{2,1,0:T(8,128)(2,1)} %place.1), calls=%async_computation.1 | async-start | bytes 786432 | tf_op jit(solution)/shard_map/all_to_all | solution.py:453
  81.7 14.8 %all-to-all-start.3 = ((f32[8,32,128]{2,1,0:T(8,128)}), f32[8,32,128]{2,1,0:T(8,128)S(1)}, u32[]{:S(2)}, u32[]{:S(2)}) async-start(f32[8,32,128]{2,1,0:T(8,128)} %bitcast.9), calls=%async_computation.3 | async-start | bytes 262144 | tf_op jit(solution)/shard_map/all_to_all | solution.py:477

commit v3 on v2

--- a/solution.py
+++ b/solution.py
@@ -15,6 +15,7 @@
 PAIR = 2
 VMEM_LIMIT = 16 * 2**20
 WEIGHT_COPIES = 4
+AT_ONCE = 32
 F32 = jnp.float32
 BF16 = jnp.bfloat16
 
@@ -70,46 +71,49 @@
     return copies
 
 
-def project_kernel(
-    row_len, chunks, rows_hbm, wq_hbm, theirs_ref, kept_ref, rows_ref, wq_ref, acc_ref, sq_ref, sems
-):
+def project_kernel(mine, row_len, chunks, *refs):
+    if mine:
+        squares_ref, rows_ref, wq_ref, out_ref, acc_ref = refs
+    else:
+        rows_hbm, wq_hbm, out_ref, squares_ref, rows_ref, wq_ref, acc_ref, sq_ref, sems = refs
     many = rows_ref.shape[0] // chunks
     depth = wq_ref.shape[0] // WEIGHT_COPIES
-    pieces = [(wq_hbm, wq_ref, k * depth, depth) for k in range(WEIGHT_COPIES)]
-    pieces += [(rows_hbm, rows_ref, k * many, many) for k in range(chunks)]
-    copies = start_copies(
-        [(a.at[pl.ds(first, n)], b.at[pl.ds(first, n)]) for a, b, first, n in pieces], sems
-    )
-    chunk = many // row_len
     width = wq_ref.shape[1] // CORES
     heads = width // HD
+    core = lax.axis_index("tc")
+    half = core if mine else 1 - core
+    columns = pl.ds(pl.multiple_of(half * width, width), width)
+    if not mine:
+        pieces = [(wq_hbm, wq_ref, pl.ds(k * depth, depth)) for k in range(WEIGHT_COPIES)]
+        pieces += [(rows_hbm, rows_ref, pl.ds(k * many, many)) for k in range(chunks)]
+        copies = start_copies([(a.at[k], b.at[k]) for a, b, k in pieces], sems)
+    chunk = many // row_len
     pairs = row_len // PAIR
-    each = kept_ref.shape[0] // pairs
+    each = out_ref.shape[0] // pairs
     body = each - 8
     seqs = body // (heads * PAIR)
-    core = lax.axis_index("tc")
     across = lax.broadcasted_iota(jnp.int32, (chunk, HD), 0)
     lane = lax.broadcasted_iota(jnp.int32, (chunk, HD), 1)
     squares = [jnp.zeros((1, HD), F32) for _ in range(pairs)]
-    for copy in copies[:WEIGHT_COPIES]:
-        copy.wait()
+    if not mine:
+        for copy in copies[:WEIGHT_COPIES]:
+            copy.wait()
     for step in range(chunks):
-        copies[WEIGHT_COPIES + step].wait()
+        if not mine:
+            copies[WEIGHT_COPIES + step].wait()
         rows = rows_ref[step * many : (step + 1) * many, :]
-        for turn, (half, out_ref) in enumerate([(1 - core, theirs_ref), (core, kept_ref)]):
-            columns = pl.ds(pl.multiple_of(half * width, width), width)
-            product = mm(rows, wq_ref[:, columns])
-            slab = (step * 2 + turn) * heads * many
+        product = mm(rows, wq_ref[:, columns])
+        slab = step * heads * many
+        for h in range(heads):
+            acc_ref[slab + h * many : slab + (h + 1) * many, :] = product[:, h * HD : (h + 1) * HD]
+        for t in range(row_len):
             for h in range(heads):
-                acc_ref[slab + h * many : slab + (h + 1) * many, :] = product[
-                    :, h * HD : (h + 1) * HD
+                first = (t // PAIR) * each + (h * PAIR + t % PAIR) * seqs + step * chunk
+                out_ref[first : first + chunk, :] = acc_ref[
+                    rows_at(slab + h * many + t, chunk, row_len), :
                 ]
-            for t in range(row_len):
-                for h in range(heads):
-                    first = (t // PAIR) * each + (h * PAIR + t % PAIR) * seqs + step * chunk
-                    out_ref[first : first + chunk, :] = acc_ref[
-                        rows_at(slab + h * many + t, chunk, row_len), :
-                    ]
+        if mine:
+            continue
         wide_rows = rows.astype(F32)
         sums = jnp.sum(wide_rows * wide_rows, axis=1, keepdims=True)
         sq_ref[step * many : (step + 1) * many, :] = jnp.broadcast_to(sums, (many, HD))
@@ -118,9 +122,12 @@
             picked = jnp.where(spot, sq_ref[rows_at(step * many + t, chunk, row_len), :], 0.0)
             squares[t // PAIR] += jnp.sum(picked, axis=0, keepdims=True)
     for p in range(pairs):
-        tail = jnp.broadcast_to(squares[p], (8, HD))
-        for out_ref in (theirs_ref, kept_ref):
-            out_ref[p * each + body : (p + 1) * each, :] = tail
+        if mine:
+            tail = squares_ref[p * 8 : (p + 1) * 8, :]
+        else:
+            tail = jnp.broadcast_to(squares[p], (8, HD))
+            squares_ref[p * 8 : (p + 1) * 8, :] = tail
+        out_ref[p * each + body : (p + 1) * each, :] = tail
 
 
 def add_kernel(a_ref, b_ref, out_ref):
@@ -208,12 +215,14 @@
     turned = jnp.concatenate([attn[seqs:], attn[:seqs]], axis=0)
     both = jnp.concatenate([attn, turned], axis=1).astype(BF16)
     blocks = w_ref.shape[1] // HD
+    shards = blocks // 4
     for copy in copies[-WEIGHT_COPIES:]:
         copy.wait()
     for first in range(0, blocks, 4):
         part = mm(both, w_ref[:, first * HD : (first + 4) * HD])
         for c in range(4):
-            out_ref[(first + c) * rows : (first + c + 1) * rows, :] = part[:, c * HD : (c + 1) * HD]
+            own = rows_at(c * seqs * shards + first // 4, seqs, shards)
+            out_ref[own, :] = part[:seqs, c * HD : (c + 1) * HD]
     slots = place_ref.shape[0]
     groups = slots // CAP
     down = lax.broadcasted_iota(jnp.int32, (HD, HD), 0)
@@ -273,9 +282,10 @@
     out_ref[:, tile:, :] = attn
 
 
-def score_kernel(index_ref, x_ref, keys_ref, values_ref, weight_ref, delta_ref, out_ref):
-    tile = out_ref.shape[1]
-    seqs = tile // 2
+def score_kernel(
+    seqs, index_ref, x_ref, keys_ref, values_ref, weight_ref, delta_ref, out_ref, lay_ref
+):
+    tile = 2 * seqs
     senders = x_ref.shape[0]
     keys = keys_ref[...]
     keys2 = jnp.concatenate([keys, keys], axis=1)
@@ -286,10 +296,8 @@
     columns = 32
     row_block = block // columns
     column = (block % columns).astype(F32)
-    at_once = min(16, senders)
+    at_once = min(AT_ONCE, senders)
     row = lax.broadcasted_iota(jnp.int32, (1, tile, HD), 1)
-    lane = lax.broadcasted_iota(jnp.int32, (1, tile, HD), 2)
-    named = jnp.logical_and(row == seqs, lane == HD - 1)
     for first in range(0, senders, at_once):
         x = x_ref[first : first + at_once].astype(F32)
         flat = [
@@ -308,17 +316,28 @@
         product = mm(flat[2], delta).reshape(at_once, tile, HD)
         turned = jnp.concatenate([product[:, seqs:], product[:, :seqs]], axis=1)
         result = jnp.where(row_block == 0, product, turned)
-        result = jnp.where(row < seqs, result, jnp.where(named, column, score))
-        out_ref[first : first + at_once] = result
-
-
-def merge_kernel(tile, x_ref, partial_ref, place_ref, out_ref):
-    senders = x_ref.shape[0] // tile
-    blocks = partial_ref.shape[0] // tile
-    seqs = tile // 2
-    column = x_ref[rows_at(seqs, senders, tile), :][:, HD - 1 :]
+        result = jnp.where(row < seqs, result, score)
+        span = slice(first * tile, (first + at_once) * tile)
+        lay_ref[span, :] = result.reshape(at_once * tile, HD)
+    for q in range(seqs):
+        out_ref[rows_at(q, senders, seqs + 1), :] = lay_ref[rows_at(q, senders, tile), :]
+    lane = lax.broadcasted_iota(jnp.int32, (senders, HD), 1)
+    last = jnp.broadcast_to(column, (senders, HD))
+    for q in range(seqs):
+        last = jnp.where(lane == q, lay_ref[rows_at(seqs + q, senders, tile), :], last)
+    out_ref[rows_at(seqs, senders, seqs + 1), :] = last
+
+
+def merge_kernel(seqs, shards, x_ref, partial_ref, place_ref, out_ref):
+    each = seqs + 1
+    senders = x_ref.shape[0] // each
+    blocks = partial_ref.shape[0] // seqs
+    own_blocks = blocks // shards
+    message = out_ref.shape[0] // shards
+    last = x_ref[rows_at(seqs, senders, each), :]
+    column = last[:, HD - 1 :]
     pieces = split3(
-        jnp.concatenate([x_ref[rows_at(s, senders, tile), :] for s in range(seqs)], axis=1)
+        jnp.concatenate([x_ref[rows_at(s, senders, each), :] for s in range(seqs)], axis=1)
     )
     down = lax.broadcasted_iota(jnp.int32, (senders, senders), 0)
     across = lax.broadcasted_iota(jnp.int32, (senders, senders), 1)
@@ -327,40 +346,46 @@
         axis=0,
         keepdims=True,
     )
-    wanted = lax.broadcasted_iota(jnp.int32, (blocks, senders), 0).astype(F32)
+    order = lax.broadcasted_iota(jnp.int32, (blocks, senders), 0)
+    wanted = (order % shards * own_blocks + order // shards).astype(F32)
     pick = jnp.where(wanted == column_across, 1.0, 0.0).astype(BF16)
     high, mid, low = pieces
     added = (mm(pick, low) + mm(pick, mid)) + mm(pick, high)
-    out_ref[...] = partial_ref[...]
-    for s in range(seqs):
-        where = rows_at(s, blocks, tile)
-        out_ref[where, :] = partial_ref[where, :] + added[:, s * HD : (s + 1) * HD]
+    for c in range(own_blocks):
+        for s in range(seqs):
+            q = c * seqs + s
+            out_ref[rows_at(q, shards, message), :] = (
+                partial_ref[q * shards : (q + 1) * shards, :]
+                + added[c * shards : (c + 1) * shards, s * HD : (s + 1) * HD]
+            )
     place = place_ref[...].astype(F32)
-    shards = 8
     for p in range(PAIR):
         score = jnp.concatenate(
-            [x_ref[rows_at(seqs + r * PAIR + p, senders, tile), :] for r in range(CAP)], axis=0
-        )[:, :1]
+            [last[:, r * PAIR + p : r * PAIR + p + 1] for r in range(CAP)], axis=0
+        )
         back = jnp.sum(place * score, axis=0, keepdims=True)
-        out_ref[rows_at(seqs + p, shards, blocks // shards * tile), :] = jnp.broadcast_to(
+        out_ref[rows_at(own_blocks * seqs + p, shards, message), :] = jnp.broadcast_to(
             back, (shards, HD)
         )
 
 
-def final_kernel(tile, x_ref, length_ref, decoded_ref, rewards_ref):
-    seqs = tile // 2
-    total = x_ref[0]
-    for k in range(1, x_ref.shape[0]):
-        total = total + x_ref[k]
-    for c in range(total.shape[0] // tile):
-        decoded_ref[:, c * HD : (c + 1) * HD] = total[c * tile : c * tile + seqs, :].astype(BF16)
+def final_kernel(shards, x_ref, length_ref, decoded_ref, rewards_ref):
+    each = x_ref.shape[0] // shards
+    seqs = decoded_ref.shape[0]
+    body = each - PAIR
+    parts = [x_ref[k * each : (k + 1) * each, :] for k in range(shards)]
+    total = parts[0]
+    for part in parts[1:]:
+        total = total + part
+    for c in range(body // seqs):
+        decoded_ref[:, c * HD : (c + 1) * HD] = total[c * seqs : (c + 1) * seqs, :].astype(BF16)
     length = length_ref[...]
     count = rewards_ref.shape[1]
     reward = jnp.zeros((1, HD), F32)
-    for k in range(x_ref.shape[0]):
+    for k in range(shards):
         for p in range(PAIR):
             token = k // CORES * PAIR + p
-            row = x_ref[k, seqs + p : seqs + p + 1, :]
+            row = parts[k][body + p : body + p + 1, :]
             reward = reward + jnp.where(length > token, row, 0.0)
     rewards_ref[...] = (reward / length)[:, :count]
 
@@ -394,26 +419,33 @@
     slots = CAP * wide_count
     parts = PAIR * heads
     message = parts * finished + 8
-    chunks = 4 if finished % 32 == 0 else 1
+    chunks = 1
     shape = jax.ShapeDtypeStruct
 
     rows = fin_rows.reshape(finished * row_len, features)
     partial = shape((chips * message, HD), F32)
-    theirs, kept = local_call(
-        functools.partial(project_kernel, row_len, chunks),
-        "project",
+    squares_shape = shape((chips * 8, HD), F32)
+    acc = pltpu.VMEM((heads * finished * row_len, HD), F32)
+    theirs, squares, rows, weights = local_call(
+        functools.partial(project_kernel, False, row_len, chunks),
+        "project_theirs",
         (rows, reward_query),
-        [partial, partial],
+        [partial, squares_shape, shape(rows.shape, BF16), shape(reward_query.shape, BF16)],
         [
-            pltpu.VMEM(rows.shape, BF16),
-            pltpu.VMEM(reward_query.shape, BF16),
-            pltpu.VMEM((CORES * heads * finished * row_len, HD), F32),
+            acc,
             pltpu.VMEM((finished * row_len, HD), F32),
             pltpu.SemaphoreType.DMA((WEIGHT_COPIES + chunks,)),
         ],
         fetched=2,
     )
     got = lax.ppermute(theirs, "tc", [(0, 1), (1, 0)])
+    (kept,) = local_call(
+        functools.partial(project_kernel, True, row_len, chunks),
+        "project_kept",
+        (squares, rows, weights),
+        [partial],
+        [acc],
+    )
     (both,) = local_call(add_kernel, "add", (kept, got), [partial])
     summed_tokens = lax.all_to_all(
         both.reshape(chips, message, HD), "th", split_axis=0, concat_axis=0, tiled=True
@@ -431,7 +463,7 @@
         small + large,
         [
             shape((tile, HD), F32),
-            shape((blocks * tile, HD), F32),
+            shape((blocks * seq_count, HD), F32),
             shape((slots, HD), BF16),
             shape((tile, HD), F32),
             shape(delta_values.shape[1:], BF16),
@@ -452,8 +484,9 @@
     )
     received = lax.all_to_all(outgoing, "wide", split_axis=0, concat_axis=0, tiled=True)
 
+    answer = seq_count + 1
     (answers,) = local_call(
-        score_kernel,
+        functools.partial(score_kernel, seq_count),
         "score",
         (
             delta_index,
@@ -463,27 +496,31 @@
             weight_tile,
             delta,
         ),
-        [shape((wide_count, tile, HD), F32)],
+        [shape((wide_count * answer, HD), F32)],
+        [pltpu.VMEM((wide_count * tile, HD), F32)],
         scalars=1,
     )
-    returned = lax.all_to_all(answers, "wide", split_axis=0, concat_axis=0, tiled=True)
-
+    returned = lax.all_to_all(
+        answers.reshape(wide_count, 1, answer * HD), "wide", split_axis=0, concat_axis=0, tiled=True
+    ).reshape(answers.shape)
+
+    share = blocks // tp_count * seq_count + PAIR
     (merged,) = local_call(
-        functools.partial(merge_kernel, tile),
+        functools.partial(merge_kernel, seq_count, tp_count),
         "merge",
-        (returned.reshape(wide_count * tile, HD), partial_out, place),
-        [shape((blocks * tile, HD), F32)],
+        (returned, partial_out, place),
+        [shape((tp_count * share, HD), F32)],
     )
     shares = lax.all_to_all(
-        merged.reshape(tp_count, blocks // tp_count * tile, HD),
+        merged.reshape(tp_count, 1, share * HD),
         ("th", "tc"),
         split_axis=0,
         concat_axis=0,
         tiled=True,
-    )
+    ).reshape(merged.shape)
 
     decoded, rewards = local_call(
-        functools.partial(final_kernel, tile),
+        functools.partial(final_kernel, tp_count),
         "final",
         (shares, lengths),
         [shape((seq_count, blocks // tp_count * HD), BF16), shape((1, finished), F32)],

time: 97.5 us -> 94.2 us (0.966)
  waiting for transfers between devices: 31 us -> 29.9 us
  Pallas kernels: 10.9 us -> 9.87 us
    pallas_call x7 -> x8, Pallas kernels: 10.9 us -> 9.87 us  [local_call(): pl.pallas_call(kernel, in_specs=[smem] * scalars + [vmem] * (kept - scala...]
  transfers between devices with their start and end apart: 4 -> 4, of which waited for: 4 -> 4; matrix products, arithmetic and copies ran while one was open for 1% -> 1% of each run, Pallas kernels for 2% -> 3%
where the time goes in v3:
time: 94.2 us; the launch traced here: 93.7 us
  starting transfers between devices  35.2 us (37%)
  waiting for transfers between devices  29.9 us (32%)
  blocking collectives  16.8 us (18%)
  Pallas kernels  9.87 us (10%)
  between operations  1.37 us (1%)
    all_to_all x1, blocking collectives, per_device(): lax.all_to_all(answers.reshape(wide_count, 1, answer * HD), 'wide', split...  16.8 us
    all_to_all x1, starting transfers between devices, per_device(): lax.all_to_all(outgoing, 'wide', split_axis=0, concat_axis=0, tiled=True)  15.4 us
    all_to_all x1, waiting for transfers between devices, per_device(): lax.all_to_all(outgoing, 'wide', split_axis=0, concat_axis=0, tiled=True)  12 us
    pallas_call x8, Pallas kernels, local_call(): pl.pallas_call(kernel, in_specs=[smem] * scalars + [vmem] * (kept - scala...  9.87 us
    all_to_all x1, waiting for transfers between devices, per_device(): lax.all_to_all(both.reshape(chips, message, HD), 'th', split_axis=0, conc...  9.45 us
    ppermute x1, starting transfers between devices, per_device(): got = lax.ppermute(theirs, 'tc', [(0, 1), (1, 0)])  8.79 us
    all_to_all x1, waiting for transfers between devices, per_device(): lax.all_to_all(merged.reshape(tp_count, 1, share * HD), ('th', 'tc'), spl...  7.42 us
    all_to_all x1, starting transfers between devices, per_device(): lax.all_to_all(merged.reshape(tp_count, 1, share * HD), ('th', 'tc'), spl...  6.34 us
  transfers between devices with their start and end apart: 4, of which 4 were waited for; matrix products, arithmetic and copies ran while one was open for 1% of the time, Pallas kernels for 3%

profile of v3, /device:TPU:1, one launch (start us, length us, event | category | flops | bytes accessed | tf_op | source)
XLA Modules:
  0.0 93.7 jit_solution(13013573507634172238)
XLA Ops:
  0.6 2.1 %project_theirs.1 = (f32[1056,128]{1,0:T(8,128)S(1)}, f32[32,128]{1,0:T(8,128)S(1)}, bf16[512,1024]{1,0:T(8,128)(2,1)S(1)}, bf16[1024,512]{1,0:T(8,128)(2,1)S(1)}) custom-call(bf16[512,1024]{1,0:T(8,128)(2,1)} %bitcast.22, bf16[1024,512]{1,0:T(8,128)(2,1)} %refs_1_.1), custom_call_target="tpu_custom_call" | custom-call | tf_op jit(solution)/shard_map/project_theirs/pallas_call | solution.py:56
  2.8 8.8 %collective-permute-start = (f32[1056,128]{1,0:T(8,128)S(1)}, f32[1056,128]{1,0:T(8,128)S(1)}, u32[]{:S(2)}, u32[]{:S(2)}) collective-permute-start(f32[1056,128]{1,0:T(8,128)S(1)} %get-tuple-element.16), channel_id=1, source_target_pairs={{0,1},{1,0},{2,3},{3,2},{4,5},{5,4},{6,7},{7,6},{8,9},{9,8},{10,11... | collective-permute-start | bytes 1622024 | tf_op jit(solution)/shard_map/ppermute | solution.py:441
  11.5 0.0 copy-start.2
  11.6 0.5 project_kept.1.a_ref
  12.0 1.0 %collective-permute-done.b_ref = f32[1056,128]{1,0:T(8,128)S(1)} collective-permute-done((f32[1056,128]{1,0:T(8,128)S(1)}, f32[1056,128]{1,0:T(8,128)S(1)}, u32[]{:S(2)}, u32[]{:S(2)}) %collective-permute-start) | collective-permute-done | bytes 540704 | tf_op jit(solution)/shard_map/ppermute | solution.py:441
  13.1 0.9 add.5
  13.9 4.6 %all-to-all-start = ((f32[4,264,128]{2,1,0:T(8,128)}), f32[4,264,128]{2,1,0:T(8,128)S(1)}, u32[]{:S(2)}, u32[]{:S(2)}) async-start(f32[4,264,128]{2,1,0:T(8,128)} %bitcast.1), calls=%async_computation | async-start | bytes 1081344 | tf_op jit(solution)/shard_map/all_to_all | solution.py:450
  18.6 0.0 copy-done.2
  18.6 0.5 pad.7.route_hbm
  19.1 2.2 %decode.1 = (f32[8,128]{1,0:T(8,128)S(1)}, f32[128,128]{1,0:T(8,128)S(1)}, bf16[128,128]{1,0:T(8,128)(2,1)S(1)}, f32[8,128]{1,0:T(8,128)S(1)}, bf16[128,128]{1,0:T(8,128)(2,1)S(1)}) custom-call(s32[4]{0:T(128)} %lens_hbm.1, bf16[4,256]{1,0:T(4,128)(2,1)} %q_hbm.1, bf16[4,128]{1,0:T(4,128)(2,1)} %nk_hbm.1, bf16[4,128]{1,0:T(4,128)(2,1)} %nv_hbm.1, ...), custom_call_target="tpu_custom_call" | custom-call | tf_op jit(solution)/shard_map/decode/pallas_call | solution.py:56
  21.4 0.0 copy-start.3
  21.4 9.4 %all-to-all-done = f32[4,264,128]{2,1,0:T(8,128)S(1)} async-done(((f32[4,264,128]{2,1,0:T(8,128)}), f32[4,264,128]{2,1,0:T(8,128)S(1)}, u32[]{:S(2)}, u32[]{:S(2)}) %all-to-all-start) | async-done | bytes 540704 | tf_op jit(solution)/shard_map/all_to_all | solution.py:450
  30.8 1.1 %place.1 = bf16[64,24,128]{2,1,0:T(8,128)(2,1)} custom-call(f32[1056,128]{1,0:T(8,128)S(1)} %bitcast.16, f32[8,128]{1,0:T(8,128)S(1)} %get-tuple-element.17.attn_ref, bf16[128,128]{1,0:T(8,128)(2,1)S(1)} %get-tuple-element.18.place_ref), custom_call_target="tpu_custom_call" | custom-call | tf_op jit(solution)/shard_map/place/pallas_call | solution.py:56
  32.0 15.4 %all-to-all-start.1 = ((bf16[64,24,128]{2,1,0:T(8,128)(2,1)}), bf16[64,24,128]{2,1,0:T(8,128)(2,1)S(1)}, u32[]{:S(2)}, u32[]{:S(2)}) async-start(bf16[64,24,128]{2,1,0:T(8,128)(2,1)} %place.1), calls=%async_computation.1 | async-start | bytes 786432 | tf_op jit(solution)/shard_map/all_to_all | solution.py:485
  48.1 12.0 %all-to-all-done.1.x_ref = bf16[64,24,128]{2,1,0:T(8,128)(2,1)S(1)} async-done(((bf16[64,24,128]{2,1,0:T(8,128)(2,1)}), bf16[64,24,128]{2,1,0:T(8,128)(2,1)S(1)}, u32[]{:S(2)}, u32[]{:S(2)}) %all-to-all-start.1) | async-done | bytes 393248 | tf_op jit(solution)/shard_map/all_to_all | solution.py:485
  60.1 0.0 copy-done
  60.1 0.0 copy-done.1
  60.1 1.6 %score.1 = f32[320,128]{1,0:T(8,128)S(1)} custom-call(s32[1]{0:T(128)S(6)} %copy.20.index_ref, bf16[64,24,128]{2,1,0:T(8,128)(2,1)S(1)} %all-to-all-done.1.x_ref, bf16[1024,128]{1,0:T(8,128)(2,1)S(1)} %bitcast.20, bf16[1024,128]{1,0:T(8,128)(2,1)S(1)} %bitcast.21, f32[8,128]{1,0:T(8,128)S(1)} %get-tuple-element.19.weight_ref, ...), custom_call_target="tpu_custom_call" | custom-call | tf_op jit(solution)/shard_map/score/pallas_call | solution.py:56
  61.6 16.8 %all_to_all.20 = f32[64,1,640]{2,1,0:T(1,128)S(1)} all-to-all(f32[64,1,640]{2,1,0:T(1,128)S(1)} %bitcast.18), channel_id=1, replica_groups=mesh['wide'=64,'th'=4,'tc'=2] {'wide'}, dimensions={0} | all-to-all | bytes 327680 | tf_op jit(solution)/shard_map/all_to_all | solution.py:503
  78.5 0.9 merge.1
  79.4 6.3 %all-to-all-start.3 = ((f32[8,1,2304]{2,1,0:T(1,128)}), f32[8,1,2304]{2,1,0:T(1,128)S(1)}, u32[]{:S(2)}, u32[]{:S(2)}) async-start(f32[8,1,2304]{2,1,0:T(1,128)} %bitcast.10), calls=%async_computation.3 | async-start | bytes 147456 | tf_op jit(solution)/shard_map/all_to_all | solution.py:514
  85.7 0.0 copy-done.3
  85.7 7.4 %all-to-all-done.3 = f32[8,1,2304]{2,1,0:T(1,128)S(1)} async-done(((f32[8,1,2304]{2,1,0:T(1,128)}), f32[8,1,2304]{2,1,0:T(1,128)S(1)}, u32[]{:S(2)}, u32[]{:S(2)}) %all-to-all-start.3) | async-done | bytes 73760 | tf_op jit(solution)/shard_map/all_to_all | solution.py:514
  93.1 0.6 final.1
  (5 shorter events, 0.0 us)
Async XLA Ops:
  2.8 10.3 %collective-permute-start = (f32[1056,128]{1,0:T(8,128)S(1)}, f32[1056,128]{1,0:T(8,128)S(1)}, u32[]{:S(2)}, u32[]{:S(2)}) collective-permute-start(f32[1056,128]{1,0:T(8,128)S(1)} %get-tuple-element.16), channel_id=1, source_target_pairs={{0,1},{1,0},{2,3},{3,2},{4,5},{5,4},{6,7},{7,6},{8,9},{9,8},{10,11... | collective-permute-start | bytes 1622024 | tf_op jit(solution)/shard_map/ppermute | solution.py:441
  11.5 7.0 %copy-start.2 = (s32[64,1]{0,1:T(1,128)S(1)}, s32[64,1]{0,1:T(1,128)}, u32[]{:S(2)}) copy-start(s32[64,1]{0,1:T(1,128)} %param.25) | copy-start | bytes 772
  13.9 16.9 %all-to-all-start = ((f32[4,264,128]{2,1,0:T(8,128)}), f32[4,264,128]{2,1,0:T(8,128)S(1)}, u32[]{:S(2)}, u32[]{:S(2)}) async-start(f32[4,264,128]{2,1,0:T(8,128)} %bitcast.1), calls=%async_computation | async-start | bytes 1081344 | tf_op jit(solution)/shard_map/all_to_all | solution.py:450
  18.6 41.5 %copy-start = (bf16[1,1024,128]{2,1,0:T(8,128)(2,1)S(1)}, bf16[1,1024,128]{2,1,0:T(8,128)(2,1)}, u32[]{:S(2)}) copy-start(bf16[1,1024,128]{2,1,0:T(8,128)(2,1)} %param.29) | copy-start | bytes 786436
  18.6 41.5 %copy-start.1 = (bf16[1,1024,128]{2,1,0:T(8,128)(2,1)S(1)}, bf16[1,1024,128]{2,1,0:T(8,128)(2,1)}, u32[]{:S(2)}) copy-start(bf16[1,1024,128]{2,1,0:T(8,128)(2,1)} %param.30) | copy-start | bytes 786436
  21.4 64.3 %copy-start.3 = (s32[64]{0:T(128)S(1)}, s32[64]{0:T(128)}, u32[]{:S(2)}) copy-start(s32[64]{0:T(128)} %param.26) | copy-start | bytes 772
  32.0 28.1 %all-to-all-start.1 = ((bf16[64,24,128]{2,1,0:T(8,128)(2,1)}), bf16[64,24,128]{2,1,0:T(8,128)(2,1)S(1)}, u32[]{:S(2)}, u32[]{:S(2)}) async-start(bf16[64,24,128]{2,1,0:T(8,128)(2,1)} %place.1), calls=%async_computation.1 | async-start | bytes 786432 | tf_op jit(solution)/shard_map/all_to_all | solution.py:485
  79.4 13.8 %all-to-all-start.3 = ((f32[8,1,2304]{2,1,0:T(1,128)}), f32[8,1,2304]{2,1,0:T(1,128)S(1)}, u32[]{:S(2)}, u32[]{:S(2)}) async-start(f32[8,1,2304]{2,1,0:T(1,128)} %bitcast.10), calls=%async_computation.3 | async-start | bytes 147456 | tf_op jit(solution)/shard_map/all_to_all | solution.py:514

commit v4 on v3

--- a/solution.py
+++ b/solution.py
@@ -42,20 +42,16 @@
     return pl.ds(first, count, stride=stride)
 
 
-def local_call(kernel, name, operands, outs, scratch=(), scalars=0, fetched=0, pinned=()):
+def local_call(kernel, name, operands, outs, scratch=(), fetched=0):
     vmem = pl.BlockSpec(memory_space=pltpu.VMEM)
-    smem = pl.BlockSpec(memory_space=pltpu.SMEM)
     hbm = pl.BlockSpec(memory_space=pltpu.HBM)
     kept = len(operands) - fetched
-    operands = list(operands)
-    for k in range(len(operands)):
-        if k >= kept:
-            operands[k] = pltpu.with_memory_space_constraint(operands[k], pltpu.HBM)
-        elif k in pinned:
-            operands[k] = pltpu.with_memory_space_constraint(operands[k], pltpu.VMEM)
+    operands = list(operands[:kept]) + [
+        pltpu.with_memory_space_constraint(a, pltpu.HBM) for a in operands[kept:]
+    ]
     return pl.pallas_call(
         kernel,
-        in_specs=[smem] * scalars + [vmem] * (kept - scalars) + [hbm] * fetched,
+        in_specs=[vmem] * kept + [hbm] * fetched,
         out_specs=[vmem] * len(outs),
         out_shape=outs,
         scratch_shapes=list(scratch),
@@ -84,9 +80,12 @@
     half = core if mine else 1 - core
     columns = pl.ds(pl.multiple_of(half * width, width), width)
     if not mine:
-        pieces = [(wq_hbm, wq_ref, pl.ds(k * depth, depth)) for k in range(WEIGHT_COPIES)]
-        pieces += [(rows_hbm, rows_ref, pl.ds(k * many, many)) for k in range(chunks)]
-        copies = start_copies([(a.at[k], b.at[k]) for a, b, k in pieces], sems)
+        kept = pl.ds(pl.multiple_of(core * width, width), width)
+        weights = [pl.ds(k * depth, depth) for k in range(WEIGHT_COPIES)]
+        pieces = [(wq_hbm.at[k, columns], wq_ref.at[k, columns]) for k in weights]
+        pieces += [(rows_hbm, rows_ref)]
+        pieces += [(wq_hbm.at[k, kept], wq_ref.at[k, kept]) for k in weights]
+        copies = start_copies(pieces, sems)
     chunk = many // row_len
     pairs = row_len // PAIR
     each = out_ref.shape[0] // pairs
@@ -96,11 +95,9 @@
     lane = lax.broadcasted_iota(jnp.int32, (chunk, HD), 1)
     squares = [jnp.zeros((1, HD), F32) for _ in range(pairs)]
     if not mine:
-        for copy in copies[:WEIGHT_COPIES]:
+        for copy in copies[: WEIGHT_COPIES + 1]:
             copy.wait()
     for step in range(chunks):
-        if not mine:
-            copies[WEIGHT_COPIES + step].wait()
         rows = rows_ref[step * many : (step + 1) * many, :]
         product = mm(rows, wq_ref[:, columns])
         slab = step * heads * many
@@ -121,6 +118,9 @@
             spot = lane == across + ((t % PAIR) * seqs + step * chunk)
             picked = jnp.where(spot, sq_ref[rows_at(step * many + t, chunk, row_len), :], 0.0)
             squares[t // PAIR] += jnp.sum(picked, axis=0, keepdims=True)
+    if not mine:
+        for copy in copies[WEIGHT_COPIES + 1 :]:
+            copy.wait()
     for p in range(pairs):
         if mine:
             tail = squares_ref[p * 8 : (p + 1) * 8, :]
@@ -150,6 +150,7 @@
     place_ref,
     tile_ref,
     delta_ref,
+    length_ref,
     lens_ref,
     q_ref,
     nk_ref,
@@ -227,14 +228,15 @@
     groups = slots // CAP
     down = lax.broadcasted_iota(jnp.int32, (HD, HD), 0)
     across = lax.broadcasted_iota(jnp.int32, (HD, HD), 1)
-    target = jnp.broadcast_to(route_ref[...], (HD, HD))
+    route = route_ref[0:1, :]
+    target = jnp.broadcast_to(route, (HD, HD))
     target_down = jnp.sum(jnp.where(down == across, target, 0.0), axis=1, keepdims=True)
     earlier = jnp.where(jnp.logical_and(target == target_down, down < across), 1.0, 0.0)
     rank = jnp.sum(earlier, axis=0, keepdims=True)
     slot = lax.broadcasted_iota(jnp.int32, (slots, HD), 0)
     group = (slot % groups).astype(F32)
     order = (slot // groups).astype(F32)
-    held = jnp.logical_and(route_ref[...] == group, rank == order)
+    held = jnp.logical_and(route == group, rank == order)
     place_ref[...] = jnp.where(held, 1.0, 0.0).astype(BF16)
     weight = score_ref[...].astype(F32)
     heads = weight.shape[0] // CORES
@@ -242,6 +244,11 @@
     for h in range(heads):
         own = slice(h * rows // heads, (h + 1) * rows // heads)
         tile_ref[own, :] = jnp.broadcast_to(weight[h : h + 1], (rows // heads, HD))
+    block = jnp.broadcast_to(route_ref[2:3, :], (8, HD))
+    row_block = jnp.floor(block / blocks)
+    tile_ref[rows : rows + 8, :] = row_block
+    tile_ref[rows + 8 : rows + 16, :] = block - row_block * blocks
+    length_ref[...] = jnp.broadcast_to(route_ref[1:2, :], length_ref.shape)
 
 
 def place_kernel(sources, x_ref, attn_ref, place_ref, out_ref, lay_ref):
@@ -283,19 +290,17 @@
 
 
 def score_kernel(
-    seqs, index_ref, x_ref, keys_ref, values_ref, weight_ref, delta_ref, out_ref, lay_ref
+    seqs, x_ref, keys_ref, values_ref, weight_ref, delta_ref, out_ref, lay_ref
 ):
     tile = 2 * seqs
     senders = x_ref.shape[0]
     keys = keys_ref[...]
     keys2 = jnp.concatenate([keys, keys], axis=1)
     values = values_ref[...]
-    weight = weight_ref[...][None]
+    weight = weight_ref[0:tile, :][None]
+    row_block = weight_ref[tile : tile + 1, :][None]
+    column = weight_ref[tile + 8 : tile + 9, :]
     delta = delta_ref[...]
-    block = index_ref[0]
-    columns = 32
-    row_block = block // columns
-    column = (block % columns).astype(F32)
     at_once = min(AT_ONCE, senders)
     row = lax.broadcasted_iota(jnp.int32, (1, tile, HD), 1)
     for first in range(0, senders, at_once):
@@ -315,7 +320,7 @@
         score = by_head + jnp.concatenate([by_head[:, seqs:], by_head[:, :seqs]], axis=1)
         product = mm(flat[2], delta).reshape(at_once, tile, HD)
         turned = jnp.concatenate([product[:, seqs:], product[:, :seqs]], axis=1)
-        result = jnp.where(row_block == 0, product, turned)
+        result = jnp.where(row_block == 0.0, product, turned)
         result = jnp.where(row < seqs, result, score)
         span = slice(first * tile, (first + at_once) * tile)
         lay_ref[span, :] = result.reshape(at_once * tile, HD)
@@ -379,7 +384,7 @@
         total = total + part
     for c in range(body // seqs):
         decoded_ref[:, c * HD : (c + 1) * HD] = total[c * seqs : (c + 1) * seqs, :].astype(BF16)
-    length = length_ref[...]
+    length = length_ref[0:1, :]
     count = rewards_ref.shape[1]
     reward = jnp.zeros((1, HD), F32)
     for k in range(shards):
@@ -434,7 +439,7 @@
         [
             acc,
             pltpu.VMEM((finished * row_len, HD), F32),
-            pltpu.SemaphoreType.DMA((WEIGHT_COPIES + chunks,)),
+            pltpu.SemaphoreType.DMA((2 * WEIGHT_COPIES + 1,)),
         ],
         fetched=2,
     )
@@ -452,12 +457,17 @@
     ).reshape(partial.shape)
 
     pad = ((0, 0), (0, HD - finished))
-    route = jnp.pad(fin_route.reshape(1, finished).astype(F32), pad, constant_values=-1.0)
-    lengths = jnp.pad(fin_lengths.reshape(1, finished).astype(F32), pad, constant_values=1.0)
+    routing = jnp.concatenate(
+        [
+            jnp.pad(fin_route.reshape(1, finished), pad, constant_values=-1),
+            jnp.pad(fin_lengths.reshape(1, finished), pad, constant_values=1),
+            jnp.broadcast_to(delta_index.reshape(1, 1), (1, HD)),
+        ]
+    ).astype(F32)
     weights = score_weight.reshape(heads * CORES, HD)
-    small = (cache_lengths, query, new_key, new_value, route, weights, delta_values[0])
+    small = (cache_lengths, query, new_key, new_value, routing, weights, delta_values[0])
     large = (key_cache, value_cache, out_weight)
-    attn, partial_out, place, weight_tile, delta = local_call(
+    attn, partial_out, place, weight_tile, delta, lengths = local_call(
         decode_kernel,
         "decode",
         small + large,
@@ -465,8 +475,9 @@
             shape((tile, HD), F32),
             shape((blocks * seq_count, HD), F32),
             shape((slots, HD), BF16),
-            shape((tile, HD), F32),
+            shape((tile + 16, HD), F32),
             shape(delta_values.shape[1:], BF16),
+            shape((8, HD), F32),
         ],
         [pltpu.SMEM(cache_lengths.shape, jnp.int32)]
         + [pltpu.VMEM(a.shape, a.dtype) for a in small[1:-1] + large]
@@ -489,7 +500,6 @@
         functools.partial(score_kernel, seq_count),
         "score",
         (
-            delta_index,
             received,
             rubric_keys[0],
             rubric_values[0],
@@ -498,7 +508,6 @@
         ),
         [shape((wide_count * answer, HD), F32)],
         [pltpu.VMEM((wide_count * tile, HD), F32)],
-        scalars=1,
     )
     returned = lax.all_to_all(
         answers.reshape(wide_count, 1, answer * HD), "wide", split_axis=0, concat_axis=0, tiled=True

time: 94.2 us -> 92 us (0.977)
  blocking collectives: 16.8 us -> 58 us
  starting transfers between devices: 35.2 us -> 13.4 us
  waiting for transfers between devices: 29.9 us -> 9.59 us
  Pallas kernels: 9.87 us -> 8.49 us
    all_to_all x0 -> x2, blocking collectives: none -> 41.2 us  [the longest x1 27.9 us: per_device(): lax.all_to_all(outgoing, 'wide', split_axis=0, concat_axis=0, tiled=True)]
    all_to_all x2 -> x0, starting transfers between devices: 21.8 us -> none  [the longest x1 15.4 us: per_device(): lax.all_to_all(outgoing, 'wide', split_axis=0, concat_axis=0, tiled=True)]
    all_to_all x2 -> x0, waiting for transfers between devices: 19.4 us -> none  [the longest x1 12 us: per_device(): lax.all_to_all(outgoing, 'wide', split_axis=0, concat_axis=0, tiled=True)]
    pallas_call x8, Pallas kernels: 9.87 us -> 8.49 us  [local_call(): pl.pallas_call(kernel, in_specs=[vmem] * kept + [hbm] * fetched, out_spec...]
  transfers between devices with their start and end apart: 4 -> 2, of which waited for: 4 -> 2; matrix products, arithmetic and copies ran while one was open for 1% -> 1% of each run, Pallas kernels for 3% -> 3%
where the time goes in v4:
time: 92 us; the launch traced here: 91.7 us
  blocking collectives  58 us (63%)
  starting transfers between devices  13.4 us (15%)
  waiting for transfers between devices  9.59 us (10%)
  Pallas kernels  8.49 us (9%)
  between operations  1.41 us (2%)
    all_to_all x1, blocking collectives, per_device(): lax.all_to_all(outgoing, 'wide', split_axis=0, concat_axis=0, tiled=True)  27.9 us
    all_to_all x1, blocking collectives, per_device(): lax.all_to_all(answers.reshape(wide_count, 1, answer * HD), 'wide', split...  16.8 us
    all_to_all x1, blocking collectives, per_device(): lax.all_to_all(merged.reshape(tp_count, 1, share * HD), ('th', 'tc'), spl...  13.3 us
    ppermute x1, starting transfers between devices, per_device(): got = lax.ppermute(theirs, 'tc', [(0, 1), (1, 0)])  8.79 us
    all_to_all x1, waiting for transfers between devices, per_device(): lax.all_to_all(both.reshape(chips, message, HD), 'th', split_axis=0, conc...  8.56 us
    pallas_call x8, Pallas kernels, local_call(): pl.pallas_call(kernel, in_specs=[vmem] * kept + [hbm] * fetched, out_spec...  8.49 us
    all_to_all x1, starting transfers between devices, per_device(): lax.all_to_all(both.reshape(chips, message, HD), 'th', split_axis=0, conc...  4.64 us
  transfers between devices with their start and end apart: 2, of which 2 were waited for; matrix products, arithmetic and copies ran while one was open for 1% of the time, Pallas kernels for 3%

profile of v4, /device:TPU:1, one launch (start us, length us, event | category | flops | bytes accessed | tf_op | source)
XLA Modules:
  0.0 91.7 jit_solution(15269318779182915078)
XLA Ops:
  0.6 2.1 %project_theirs.1 = (f32[1056,128]{1,0:T(8,128)S(1)}, f32[32,128]{1,0:T(8,128)S(1)}, bf16[512,1024]{1,0:T(8,128)(2,1)S(1)}, bf16[1024,512]{1,0:T(8,128)(2,1)S(1)}) custom-call(bf16[512,1024]{1,0:T(8,128)(2,1)} %bitcast.22, bf16[1024,512]{1,0:T(8,128)(2,1)} %refs_1_.1), custom_call_target="tpu_custom_call" | custom-call | tf_op jit(solution)/shard_map/project_theirs/pallas_call | solution.py:52
  2.7 8.8 %collective-permute-start = (f32[1056,128]{1,0:T(8,128)S(1)}, f32[1056,128]{1,0:T(8,128)S(1)}, u32[]{:S(2)}, u32[]{:S(2)}) collective-permute-start(f32[1056,128]{1,0:T(8,128)S(1)} %get-tuple-element.17), channel_id=1, source_target_pairs={{0,1},{1,0},{2,3},{3,2},{4,5},{5,4},{6,7},{7,6},{8,9},{9,8},{10,11... | collective-permute-start | bytes 1622024 | tf_op jit(solution)/shard_map/ppermute | solution.py:446
  11.5 0.0 copy-start.2
  11.6 0.0 copy-start.3
  11.6 0.5 project_kept.1.a_ref
  12.0 1.0 %collective-permute-done.b_ref = f32[1056,128]{1,0:T(8,128)S(1)} collective-permute-done((f32[1056,128]{1,0:T(8,128)S(1)}, f32[1056,128]{1,0:T(8,128)S(1)}, u32[]{:S(2)}, u32[]{:S(2)}) %collective-permute-start) | collective-permute-done | bytes 540704 | tf_op jit(solution)/shard_map/ppermute | solution.py:446
  13.1 0.9 add.15
  13.9 4.6 %all-to-all-start = ((f32[4,264,128]{2,1,0:T(8,128)}), f32[4,264,128]{2,1,0:T(8,128)S(1)}, u32[]{:S(2)}, u32[]{:S(2)}) async-start(f32[4,264,128]{2,1,0:T(8,128)} %bitcast.1), calls=%async_computation | async-start | bytes 1081344 | tf_op jit(solution)/shard_map/all_to_all | solution.py:455
  18.6 0.0 copy-start
  19.3 0.1 pad.11.clone
  19.4 0.0 copy-done.2
  19.4 0.0 copy-done.3
  19.4 0.6 fusion.1.route_hbm
  20.0 2.2 %decode.1 = (f32[8,128]{1,0:T(8,128)S(1)}, f32[128,128]{1,0:T(8,128)S(1)}, bf16[128,128]{1,0:T(8,128)(2,1)S(1)}, f32[24,128]{1,0:T(8,128)S(1)}, bf16[128,128]{1,0:T(8,128)(2,1)S(1)}, /*index=5*/f32[8,128]{1,0:T(8,128)S(1)}) custom-call(s32[4]{0:T(128)} %lens_hbm.1, bf16[4,256]{1,0:T(4,128)(2,1)} %q_hbm.1, bf16[4,128]{1,0:T(4,128)(2,1)} %nk_hbm.1, ...), custom_call_target="tpu_custom_call" | custom-call | tf_op jit(solution)/shard_map/decode/pallas_call | solution.py:52
  22.3 8.6 %all-to-all-done = f32[4,264,128]{2,1,0:T(8,128)S(1)} async-done(((f32[4,264,128]{2,1,0:T(8,128)}), f32[4,264,128]{2,1,0:T(8,128)S(1)}, u32[]{:S(2)}, u32[]{:S(2)}) %all-to-all-start) | async-done | bytes 540704 | tf_op jit(solution)/shard_map/all_to_all | solution.py:455
  30.8 0.4 place.1
  31.2 27.9 %all_to_all.20.x_ref = bf16[64,24,128]{2,1,0:T(8,128)(2,1)S(1)} all-to-all(bf16[64,24,128]{2,1,0:T(8,128)(2,1)S(1)} %place.1), channel_id=1, replica_groups=mesh['wide'=64,'th'=4,'tc'=2] {'wide'}, dimensions={0} | all-to-all | bytes 786432 | tf_op jit(solution)/shard_map/all_to_all | solution.py:496
  59.1 0.0 copy-done
  59.1 0.0 copy-done.1
  59.1 1.6 %score.1 = f32[320,128]{1,0:T(8,128)S(1)} custom-call(bf16[64,24,128]{2,1,0:T(8,128)(2,1)S(1)} %all_to_all.20.x_ref, bf16[1024,128]{1,0:T(8,128)(2,1)S(1)} %bitcast.20, bf16[1024,128]{1,0:T(8,128)(2,1)S(1)} %bitcast.21, f32[24,128]{1,0:T(8,128)S(1)} %get-tuple-element.20.weight_ref, bf16[128,128]{1,0:T(8,128)(2,1)S(1)} %get-tuple-element.21.delta_ref), custom_call_target="tpu_custom_call" | custom-call | tf_op jit(solution)/shard_map/score/pallas_call | solution.py:52
  60.7 16.8 %all_to_all.21 = f32[64,1,640]{2,1,0:T(1,128)S(1)} all-to-all(f32[64,1,640]{2,1,0:T(1,128)S(1)} %bitcast.16), channel_id=1, replica_groups=mesh['wide'=64,'th'=4,'tc'=2] {'wide'}, dimensions={0} | all-to-all | bytes 327680 | tf_op jit(solution)/shard_map/all_to_all | solution.py:512
  77.5 0.2 merge.1
  77.8 13.3 %all_to_all.22 = f32[8,1,2304]{2,1,0:T(1,128)S(1)} all-to-all(f32[8,1,2304]{2,1,0:T(1,128)S(1)} %bitcast.19), channel_id=1, replica_groups=mesh['wide'=64,'th'=4,'tc'=2] {'th','tc'}, dimensions={0} | all-to-all | bytes 147456 | tf_op jit(solution)/shard_map/all_to_all | solution.py:523
  91.1 0.6 final.1
  (1 shorter events, 0.0 us)
Async XLA Ops:
  2.7 10.3 %collective-permute-start = (f32[1056,128]{1,0:T(8,128)S(1)}, f32[1056,128]{1,0:T(8,128)S(1)}, u32[]{:S(2)}, u32[]{:S(2)}) collective-permute-start(f32[1056,128]{1,0:T(8,128)S(1)} %get-tuple-element.17), channel_id=1, source_target_pairs={{0,1},{1,0},{2,3},{3,2},{4,5},{5,4},{6,7},{7,6},{8,9},{9,8},{10,11... | collective-permute-start | bytes 1622024 | tf_op jit(solution)/shard_map/ppermute | solution.py:446
  11.5 7.8 %copy-start.2 = (s32[64]{0:T(128)S(1)}, s32[64]{0:T(128)}, u32[]{:S(2)}) copy-start(s32[64]{0:T(128)} %param.26) | copy-start | bytes 772
  11.6 7.8 %copy-start.3 = (s32[64,1]{0,1:T(1,128)S(1)}, s32[64,1]{0,1:T(1,128)}, u32[]{:S(2)}) copy-start(s32[64,1]{0,1:T(1,128)} %param.25) | copy-start | bytes 772
  13.9 16.9 %all-to-all-start = ((f32[4,264,128]{2,1,0:T(8,128)}), f32[4,264,128]{2,1,0:T(8,128)S(1)}, u32[]{:S(2)}, u32[]{:S(2)}) async-start(f32[4,264,128]{2,1,0:T(8,128)} %bitcast.1), calls=%async_computation | async-start | bytes 1081344 | tf_op jit(solution)/shard_map/all_to_all | solution.py:455
  18.6 40.5 %copy-start = (bf16[1,1024,128]{2,1,0:T(8,128)(2,1)S(1)}, bf16[1,1024,128]{2,1,0:T(8,128)(2,1)}, u32[]{:S(2)}) copy-start(bf16[1,1024,128]{2,1,0:T(8,128)(2,1)} %param.29) | copy-start | bytes 786436
  18.6 40.5 %copy-start.1 = (bf16[1,1024,128]{2,1,0:T(8,128)(2,1)S(1)}, bf16[1,1024,128]{2,1,0:T(8,128)(2,1)}, u32[]{:S(2)}) copy-start(bf16[1,1024,128]{2,1,0:T(8,128)(2,1)} %param.30) | copy-start | bytes 786436

commit v5 on v4

--- a/solution.py
+++ b/solution.py
@@ -15,6 +15,7 @@
 PAIR = 2
 VMEM_LIMIT = 16 * 2**20
 WEIGHT_COPIES = 4
+FEATURE_COPIES = 2
 AT_ONCE = 32
 F32 = jnp.float32
 BF16 = jnp.bfloat16
@@ -67,67 +68,71 @@
     return copies
 
 
-def project_kernel(mine, row_len, chunks, *refs):
+def project_kernel(mine, row_len, *refs):
     if mine:
         squares_ref, rows_ref, wq_ref, out_ref, acc_ref = refs
     else:
         rows_hbm, wq_hbm, out_ref, squares_ref, rows_ref, wq_ref, acc_ref, sq_ref, sems = refs
-    many = rows_ref.shape[0] // chunks
-    depth = wq_ref.shape[0] // WEIGHT_COPIES
+    many = rows_ref.shape[0]
     width = wq_ref.shape[1] // CORES
     heads = width // HD
     core = lax.axis_index("tc")
     half = core if mine else 1 - core
     columns = pl.ds(pl.multiple_of(half * width, width), width)
+    steps = 1 if mine else FEATURE_COPIES
+    depth = wq_ref.shape[0] // steps
+    spans = [pl.ds(k * depth, depth) for k in range(steps)]
     if not mine:
         kept = pl.ds(pl.multiple_of(core * width, width), width)
-        weights = [pl.ds(k * depth, depth) for k in range(WEIGHT_COPIES)]
-        pieces = [(wq_hbm.at[k, columns], wq_ref.at[k, columns]) for k in weights]
-        pieces += [(rows_hbm, rows_ref)]
-        pieces += [(wq_hbm.at[k, kept], wq_ref.at[k, kept]) for k in weights]
+        pieces = []
+        for k in spans:
+            pieces += [(wq_hbm.at[k, columns], wq_ref.at[k, columns])]
+            pieces += [(rows_hbm.at[:, k], rows_ref.at[:, k])]
+        pieces += [(wq_hbm.at[:, kept], wq_ref.at[:, kept])]
         copies = start_copies(pieces, sems)
     chunk = many // row_len
     pairs = row_len // PAIR
     each = out_ref.shape[0] // pairs
     body = each - 8
     seqs = body // (heads * PAIR)
+    product = sums = None
+    for step, k in enumerate(spans):
+        if not mine:
+            copies[2 * step].wait()
+            copies[2 * step + 1].wait()
+        rows = rows_ref[:, k]
+        part = mm(rows, wq_ref[k, columns])
+        product = part if product is None else product + part
+        if not mine:
+            wide_rows = rows.astype(F32)
+            wide_rows = wide_rows * wide_rows
+            for first in range(0, depth, HD):
+                slab = wide_rows[:, first : first + HD]
+                sums = slab if sums is None else sums + slab
+    for h in range(heads):
+        acc_ref[h * many : (h + 1) * many, :] = product[:, h * HD : (h + 1) * HD]
+    for t in range(row_len):
+        for h in range(heads):
+            first = (t // PAIR) * each + (h * PAIR + t % PAIR) * seqs
+            out_ref[first : first + chunk, :] = acc_ref[rows_at(h * many + t, chunk, row_len), :]
+    if mine:
+        for p in range(pairs):
+            tail = slice(p * each + body, (p + 1) * each)
+            out_ref[tail, :] = squares_ref[p * 8 : (p + 1) * 8, :]
+        return
+    sq_ref[...] = jnp.broadcast_to(jnp.sum(sums, axis=1, keepdims=True), sq_ref.shape)
     across = lax.broadcasted_iota(jnp.int32, (chunk, HD), 0)
     lane = lax.broadcasted_iota(jnp.int32, (chunk, HD), 1)
-    squares = [jnp.zeros((1, HD), F32) for _ in range(pairs)]
-    if not mine:
-        for copy in copies[: WEIGHT_COPIES + 1]:
-            copy.wait()
-    for step in range(chunks):
-        rows = rows_ref[step * many : (step + 1) * many, :]
-        product = mm(rows, wq_ref[:, columns])
-        slab = step * heads * many
-        for h in range(heads):
-            acc_ref[slab + h * many : slab + (h + 1) * many, :] = product[:, h * HD : (h + 1) * HD]
-        for t in range(row_len):
-            for h in range(heads):
-                first = (t // PAIR) * each + (h * PAIR + t % PAIR) * seqs + step * chunk
-                out_ref[first : first + chunk, :] = acc_ref[
-                    rows_at(slab + h * many + t, chunk, row_len), :
-                ]
-        if mine:
-            continue
-        wide_rows = rows.astype(F32)
-        sums = jnp.sum(wide_rows * wide_rows, axis=1, keepdims=True)
-        sq_ref[step * many : (step + 1) * many, :] = jnp.broadcast_to(sums, (many, HD))
-        for t in range(row_len):
-            spot = lane == across + ((t % PAIR) * seqs + step * chunk)
-            picked = jnp.where(spot, sq_ref[rows_at(step * many + t, chunk, row_len), :], 0.0)
-            squares[t // PAIR] += jnp.sum(picked, axis=0, keepdims=True)
-    if not mine:
-        for copy in copies[WEIGHT_COPIES + 1 :]:
-            copy.wait()
     for p in range(pairs):
-        if mine:
-            tail = squares_ref[p * 8 : (p + 1) * 8, :]
-        else:
-            tail = jnp.broadcast_to(squares[p], (8, HD))
-            squares_ref[p * 8 : (p + 1) * 8, :] = tail
+        total = jnp.zeros((1, HD), F32)
+        for t in range(p * PAIR, (p + 1) * PAIR):
+            spot = lane == across + (t % PAIR) * seqs
+            picked = jnp.where(spot, sq_ref[rows_at(t, chunk, row_len), :], 0.0)
+            total += jnp.sum(picked, axis=0, keepdims=True)
+        tail = jnp.broadcast_to(total, (8, HD))
+        squares_ref[p * 8 : (p + 1) * 8, :] = tail
         out_ref[p * each + body : (p + 1) * each, :] = tail
+    copies[-1].wait()
 
 
 def add_kernel(a_ref, b_ref, out_ref):
@@ -424,7 +429,6 @@
     slots = CAP * wide_count
     parts = PAIR * heads
     message = parts * finished + 8
-    chunks = 1
     shape = jax.ShapeDtypeStruct
 
     rows = fin_rows.reshape(finished * row_len, features)
@@ -432,20 +436,20 @@
     squares_shape = shape((chips * 8, HD), F32)
     acc = pltpu.VMEM((heads * finished * row_len, HD), F32)
     theirs, squares, rows, weights = local_call(
-        functools.partial(project_kernel, False, row_len, chunks),
+        functools.partial(project_kernel, False, row_len),
         "project_theirs",
         (rows, reward_query),
         [partial, squares_shape, shape(rows.shape, BF16), shape(reward_query.shape, BF16)],
         [
             acc,
             pltpu.VMEM((finished * row_len, HD), F32),
-            pltpu.SemaphoreType.DMA((2 * WEIGHT_COPIES + 1,)),
+            pltpu.SemaphoreType.DMA((2 * FEATURE_COPIES + 1,)),
         ],
         fetched=2,
     )
     got = lax.ppermute(theirs, "tc", [(0, 1), (1, 0)])
     (kept,) = local_call(
-        functools.partial(project_kernel, True, row_len, chunks),
+        functools.partial(project_kernel, True, row_len),
         "project_kept",
         (squares, rows, weights),
         [partial],

time: 92 us -> 91.8 us (level)
  no operation moved by 1% of the time
where the time goes in v5:
time: 91.8 us; the launch traced here: 91.5 us
  blocking collectives  58 us (63%)
  starting transfers between devices  13.4 us (15%)
  waiting for transfers between devices  9.59 us (10%)
  Pallas kernels  8.3 us (9%)
  between operations  1.41 us (2%)
    all_to_all x1, blocking collectives, per_device(): lax.all_to_all(outgoing, 'wide', split_axis=0, concat_axis=0, tiled=True)  27.9 us
    all_to_all x1, blocking collectives, per_device(): lax.all_to_all(answers.reshape(wide_count, 1, answer * HD), 'wide', split...  16.8 us
    all_to_all x1, blocking collectives, per_device(): lax.all_to_all(merged.reshape(tp_count, 1, share * HD), ('th', 'tc'), spl...  13.3 us
    ppermute x1, starting transfers between devices, per_device(): got = lax.ppermute(theirs, 'tc', [(0, 1), (1, 0)])  8.79 us
    all_to_all x1, waiting for transfers between devices, per_device(): lax.all_to_all(both.reshape(chips, message, HD), 'th', split_axis=0, conc...  8.56 us
    pallas_call x8, Pallas kernels, local_call(): pl.pallas_call(kernel, in_specs=[vmem] * kept + [hbm] * fetched, out_spec...  8.3 us
    all_to_all x1, starting transfers between devices, per_device(): lax.all_to_all(both.reshape(chips, message, HD), 'th', split_axis=0, conc...  4.65 us
  transfers between devices with their start and end apart: 2, of which 2 were waited for; matrix products, arithmetic and copies ran while one was open for 1% of the time, Pallas kernels for 3%

profile of v5, /device:TPU:1, one launch (start us, length us, event | category | flops | bytes accessed | tf_op | source)
XLA Modules:
  0.0 91.5 jit_solution(12721882394552223130)
XLA Ops:
  0.6 1.9 %project_theirs.1 = (f32[1056,128]{1,0:T(8,128)S(1)}, f32[32,128]{1,0:T(8,128)S(1)}, bf16[512,1024]{1,0:T(8,128)(2,1)S(1)}, bf16[1024,512]{1,0:T(8,128)(2,1)S(1)}) custom-call(bf16[512,1024]{1,0:T(8,128)(2,1)} %bitcast.22, bf16[1024,512]{1,0:T(8,128)(2,1)} %refs_1_.1), custom_call_target="tpu_custom_call" | custom-call | tf_op jit(solution)/shard_map/project_theirs/pallas_call | solution.py:53
  2.5 8.8 %collective-permute-start = (f32[1056,128]{1,0:T(8,128)S(1)}, f32[1056,128]{1,0:T(8,128)S(1)}, u32[]{:S(2)}, u32[]{:S(2)}) collective-permute-start(f32[1056,128]{1,0:T(8,128)S(1)} %get-tuple-element.17), channel_id=1, source_target_pairs={{0,1},{1,0},{2,3},{3,2},{4,5},{5,4},{6,7},{7,6},{8,9},{9,8},{10,11... | collective-permute-start | bytes 1622024 | tf_op jit(solution)/shard_map/ppermute | solution.py:450
  11.3 0.0 copy-start.2
  11.4 0.0 copy-start.3
  11.4 0.5 project_kept.1.a_ref
  11.9 1.0 %collective-permute-done.b_ref = f32[1056,128]{1,0:T(8,128)S(1)} collective-permute-done((f32[1056,128]{1,0:T(8,128)S(1)}, f32[1056,128]{1,0:T(8,128)S(1)}, u32[]{:S(2)}, u32[]{:S(2)}) %collective-permute-start) | collective-permute-done | bytes 540704 | tf_op jit(solution)/shard_map/ppermute | solution.py:450
  12.9 0.9 add.15
  13.7 4.6 %all-to-all-start = ((f32[4,264,128]{2,1,0:T(8,128)}), f32[4,264,128]{2,1,0:T(8,128)S(1)}, u32[]{:S(2)}, u32[]{:S(2)}) async-start(f32[4,264,128]{2,1,0:T(8,128)} %bitcast.1), calls=%async_computation | async-start | bytes 1081344 | tf_op jit(solution)/shard_map/all_to_all | solution.py:459
  18.4 0.0 copy-start
  19.1 0.1 pad.11.clone
  19.2 0.0 copy-done.2
  19.2 0.0 copy-done.3
  19.2 0.6 fusion.1.route_hbm
  19.8 2.2 %decode.1 = (f32[8,128]{1,0:T(8,128)S(1)}, f32[128,128]{1,0:T(8,128)S(1)}, bf16[128,128]{1,0:T(8,128)(2,1)S(1)}, f32[24,128]{1,0:T(8,128)S(1)}, bf16[128,128]{1,0:T(8,128)(2,1)S(1)}, /*index=5*/f32[8,128]{1,0:T(8,128)S(1)}) custom-call(s32[4]{0:T(128)} %lens_hbm.1, bf16[4,256]{1,0:T(4,128)(2,1)} %q_hbm.1, bf16[4,128]{1,0:T(4,128)(2,1)} %nk_hbm.1, ...), custom_call_target="tpu_custom_call" | custom-call | tf_op jit(solution)/shard_map/decode/pallas_call | solution.py:53
  22.1 8.6 %all-to-all-done = f32[4,264,128]{2,1,0:T(8,128)S(1)} async-done(((f32[4,264,128]{2,1,0:T(8,128)}), f32[4,264,128]{2,1,0:T(8,128)S(1)}, u32[]{:S(2)}, u32[]{:S(2)}) %all-to-all-start) | async-done | bytes 540704 | tf_op jit(solution)/shard_map/all_to_all | solution.py:459
  30.6 0.4 place.1
  31.0 27.9 %all_to_all.20.x_ref = bf16[64,24,128]{2,1,0:T(8,128)(2,1)S(1)} all-to-all(bf16[64,24,128]{2,1,0:T(8,128)(2,1)S(1)} %place.1), channel_id=1, replica_groups=mesh['wide'=64,'th'=4,'tc'=2] {'wide'}, dimensions={0} | all-to-all | bytes 786432 | tf_op jit(solution)/shard_map/all_to_all | solution.py:500
  58.9 0.0 copy-done
  58.9 0.0 copy-done.1
  58.9 1.6 %score.1 = f32[320,128]{1,0:T(8,128)S(1)} custom-call(bf16[64,24,128]{2,1,0:T(8,128)(2,1)S(1)} %all_to_all.20.x_ref, bf16[1024,128]{1,0:T(8,128)(2,1)S(1)} %bitcast.20, bf16[1024,128]{1,0:T(8,128)(2,1)S(1)} %bitcast.21, f32[24,128]{1,0:T(8,128)S(1)} %get-tuple-element.20.weight_ref, bf16[128,128]{1,0:T(8,128)(2,1)S(1)} %get-tuple-element.21.delta_ref), custom_call_target="tpu_custom_call" | custom-call | tf_op jit(solution)/shard_map/score/pallas_call | solution.py:53
  60.5 16.8 %all_to_all.21 = f32[64,1,640]{2,1,0:T(1,128)S(1)} all-to-all(f32[64,1,640]{2,1,0:T(1,128)S(1)} %bitcast.16), channel_id=1, replica_groups=mesh['wide'=64,'th'=4,'tc'=2] {'wide'}, dimensions={0} | all-to-all | bytes 327680 | tf_op jit(solution)/shard_map/all_to_all | solution.py:516
  77.3 0.2 merge.1
  77.6 13.3 %all_to_all.22 = f32[8,1,2304]{2,1,0:T(1,128)S(1)} all-to-all(f32[8,1,2304]{2,1,0:T(1,128)S(1)} %bitcast.19), channel_id=1, replica_groups=mesh['wide'=64,'th'=4,'tc'=2] {'th','tc'}, dimensions={0} | all-to-all | bytes 147456 | tf_op jit(solution)/shard_map/all_to_all | solution.py:527
  90.9 0.6 final.1
  (1 shorter events, 0.0 us)
Async XLA Ops:
  2.5 10.3 %collective-permute-start = (f32[1056,128]{1,0:T(8,128)S(1)}, f32[1056,128]{1,0:T(8,128)S(1)}, u32[]{:S(2)}, u32[]{:S(2)}) collective-permute-start(f32[1056,128]{1,0:T(8,128)S(1)} %get-tuple-element.17), channel_id=1, source_target_pairs={{0,1},{1,0},{2,3},{3,2},{4,5},{5,4},{6,7},{7,6},{8,9},{9,8},{10,11... | collective-permute-start | bytes 1622024 | tf_op jit(solution)/shard_map/ppermute | solution.py:450
  11.3 7.8 %copy-start.2 = (s32[64]{0:T(128)S(1)}, s32[64]{0:T(128)}, u32[]{:S(2)}) copy-start(s32[64]{0:T(128)} %param.26) | copy-start | bytes 772
  11.4 7.8 %copy-start.3 = (s32[64,1]{0,1:T(1,128)S(1)}, s32[64,1]{0,1:T(1,128)}, u32[]{:S(2)}) copy-start(s32[64,1]{0,1:T(1,128)} %param.25) | copy-start | bytes 772
  13.7 16.9 %all-to-all-start = ((f32[4,264,128]{2,1,0:T(8,128)}), f32[4,264,128]{2,1,0:T(8,128)S(1)}, u32[]{:S(2)}, u32[]{:S(2)}) async-start(f32[4,264,128]{2,1,0:T(8,128)} %bitcast.1), calls=%async_computation | async-start | bytes 1081344 | tf_op jit(solution)/shard_map/all_to_all | solution.py:459
  18.4 40.5 %copy-start = (bf16[1,1024,128]{2,1,0:T(8,128)(2,1)S(1)}, bf16[1,1024,128]{2,1,0:T(8,128)(2,1)}, u32[]{:S(2)}) copy-start(bf16[1,1024,128]{2,1,0:T(8,128)(2,1)} %param.29) | copy-start | bytes 786436
  18.4 40.5 %copy-start.1 = (bf16[1,1024,128]{2,1,0:T(8,128)(2,1)S(1)}, bf16[1,1024,128]{2,1,0:T(8,128)(2,1)}, u32[]{:S(2)}) copy-start(bf16[1,1024,128]{2,1,0:T(8,128)(2,1)} %param.30) | copy-start | bytes 786436

commit v6 on v5

--- a/solution.py
+++ b/solution.py
@@ -233,7 +233,8 @@
     groups = slots // CAP
     down = lax.broadcasted_iota(jnp.int32, (HD, HD), 0)
     across = lax.broadcasted_iota(jnp.int32, (HD, HD), 1)
-    route = route_ref[0:1, :]
+    routing = route_ref[...]
+    route = routing[0:1]
     target = jnp.broadcast_to(route, (HD, HD))
     target_down = jnp.sum(jnp.where(down == across, target, 0.0), axis=1, keepdims=True)
     earlier = jnp.where(jnp.logical_and(target == target_down, down < across), 1.0, 0.0)
@@ -249,19 +250,19 @@
     for h in range(heads):
         own = slice(h * rows // heads, (h + 1) * rows // heads)
         tile_ref[own, :] = jnp.broadcast_to(weight[h : h + 1], (rows // heads, HD))
-    block = jnp.broadcast_to(route_ref[2:3, :], (8, HD))
+    block = jnp.broadcast_to(routing[2:3], (8, HD))
     row_block = jnp.floor(block / blocks)
     tile_ref[rows : rows + 8, :] = row_block
     tile_ref[rows + 8 : rows + 16, :] = block - row_block * blocks
-    length_ref[...] = jnp.broadcast_to(route_ref[1:2, :], length_ref.shape)
+    length_ref[...] = jnp.broadcast_to(routing[1:2], length_ref.shape)
 
 
 def place_kernel(sources, x_ref, attn_ref, place_ref, out_ref, lay_ref):
     each = x_ref.shape[0] // sources
     body = each - 8
     groups = place_ref.shape[0] // CAP
-    tile = out_ref.shape[1] - attn_ref.shape[0]
-    lay = tile // 2
+    lay = out_ref.shape[1]
+    tile = 2 * lay
     parts = lay // CAP
     heads = parts // PAIR
     seqs = body // parts
@@ -289,16 +290,19 @@
                 lay_ref[rows_at(row, groups, tile), :] = placed[
                     r * groups : (r + 1) * groups, q * HD : (q + 1) * HD
                 ]
-    attn = jnp.broadcast_to(attn_ref[...].astype(BF16)[None], (groups,) + attn_ref.shape)
-    out_ref[:, :tile, :] = lay_ref[...].reshape(groups, tile, HD).astype(BF16)
-    out_ref[:, tile:, :] = attn
+    attn = attn_ref[...].astype(BF16)
+    for g in range(groups):
+        for k in range(2):
+            own = slice(g * tile + k * lay, g * tile + (k + 1) * lay)
+            out_ref[3 * g + k] = lay_ref[own, :].astype(BF16)
+        out_ref[3 * g + 2] = attn
 
 
 def score_kernel(
     seqs, x_ref, keys_ref, values_ref, weight_ref, delta_ref, out_ref, lay_ref
 ):
     tile = 2 * seqs
-    senders = x_ref.shape[0]
+    senders = x_ref.shape[0] // 3
     keys = keys_ref[...]
     keys2 = jnp.concatenate([keys, keys], axis=1)
     values = values_ref[...]
@@ -309,11 +313,9 @@
     at_once = min(AT_ONCE, senders)
     row = lax.broadcasted_iota(jnp.int32, (1, tile, HD), 1)
     for first in range(0, senders, at_once):
-        x = x_ref[first : first + at_once].astype(F32)
-        flat = [
-            x[:, k * tile : (k + 1) * tile, :].reshape(at_once * tile, HD).astype(BF16)
-            for k in range(3)
-        ]
+        x = x_ref[3 * first : 3 * (first + at_once)].astype(F32)
+        x = x.reshape(at_once, 3, tile, HD)
+        flat = [x[:, k].reshape(at_once * tile, HD).astype(BF16) for k in range(3)]
         scores = mm_t(jnp.concatenate(flat[:2], axis=1), keys2)
         highest = jnp.max(scores, axis=1, keepdims=True)
         weights = jnp.exp2(scores - highest)
@@ -341,7 +343,7 @@
 def merge_kernel(seqs, shards, x_ref, partial_ref, place_ref, out_ref):
     each = seqs + 1
     senders = x_ref.shape[0] // each
-    blocks = partial_ref.shape[0] // seqs
+    blocks = partial_ref.shape[0] // seqs - 8
     own_blocks = blocks // shards
     message = out_ref.shape[0] // shards
     last = x_ref[rows_at(seqs, senders, each), :]
@@ -383,20 +385,19 @@
     each = x_ref.shape[0] // shards
     seqs = decoded_ref.shape[0]
     body = each - PAIR
-    parts = [x_ref[k * each : (k + 1) * each, :] for k in range(shards)]
-    total = parts[0]
-    for part in parts[1:]:
-        total = total + part
+    rows = [x_ref[rows_at(q, shards, each), :] for q in range(each)]
+    sums = [jnp.sum(row, axis=0, keepdims=True) for row in rows[:body]]
     for c in range(body // seqs):
-        decoded_ref[:, c * HD : (c + 1) * HD] = total[c * seqs : (c + 1) * seqs, :].astype(BF16)
+        block = jnp.concatenate(sums[c * seqs : (c + 1) * seqs], axis=0)
+        decoded_ref[:, c * HD : (c + 1) * HD] = block.astype(BF16)
     length = length_ref[0:1, :]
     count = rewards_ref.shape[1]
+    shard = lax.broadcasted_iota(jnp.int32, (shards, HD), 0)
     reward = jnp.zeros((1, HD), F32)
-    for k in range(shards):
-        for p in range(PAIR):
-            token = k // CORES * PAIR + p
-            row = parts[k][body + p : body + p + 1, :]
-            reward = reward + jnp.where(length > token, row, 0.0)
+    for p in range(PAIR):
+        token = (shard // CORES * PAIR + p).astype(F32)
+        scored = jnp.where(length > token, rows[body + p], 0.0)
+        reward = reward + jnp.sum(scored, axis=0, keepdims=True)
     rewards_ref[...] = (reward / length)[:, :count]
 
 
@@ -477,7 +478,7 @@
         small + large,
         [
             shape((tile, HD), F32),
-            shape((blocks * seq_count, HD), F32),
+            shape(((blocks + 8) * seq_count, HD), F32),
             shape((slots, HD), BF16),
             shape((tile + 16, HD), F32),
             shape(delta_values.shape[1:], BF16),
@@ -494,7 +495,7 @@
         functools.partial(place_kernel, chips),
         "place",
         (summed_tokens, attn, place),
-        [shape((wide_count, 2 * lay + tile, HD), BF16)],
+        [shape((wide_count * 3, lay, HD), BF16)],
         [pltpu.VMEM((wide_count * 2 * lay, HD), F32)],
     )
     received = lax.all_to_all(outgoing, "wide", split_axis=0, concat_axis=0, tiled=True)

time: 91.8 us -> 91.8 us (level)
  no operation moved by 1% of the time
where the time goes in v6:
time: 91.8 us; the launch traced here: 91.5 us
  blocking collectives  58 us (63%)
  starting transfers between devices  13.4 us (15%)
  waiting for transfers between devices  9.59 us (10%)
  Pallas kernels  8.3 us (9%)
  between operations  1.41 us (2%)
    all_to_all x1, blocking collectives, per_device(): lax.all_to_all(outgoing, 'wide', split_axis=0, concat_axis=0, tiled=True)  27.9 us
    all_to_all x1, blocking collectives, per_device(): lax.all_to_all(answers.reshape(wide_count, 1, answer * HD), 'wide', split...  16.9 us
    all_to_all x1, blocking collectives, per_device(): lax.all_to_all(merged.reshape(tp_count, 1, share * HD), ('th', 'tc'), spl...  13.3 us
    ppermute x1, starting transfers between devices, per_device(): got = lax.ppermute(theirs, 'tc', [(0, 1), (1, 0)])  8.79 us
    all_to_all x1, waiting for transfers between devices, per_device(): lax.all_to_all(both.reshape(chips, message, HD), 'th', split_axis=0, conc...  8.56 us
    pallas_call x8, Pallas kernels, local_call(): pl.pallas_call(kernel, in_specs=[vmem] * kept + [hbm] * fetched, out_spec...  8.3 us
    all_to_all x1, starting transfers between devices, per_device(): lax.all_to_all(both.reshape(chips, message, HD), 'th', split_axis=0, conc...  4.65 us
  transfers between devices with their start and end apart: 2, of which 2 were waited for; matrix products, arithmetic and copies ran while one was open for 1% of the time, Pallas kernels for 3%

profile of v6, /device:TPU:1, one launch (start us, length us, event | category | flops | bytes accessed | tf_op | source)
XLA Modules:
  0.0 91.5 jit_solution(8727106503988682247)
XLA Ops:
  0.6 1.9 %project_theirs.1 = (f32[1056,128]{1,0:T(8,128)S(1)}, f32[32,128]{1,0:T(8,128)S(1)}, bf16[512,1024]{1,0:T(8,128)(2,1)S(1)}, bf16[1024,512]{1,0:T(8,128)(2,1)S(1)}) custom-call(bf16[512,1024]{1,0:T(8,128)(2,1)} %bitcast.22, bf16[1024,512]{1,0:T(8,128)(2,1)} %refs_1_.1), custom_call_target="tpu_custom_call" | custom-call | tf_op jit(solution)/shard_map/project_theirs/pallas_call | solution.py:53
  2.5 8.8 %collective-permute-start = (f32[1056,128]{1,0:T(8,128)S(1)}, f32[1056,128]{1,0:T(8,128)S(1)}, u32[]{:S(2)}, u32[]{:S(2)}) collective-permute-start(f32[1056,128]{1,0:T(8,128)S(1)} %get-tuple-element.17), channel_id=1, source_target_pairs={{0,1},{1,0},{2,3},{3,2},{4,5},{5,4},{6,7},{7,6},{8,9},{9,8},{10,11... | collective-permute-start | bytes 1622024 | tf_op jit(solution)/shard_map/ppermute | solution.py:451
  11.3 0.0 copy-start.2
  11.4 0.0 copy-start.3
  11.4 0.5 project_kept.1.a_ref
  11.9 1.0 %collective-permute-done.b_ref = f32[1056,128]{1,0:T(8,128)S(1)} collective-permute-done((f32[1056,128]{1,0:T(8,128)S(1)}, f32[1056,128]{1,0:T(8,128)S(1)}, u32[]{:S(2)}, u32[]{:S(2)}) %collective-permute-start) | collective-permute-done | bytes 540704 | tf_op jit(solution)/shard_map/ppermute | solution.py:451
  12.9 0.9 add.15
  13.7 4.6 %all-to-all-start = ((f32[4,264,128]{2,1,0:T(8,128)}), f32[4,264,128]{2,1,0:T(8,128)S(1)}, u32[]{:S(2)}, u32[]{:S(2)}) async-start(f32[4,264,128]{2,1,0:T(8,128)} %bitcast.1), calls=%async_computation | async-start | bytes 1081344 | tf_op jit(solution)/shard_map/all_to_all | solution.py:460
  18.4 0.0 copy-start
  19.1 0.1 pad.11.clone
  19.2 0.0 copy-done.2
  19.2 0.0 copy-done.3
  19.2 0.6 fusion.1.route_hbm
  19.8 2.2 %decode.1 = (f32[8,128]{1,0:T(8,128)S(1)}, f32[160,128]{1,0:T(8,128)S(1)}, bf16[128,128]{1,0:T(8,128)(2,1)S(1)}, f32[24,128]{1,0:T(8,128)S(1)}, bf16[128,128]{1,0:T(8,128)(2,1)S(1)}, /*index=5*/f32[8,128]{1,0:T(8,128)S(1)}) custom-call(s32[4]{0:T(128)} %lens_hbm.1, bf16[4,256]{1,0:T(4,128)(2,1)} %q_hbm.1, bf16[4,128]{1,0:T(4,128)(2,1)} %nk_hbm.1, ...), custom_call_target="tpu_custom_call" | custom-call | tf_op jit(solution)/shard_map/decode/pallas_call | solution.py:53
  22.1 8.6 %all-to-all-done = f32[4,264,128]{2,1,0:T(8,128)S(1)} async-done(((f32[4,264,128]{2,1,0:T(8,128)}), f32[4,264,128]{2,1,0:T(8,128)S(1)}, u32[]{:S(2)}, u32[]{:S(2)}) %all-to-all-start) | async-done | bytes 540704 | tf_op jit(solution)/shard_map/all_to_all | solution.py:460
  30.6 0.4 place.1
  31.0 27.9 %all_to_all.20.x_ref = bf16[192,8,128]{2,1,0:T(8,128)(2,1)S(1)} all-to-all(bf16[192,8,128]{2,1,0:T(8,128)(2,1)S(1)} %place.1), channel_id=1, replica_groups=mesh['wide'=64,'th'=4,'tc'=2] {'wide'}, dimensions={0} | all-to-all | bytes 786432 | tf_op jit(solution)/shard_map/all_to_all | solution.py:501
  58.9 0.0 copy-done
  58.9 0.0 copy-done.1
  58.9 1.6 %score.1 = f32[320,128]{1,0:T(8,128)S(1)} custom-call(bf16[192,8,128]{2,1,0:T(8,128)(2,1)S(1)} %all_to_all.20.x_ref, bf16[1024,128]{1,0:T(8,128)(2,1)S(1)} %bitcast.20, bf16[1024,128]{1,0:T(8,128)(2,1)S(1)} %bitcast.21, f32[24,128]{1,0:T(8,128)S(1)} %get-tuple-element.20.weight_ref, bf16[128,128]{1,0:T(8,128)(2,1)S(1)} %get-tuple-element.21.delta_ref), custom_call_target="tpu_custom_call" | custom-call | tf_op jit(solution)/shard_map/score/pallas_call | solution.py:53
  60.5 16.9 %all_to_all.21 = f32[64,1,640]{2,1,0:T(1,128)S(1)} all-to-all(f32[64,1,640]{2,1,0:T(1,128)S(1)} %bitcast.16), channel_id=1, replica_groups=mesh['wide'=64,'th'=4,'tc'=2] {'wide'}, dimensions={0} | all-to-all | bytes 327680 | tf_op jit(solution)/shard_map/all_to_all | solution.py:517
  77.3 0.2 merge.1
  77.6 13.3 %all_to_all.22 = f32[8,1,2304]{2,1,0:T(1,128)S(1)} all-to-all(f32[8,1,2304]{2,1,0:T(1,128)S(1)} %bitcast.19), channel_id=1, replica_groups=mesh['wide'=64,'th'=4,'tc'=2] {'th','tc'}, dimensions={0} | all-to-all | bytes 147456 | tf_op jit(solution)/shard_map/all_to_all | solution.py:528
  90.9 0.6 final.1
  (1 shorter events, 0.0 us)
Async XLA Ops:
  2.5 10.3 %collective-permute-start = (f32[1056,128]{1,0:T(8,128)S(1)}, f32[1056,128]{1,0:T(8,128)S(1)}, u32[]{:S(2)}, u32[]{:S(2)}) collective-permute-start(f32[1056,128]{1,0:T(8,128)S(1)} %get-tuple-element.17), channel_id=1, source_target_pairs={{0,1},{1,0},{2,3},{3,2},{4,5},{5,4},{6,7},{7,6},{8,9},{9,8},{10,11... | collective-permute-start | bytes 1622024 | tf_op jit(solution)/shard_map/ppermute | solution.py:451
  11.3 7.8 %copy-start.2 = (s32[64]{0:T(128)S(1)}, s32[64]{0:T(128)}, u32[]{:S(2)}) copy-start(s32[64]{0:T(128)} %param.26) | copy-start | bytes 772
  11.4 7.8 %copy-start.3 = (s32[64,1]{0,1:T(1,128)S(1)}, s32[64,1]{0,1:T(1,128)}, u32[]{:S(2)}) copy-start(s32[64,1]{0,1:T(1,128)} %param.25) | copy-start | bytes 772
  13.7 16.9 %all-to-all-start = ((f32[4,264,128]{2,1,0:T(8,128)}), f32[4,264,128]{2,1,0:T(8,128)S(1)}, u32[]{:S(2)}, u32[]{:S(2)}) async-start(f32[4,264,128]{2,1,0:T(8,128)} %bitcast.1), calls=%async_computation | async-start | bytes 1081344 | tf_op jit(solution)/shard_map/all_to_all | solution.py:460
  18.4 40.5 %copy-start = (bf16[1,1024,128]{2,1,0:T(8,128)(2,1)S(1)}, bf16[1,1024,128]{2,1,0:T(8,128)(2,1)}, u32[]{:S(2)}) copy-start(bf16[1,1024,128]{2,1,0:T(8,128)(2,1)} %param.29) | copy-start | bytes 786436
  18.4 40.5 %copy-start.1 = (bf16[1,1024,128]{2,1,0:T(8,128)(2,1)S(1)}, bf16[1,1024,128]{2,1,0:T(8,128)(2,1)}, u32[]{:S(2)}) copy-start(bf16[1,1024,128]{2,1,0:T(8,128)(2,1)} %param.30) | copy-start | bytes 786436

commit v7 on v6

--- a/solution.py
+++ b/solution.py
@@ -312,11 +312,14 @@
     delta = delta_ref[...]
     at_once = min(AT_ONCE, senders)
     row = lax.broadcasted_iota(jnp.int32, (1, tile, HD), 1)
+    started = []
     for first in range(0, senders, at_once):
         x = x_ref[3 * first : 3 * (first + at_once)].astype(F32)
         x = x.reshape(at_once, 3, tile, HD)
         flat = [x[:, k].reshape(at_once * tile, HD).astype(BF16) for k in range(3)]
         scores = mm_t(jnp.concatenate(flat[:2], axis=1), keys2)
+        started.append((first, scores, mm(flat[2], delta)))
+    for first, scores, product in started:
         highest = jnp.max(scores, axis=1, keepdims=True)
         weights = jnp.exp2(scores - highest)
         probs = (weights * (1.0 / jnp.sum(weights, axis=1, keepdims=True))).astype(BF16)
@@ -325,7 +328,7 @@
         terms = gated.reshape(at_once, tile, HD) * weight
         by_head = jnp.broadcast_to(jnp.sum(terms, axis=2, keepdims=True), terms.shape)
         score = by_head + jnp.concatenate([by_head[:, seqs:], by_head[:, :seqs]], axis=1)
-        product = mm(flat[2], delta).reshape(at_once, tile, HD)
+        product = product.reshape(at_once, tile, HD)
         turned = jnp.concatenate([product[:, seqs:], product[:, :seqs]], axis=1)
         result = jnp.where(row_block == 0.0, product, turned)
         result = jnp.where(row < seqs, result, score)

time: 91.8 us -> 91.5 us (level)
  no operation moved by 1% of the time
where the time goes in v7:
time: 91.5 us; the launch traced here: 91.1 us
  blocking collectives  58 us (63%)
  starting transfers between devices  13.4 us (15%)
  waiting for transfers between devices  9.59 us (10%)
  Pallas kernels  7.95 us (9%)
  between operations  1.41 us (2%)
    all_to_all x1, blocking collectives, per_device(): lax.all_to_all(outgoing, 'wide', split_axis=0, concat_axis=0, tiled=True)  27.9 us
    all_to_all x1, blocking collectives, per_device(): lax.all_to_all(answers.reshape(wide_count, 1, answer * HD), 'wide', split...  16.9 us
    all_to_all x1, blocking collectives, per_device(): lax.all_to_all(merged.reshape(tp_count, 1, share * HD), ('th', 'tc'), spl...  13.3 us
    ppermute x1, starting transfers between devices, per_device(): got = lax.ppermute(theirs, 'tc', [(0, 1), (1, 0)])  8.79 us
    all_to_all x1, waiting for transfers between devices, per_device(): lax.all_to_all(both.reshape(chips, message, HD), 'th', split_axis=0, conc...  8.56 us
    pallas_call x8, Pallas kernels, local_call(): pl.pallas_call(kernel, in_specs=[vmem] * kept + [hbm] * fetched, out_spec...  7.95 us
    all_to_all x1, starting transfers between devices, per_device(): lax.all_to_all(both.reshape(chips, message, HD), 'th', split_axis=0, conc...  4.65 us
  transfers between devices with their start and end apart: 2, of which 2 were waited for; matrix products, arithmetic and copies ran while one was open for 1% of the time, Pallas kernels for 3%

profile of v7, /device:TPU:1, one launch (start us, length us, event | category | flops | bytes accessed | tf_op | source)
XLA Modules:
  0.0 91.1 jit_solution(6604782845509254713)
XLA Ops:
  0.6 1.9 %project_theirs.1 = (f32[1056,128]{1,0:T(8,128)S(1)}, f32[32,128]{1,0:T(8,128)S(1)}, bf16[512,1024]{1,0:T(8,128)(2,1)S(1)}, bf16[1024,512]{1,0:T(8,128)(2,1)S(1)}) custom-call(bf16[512,1024]{1,0:T(8,128)(2,1)} %bitcast.22, bf16[1024,512]{1,0:T(8,128)(2,1)} %refs_1_.1), custom_call_target="tpu_custom_call" | custom-call | tf_op jit(solution)/shard_map/project_theirs/pallas_call | solution.py:53
  2.5 8.8 %collective-permute-start = (f32[1056,128]{1,0:T(8,128)S(1)}, f32[1056,128]{1,0:T(8,128)S(1)}, u32[]{:S(2)}, u32[]{:S(2)}) collective-permute-start(f32[1056,128]{1,0:T(8,128)S(1)} %get-tuple-element.17), channel_id=1, source_target_pairs={{0,1},{1,0},{2,3},{3,2},{4,5},{5,4},{6,7},{7,6},{8,9},{9,8},{10,11... | collective-permute-start | bytes 1622024 | tf_op jit(solution)/shard_map/ppermute | solution.py:454
  11.3 0.0 copy-start.2
  11.4 0.0 copy-start.3
  11.4 0.5 project_kept.1.a_ref
  11.9 1.0 %collective-permute-done.b_ref = f32[1056,128]{1,0:T(8,128)S(1)} collective-permute-done((f32[1056,128]{1,0:T(8,128)S(1)}, f32[1056,128]{1,0:T(8,128)S(1)}, u32[]{:S(2)}, u32[]{:S(2)}) %collective-permute-start) | collective-permute-done | bytes 540704 | tf_op jit(solution)/shard_map/ppermute | solution.py:454
  12.9 0.9 add.15
  13.7 4.6 %all-to-all-start = ((f32[4,264,128]{2,1,0:T(8,128)}), f32[4,264,128]{2,1,0:T(8,128)S(1)}, u32[]{:S(2)}, u32[]{:S(2)}) async-start(f32[4,264,128]{2,1,0:T(8,128)} %bitcast.1), calls=%async_computation | async-start | bytes 1081344 | tf_op jit(solution)/shard_map/all_to_all | solution.py:463
  18.4 0.0 copy-start
  19.1 0.1 pad.11.clone
  19.2 0.0 copy-done.2
  19.2 0.0 copy-done.3
  19.2 0.6 fusion.1.route_hbm
  19.8 2.2 %decode.1 = (f32[8,128]{1,0:T(8,128)S(1)}, f32[160,128]{1,0:T(8,128)S(1)}, bf16[128,128]{1,0:T(8,128)(2,1)S(1)}, f32[24,128]{1,0:T(8,128)S(1)}, bf16[128,128]{1,0:T(8,128)(2,1)S(1)}, /*index=5*/f32[8,128]{1,0:T(8,128)S(1)}) custom-call(s32[4]{0:T(128)} %lens_hbm.1, bf16[4,256]{1,0:T(4,128)(2,1)} %q_hbm.1, bf16[4,128]{1,0:T(4,128)(2,1)} %nk_hbm.1, ...), custom_call_target="tpu_custom_call" | custom-call | tf_op jit(solution)/shard_map/decode/pallas_call | solution.py:53
  22.1 8.6 %all-to-all-done = f32[4,264,128]{2,1,0:T(8,128)S(1)} async-done(((f32[4,264,128]{2,1,0:T(8,128)}), f32[4,264,128]{2,1,0:T(8,128)S(1)}, u32[]{:S(2)}, u32[]{:S(2)}) %all-to-all-start) | async-done | bytes 540704 | tf_op jit(solution)/shard_map/all_to_all | solution.py:463
  30.6 0.4 place.1
  31.0 27.9 %all_to_all.20.x_ref = bf16[192,8,128]{2,1,0:T(8,128)(2,1)S(1)} all-to-all(bf16[192,8,128]{2,1,0:T(8,128)(2,1)S(1)} %place.1), channel_id=1, replica_groups=mesh['wide'=64,'th'=4,'tc'=2] {'wide'}, dimensions={0} | all-to-all | bytes 786432 | tf_op jit(solution)/shard_map/all_to_all | solution.py:504
  58.9 0.0 copy-done
  58.9 0.0 copy-done.1
  58.9 1.2 %score.1 = f32[320,128]{1,0:T(8,128)S(1)} custom-call(bf16[192,8,128]{2,1,0:T(8,128)(2,1)S(1)} %all_to_all.20.x_ref, bf16[1024,128]{1,0:T(8,128)(2,1)S(1)} %bitcast.20, bf16[1024,128]{1,0:T(8,128)(2,1)S(1)} %bitcast.21, f32[24,128]{1,0:T(8,128)S(1)} %get-tuple-element.20.weight_ref, bf16[128,128]{1,0:T(8,128)(2,1)S(1)} %get-tuple-element.21.delta_ref), custom_call_target="tpu_custom_call" | custom-call | tf_op jit(solution)/shard_map/score/pallas_call | solution.py:53
  60.1 16.9 %all_to_all.21 = f32[64,1,640]{2,1,0:T(1,128)S(1)} all-to-all(f32[64,1,640]{2,1,0:T(1,128)S(1)} %bitcast.16), channel_id=1, replica_groups=mesh['wide'=64,'th'=4,'tc'=2] {'wide'}, dimensions={0} | all-to-all | bytes 327680 | tf_op jit(solution)/shard_map/all_to_all | solution.py:520
  77.0 0.2 merge.1
  77.2 13.3 %all_to_all.22 = f32[8,1,2304]{2,1,0:T(1,128)S(1)} all-to-all(f32[8,1,2304]{2,1,0:T(1,128)S(1)} %bitcast.19), channel_id=1, replica_groups=mesh['wide'=64,'th'=4,'tc'=2] {'th','tc'}, dimensions={0} | all-to-all | bytes 147456 | tf_op jit(solution)/shard_map/all_to_all | solution.py:531
  90.5 0.6 final.1
  (1 shorter events, 0.0 us)
Async XLA Ops:
  2.5 10.3 %collective-permute-start = (f32[1056,128]{1,0:T(8,128)S(1)}, f32[1056,128]{1,0:T(8,128)S(1)}, u32[]{:S(2)}, u32[]{:S(2)}) collective-permute-start(f32[1056,128]{1,0:T(8,128)S(1)} %get-tuple-element.17), channel_id=1, source_target_pairs={{0,1},{1,0},{2,3},{3,2},{4,5},{5,4},{6,7},{7,6},{8,9},{9,8},{10,11... | collective-permute-start | bytes 1622024 | tf_op jit(solution)/shard_map/ppermute | solution.py:454
  11.3 7.8 %copy-start.2 = (s32[64]{0:T(128)S(1)}, s32[64]{0:T(128)}, u32[]{:S(2)}) copy-start(s32[64]{0:T(128)} %param.26) | copy-start | bytes 772
  11.4 7.8 %copy-start.3 = (s32[64,1]{0,1:T(1,128)S(1)}, s32[64,1]{0,1:T(1,128)}, u32[]{:S(2)}) copy-start(s32[64,1]{0,1:T(1,128)} %param.25) | copy-start | bytes 772
  13.7 16.9 %all-to-all-start = ((f32[4,264,128]{2,1,0:T(8,128)}), f32[4,264,128]{2,1,0:T(8,128)S(1)}, u32[]{:S(2)}, u32[]{:S(2)}) async-start(f32[4,264,128]{2,1,0:T(8,128)} %bitcast.1), calls=%async_computation | async-start | bytes 1081344 | tf_op jit(solution)/shard_map/all_to_all | solution.py:463
  18.4 40.5 %copy-start = (bf16[1,1024,128]{2,1,0:T(8,128)(2,1)S(1)}, bf16[1,1024,128]{2,1,0:T(8,128)(2,1)}, u32[]{:S(2)}) copy-start(bf16[1,1024,128]{2,1,0:T(8,128)(2,1)} %param.29) | copy-start | bytes 786436
  18.4 40.5 %copy-start.1 = (bf16[1,1024,128]{2,1,0:T(8,128)(2,1)S(1)}, bf16[1,1024,128]{2,1,0:T(8,128)(2,1)}, u32[]{:S(2)}) copy-start(bf16[1,1024,128]{2,1,0:T(8,128)(2,1)} %param.30) | copy-start | bytes 786436

commit v8 on v7

--- a/solution.py
+++ b/solution.py
@@ -13,6 +13,7 @@
 CAP = 2
 CORES = 2
 PAIR = 2
+AXES = ("wide", "th", "tc")
 VMEM_LIMIT = 16 * 2**20
 WEIGHT_COPIES = 4
 FEATURE_COPIES = 2
@@ -139,6 +140,18 @@
     out_ref[...] = a_ref[...] + b_ref[...]
 
 
+def exchange_both_ways(x):
+    wide_count, chips, cores = (lax.axis_size(name) for name in AXES)
+    groups = []
+    for core in range(cores):
+        for chip in range(chips):
+            group = [(w * chips + chip) * cores + core for w in range(wide_count)]
+            groups.append(group if core == 0 else group[::-1])
+    return lax.all_to_all(
+        x, AXES, split_axis=0, concat_axis=0, axis_index_groups=groups, tiled=True
+    )
+
+
 def decode_kernel(
     lens_hbm,
     q_hbm,
@@ -153,6 +166,7 @@
     attn_ref,
     out_ref,
     place_ref,
+    sent_ref,
     tile_ref,
     delta_ref,
     length_ref,
@@ -244,6 +258,9 @@
     order = (slot // groups).astype(F32)
     held = jnp.logical_and(route == group, rank == order)
     place_ref[...] = jnp.where(held, 1.0, 0.0).astype(BF16)
+    sent = jnp.where(lax.axis_index("tc") == 0, group, groups - 1 - group)
+    held = jnp.logical_and(route == sent, rank == order)
+    sent_ref[...] = jnp.where(held, 1.0, 0.0).astype(BF16)
     weight = score_ref[...].astype(F32)
     heads = weight.shape[0] // CORES
     weight = jnp.where(lax.axis_index("tc") == 0, weight[:heads], weight[heads:])
@@ -299,7 +316,7 @@
 
 
 def score_kernel(
-    seqs, x_ref, keys_ref, values_ref, weight_ref, delta_ref, out_ref, lay_ref
+    seqs, x_ref, keys_ref, values_ref, weight_ref, delta_ref, out_ref, lay_ref, in_order_ref
 ):
     tile = 2 * seqs
     senders = x_ref.shape[0] // 3
@@ -312,9 +329,14 @@
     delta = delta_ref[...]
     at_once = min(AT_ONCE, senders)
     row = lax.broadcasted_iota(jnp.int32, (1, tile, HD), 1)
+    core = lax.axis_index("tc")
+    for w in range(senders):
+        came = jnp.where(core == 0, w, senders - 1 - w)
+        for k in range(3):
+            in_order_ref[3 * w + k] = x_ref[3 * came + k]
     started = []
     for first in range(0, senders, at_once):
-        x = x_ref[3 * first : 3 * (first + at_once)].astype(F32)
+        x = in_order_ref[3 * first : 3 * (first + at_once)].astype(F32)
         x = x.reshape(at_once, 3, tile, HD)
         flat = [x[:, k].reshape(at_once * tile, HD).astype(BF16) for k in range(3)]
         scores = mm_t(jnp.concatenate(flat[:2], axis=1), keys2)
@@ -475,13 +497,14 @@
     weights = score_weight.reshape(heads * CORES, HD)
     small = (cache_lengths, query, new_key, new_value, routing, weights, delta_values[0])
     large = (key_cache, value_cache, out_weight)
-    attn, partial_out, place, weight_tile, delta, lengths = local_call(
+    attn, partial_out, place, sent, weight_tile, delta, lengths = local_call(
         decode_kernel,
         "decode",
         small + large,
         [
             shape((tile, HD), F32),
             shape(((blocks + 8) * seq_count, HD), F32),
+            shape((slots, HD), BF16),
             shape((slots, HD), BF16),
             shape((tile + 16, HD), F32),
             shape(delta_values.shape[1:], BF16),
@@ -497,11 +520,11 @@
     (outgoing,) = local_call(
         functools.partial(place_kernel, chips),
         "place",
-        (summed_tokens, attn, place),
+        (summed_tokens, attn, sent),
         [shape((wide_count * 3, lay, HD), BF16)],
         [pltpu.VMEM((wide_count * 2 * lay, HD), F32)],
     )
-    received = lax.all_to_all(outgoing, "wide", split_axis=0, concat_axis=0, tiled=True)
+    received = exchange_both_ways(outgoing)
 
     answer = seq_count + 1
     (answers,) = local_call(
@@ -515,7 +538,7 @@
             delta,
         ),
         [shape((wide_count * answer, HD), F32)],
-        [pltpu.VMEM((wide_count * tile, HD), F32)],
+        [pltpu.VMEM((wide_count * tile, HD), F32), pltpu.VMEM(received.shape, BF16)],
     )
     returned = lax.all_to_all(
         answers.reshape(wide_count, 1, answer * HD), "wide", split_axis=0, concat_axis=0, tiled=True

time: 91.5 us -> 91.3 us (level)
    all_to_all x1, blocking collectives: 27.9 us -> 24.1 us  [exchange_both_ways(): lax.all_to_all(x, AXES, split_axis=0, concat_axis=0, axis_index_groups=gr...]
    all_to_all x1, blocking collectives: 13.3 us -> 15.3 us  [per_device(): lax.all_to_all(merged.reshape(tp_count, 1, share * HD), ('th', 'tc'), spl...]
    all_to_all x1, blocking collectives: 16.9 us -> 18.4 us  [per_device(): lax.all_to_all(answers.reshape(wide_count, 1, answer * HD), 'wide', split...]
where the time goes in v8:
time: 91.3 us; the launch traced here: 90.9 us
  blocking collectives  57.8 us (63%)
  starting transfers between devices  13.4 us (15%)
  waiting for transfers between devices  9.59 us (11%)
  Pallas kernels  7.96 us (9%)
  between operations  1.41 us (2%)
    all_to_all x1, blocking collectives, exchange_both_ways(): lax.all_to_all(x, AXES, split_axis=0, concat_axis=0, axis_index_groups=gr...  24.1 us
    all_to_all x1, blocking collectives, per_device(): lax.all_to_all(answers.reshape(wide_count, 1, answer * HD), 'wide', split...  18.4 us
    all_to_all x1, blocking collectives, per_device(): lax.all_to_all(merged.reshape(tp_count, 1, share * HD), ('th', 'tc'), spl...  15.3 us
    ppermute x1, starting transfers between devices, per_device(): got = lax.ppermute(theirs, 'tc', [(0, 1), (1, 0)])  8.79 us
    all_to_all x1, waiting for transfers between devices, per_device(): lax.all_to_all(both.reshape(chips, message, HD), 'th', split_axis=0, conc...  8.56 us
    pallas_call x8, Pallas kernels, local_call(): pl.pallas_call(kernel, in_specs=[vmem] * kept + [hbm] * fetched, out_spec...  7.96 us
    all_to_all x1, starting transfers between devices, per_device(): lax.all_to_all(both.reshape(chips, message, HD), 'th', split_axis=0, conc...  4.65 us
  transfers between devices with their start and end apart: 2, of which 2 were waited for; matrix products, arithmetic and copies ran while one was open for 1% of the time, Pallas kernels for 3%

profile of v8, /device:TPU:1, one launch (start us, length us, event | category | flops | bytes accessed | tf_op | source)
XLA Modules:
  0.0 90.9 jit_solution(13644406496616849521)
XLA Ops:
  0.6 1.9 %project_theirs.1 = (f32[1056,128]{1,0:T(8,128)S(1)}, f32[32,128]{1,0:T(8,128)S(1)}, bf16[512,1024]{1,0:T(8,128)(2,1)S(1)}, bf16[1024,512]{1,0:T(8,128)(2,1)S(1)}) custom-call(bf16[512,1024]{1,0:T(8,128)(2,1)} %bitcast.22, bf16[1024,512]{1,0:T(8,128)(2,1)} %refs_1_.1), custom_call_target="tpu_custom_call" | custom-call | tf_op jit(solution)/shard_map/project_theirs/pallas_call | solution.py:54
  2.5 8.8 %collective-permute-start = (f32[1056,128]{1,0:T(8,128)S(1)}, f32[1056,128]{1,0:T(8,128)S(1)}, u32[]{:S(2)}, u32[]{:S(2)}) collective-permute-start(f32[1056,128]{1,0:T(8,128)S(1)} %get-tuple-element.18), channel_id=1, source_target_pairs={{0,1},{1,0},{2,3},{3,2},{4,5},{5,4},{6,7},{7,6},{8,9},{9,8},{10,11... | collective-permute-start | bytes 1622024 | tf_op jit(solution)/shard_map/ppermute | solution.py:476
  11.3 0.0 copy-start.2
  11.4 0.0 copy-start.3
  11.4 0.5 project_kept.1.a_ref
  11.9 1.0 %collective-permute-done.b_ref = f32[1056,128]{1,0:T(8,128)S(1)} collective-permute-done((f32[1056,128]{1,0:T(8,128)S(1)}, f32[1056,128]{1,0:T(8,128)S(1)}, u32[]{:S(2)}, u32[]{:S(2)}) %collective-permute-start) | collective-permute-done | bytes 540704 | tf_op jit(solution)/shard_map/ppermute | solution.py:476
  12.9 0.9 add.15
  13.7 4.6 %all-to-all-start = ((f32[4,264,128]{2,1,0:T(8,128)}), f32[4,264,128]{2,1,0:T(8,128)S(1)}, u32[]{:S(2)}, u32[]{:S(2)}) async-start(f32[4,264,128]{2,1,0:T(8,128)} %bitcast.1), calls=%async_computation | async-start | bytes 1081344 | tf_op jit(solution)/shard_map/all_to_all | solution.py:485
  18.4 0.0 copy-start
  19.1 0.1 pad.11.clone
  19.2 0.0 copy-done.2
  19.2 0.0 copy-done.3
  19.2 0.6 fusion.1.route_hbm
  19.8 2.2 %decode.1 = (f32[8,128]{1,0:T(8,128)S(1)}, f32[160,128]{1,0:T(8,128)S(1)}, bf16[128,128]{1,0:T(8,128)(2,1)S(1)}, bf16[128,128]{1,0:T(8,128)(2,1)S(1)}, f32[24,12...) custom-call(s32[4]{0:T(128)} %lens_hbm.1, bf16[4,256]{1,0:T(4,128)(2,1)} %q_hbm.1, ...), custom_call_target="tpu_custom_call" | custom-call | tf_op jit(solution)/shard_map/decode/pallas_call | solution.py:54
  22.1 8.6 %all-to-all-done = f32[4,264,128]{2,1,0:T(8,128)S(1)} async-done(((f32[4,264,128]{2,1,0:T(8,128)}), f32[4,264,128]{2,1,0:T(8,128)S(1)}, u32[]{:S(2)}, u32[]{:S(2)}) %all-to-all-start) | async-done | bytes 540704 | tf_op jit(solution)/shard_map/all_to_all | solution.py:485
  30.6 0.4 place.1
  31.0 24.1 %all_to_all.20.x_ref = bf16[192,8,128]{2,1,0:T(8,128)(2,1)S(1)} all-to-all(bf16[192,8,128]{2,1,0:T(8,128)(2,1)S(1)} %place.1), channel_id=1, replica_groups={{0,8,16,24,32,40,48,56,64,72,80,88,96,104,112,120,128,136,144,152,160,1..., dimensions={0} | all-to-all | bytes 786432 | tf_op jit(solution)/shard_map/all_to_all | solution.py:150
  55.1 0.0 copy-done
  55.1 0.0 copy-done.1
  55.1 1.2 %score.1 = f32[320,128]{1,0:T(8,128)S(1)} custom-call(bf16[192,8,128]{2,1,0:T(8,128)(2,1)S(1)} %all_to_all.20.x_ref, bf16[1024,128]{1,0:T(8,128)(2,1)S(1)} %bitcast.20, bf16[1024,128]{1,0:T(8,128)(2,1)S(1)} %bitcast.21, f32[24,128]{1,0:T(8,128)S(1)} %get-tuple-element.21.weight_ref, bf16[128,128]{1,0:T(8,128)(2,1)S(1)} %get-tuple-element.22.delta_ref), custom_call_target="tpu_custom_call" | custom-call | tf_op jit(solution)/shard_map/score/pallas_call | solution.py:54
  56.4 18.4 %all_to_all.21 = f32[64,1,640]{2,1,0:T(1,128)S(1)} all-to-all(f32[64,1,640]{2,1,0:T(1,128)S(1)} %bitcast.16), channel_id=1, replica_groups=mesh['wide'=64,'th'=4,'tc'=2] {'wide'}, dimensions={0} | all-to-all | bytes 327680 | tf_op jit(solution)/shard_map/all_to_all | solution.py:543
  74.8 0.2 merge.1
  75.0 15.3 %all_to_all.22 = f32[8,1,2304]{2,1,0:T(1,128)S(1)} all-to-all(f32[8,1,2304]{2,1,0:T(1,128)S(1)} %bitcast.19), channel_id=1, replica_groups=mesh['wide'=64,'th'=4,'tc'=2] {'th','tc'}, dimensions={0} | all-to-all | bytes 147456 | tf_op jit(solution)/shard_map/all_to_all | solution.py:554
  90.3 0.6 final.1
  (1 shorter events, 0.0 us)
Async XLA Ops:
  2.5 10.3 %collective-permute-start = (f32[1056,128]{1,0:T(8,128)S(1)}, f32[1056,128]{1,0:T(8,128)S(1)}, u32[]{:S(2)}, u32[]{:S(2)}) collective-permute-start(f32[1056,128]{1,0:T(8,128)S(1)} %get-tuple-element.18), channel_id=1, source_target_pairs={{0,1},{1,0},{2,3},{3,2},{4,5},{5,4},{6,7},{7,6},{8,9},{9,8},{10,11... | collective-permute-start | bytes 1622024 | tf_op jit(solution)/shard_map/ppermute | solution.py:476
  11.3 7.8 %copy-start.2 = (s32[64]{0:T(128)S(1)}, s32[64]{0:T(128)}, u32[]{:S(2)}) copy-start(s32[64]{0:T(128)} %param.26) | copy-start | bytes 772
  11.4 7.8 %copy-start.3 = (s32[64,1]{0,1:T(1,128)S(1)}, s32[64,1]{0,1:T(1,128)}, u32[]{:S(2)}) copy-start(s32[64,1]{0,1:T(1,128)} %param.25) | copy-start | bytes 772
  13.7 16.9 %all-to-all-start = ((f32[4,264,128]{2,1,0:T(8,128)}), f32[4,264,128]{2,1,0:T(8,128)S(1)}, u32[]{:S(2)}, u32[]{:S(2)}) async-start(f32[4,264,128]{2,1,0:T(8,128)} %bitcast.1), calls=%async_computation | async-start | bytes 1081344 | tf_op jit(solution)/shard_map/all_to_all | solution.py:485
  18.4 36.7 %copy-start = (bf16[1,1024,128]{2,1,0:T(8,128)(2,1)S(1)}, bf16[1,1024,128]{2,1,0:T(8,128)(2,1)}, u32[]{:S(2)}) copy-start(bf16[1,1024,128]{2,1,0:T(8,128)(2,1)} %param.29) | copy-start | bytes 786436
  18.4 36.7 %copy-start.1 = (bf16[1,1024,128]{2,1,0:T(8,128)(2,1)S(1)}, bf16[1,1024,128]{2,1,0:T(8,128)(2,1)}, u32[]{:S(2)}) copy-start(bf16[1,1024,128]{2,1,0:T(8,128)(2,1)} %param.30) | copy-start | bytes 786436

commit v9 on v8

--- a/solution.py
+++ b/solution.py
@@ -146,7 +146,7 @@
     for core in range(cores):
         for chip in range(chips):
             group = [(w * chips + chip) * cores + core for w in range(wide_count)]
-            groups.append(group if core == 0 else group[::-1])
+            groups.append(group if core == 1 else group[::-1])
     return lax.all_to_all(
         x, AXES, split_axis=0, concat_axis=0, axis_index_groups=groups, tiled=True
     )
@@ -258,7 +258,7 @@
     order = (slot // groups).astype(F32)
     held = jnp.logical_and(route == group, rank == order)
     place_ref[...] = jnp.where(held, 1.0, 0.0).astype(BF16)
-    sent = jnp.where(lax.axis_index("tc") == 0, group, groups - 1 - group)
+    sent = jnp.where(lax.axis_index("tc") == 1, group, groups - 1 - group)
     held = jnp.logical_and(route == sent, rank == order)
     sent_ref[...] = jnp.where(held, 1.0, 0.0).astype(BF16)
     weight = score_ref[...].astype(F32)
@@ -331,7 +331,7 @@
     row = lax.broadcasted_iota(jnp.int32, (1, tile, HD), 1)
     core = lax.axis_index("tc")
     for w in range(senders):
-        came = jnp.where(core == 0, w, senders - 1 - w)
+        came = jnp.where(core == 1, w, senders - 1 - w)
         for k in range(3):
             in_order_ref[3 * w + k] = x_ref[3 * came + k]
     started = []

time: 91.3 us -> 91.2 us (level)
    all_to_all x1, blocking collectives: 24.1 us -> 30 us  [exchange_both_ways(): lax.all_to_all(x, AXES, split_axis=0, concat_axis=0, axis_index_groups=gr...]
    all_to_all x1, blocking collectives: 18.4 us -> 15.3 us  [per_device(): lax.all_to_all(answers.reshape(wide_count, 1, answer * HD), 'wide', split...]
    all_to_all x1, blocking collectives: 15.3 us -> 12.4 us  [per_device(): lax.all_to_all(merged.reshape(tp_count, 1, share * HD), ('th', 'tc'), spl...]
where the time goes in v9:
time: 91.2 us; the launch traced here: 90.8 us
  blocking collectives  57.7 us (63%)
  starting transfers between devices  13.4 us (15%)
  waiting for transfers between devices  9.59 us (11%)
  Pallas kernels  7.96 us (9%)
  between operations  1.41 us (2%)
    all_to_all x1, blocking collectives, exchange_both_ways(): lax.all_to_all(x, AXES, split_axis=0, concat_axis=0, axis_index_groups=gr...  30 us
    all_to_all x1, blocking collectives, per_device(): lax.all_to_all(answers.reshape(wide_count, 1, answer * HD), 'wide', split...  15.3 us
    all_to_all x1, blocking collectives, per_device(): lax.all_to_all(merged.reshape(tp_count, 1, share * HD), ('th', 'tc'), spl...  12.4 us
    ppermute x1, starting transfers between devices, per_device(): got = lax.ppermute(theirs, 'tc', [(0, 1), (1, 0)])  8.79 us
    all_to_all x1, waiting for transfers between devices, per_device(): lax.all_to_all(both.reshape(chips, message, HD), 'th', split_axis=0, conc...  8.56 us
    pallas_call x8, Pallas kernels, local_call(): pl.pallas_call(kernel, in_specs=[vmem] * kept + [hbm] * fetched, out_spec...  7.96 us
    all_to_all x1, starting transfers between devices, per_device(): lax.all_to_all(both.reshape(chips, message, HD), 'th', split_axis=0, conc...  4.65 us
  transfers between devices with their start and end apart: 2, of which 2 were waited for; matrix products, arithmetic and copies ran while one was open for 1% of the time, Pallas kernels for 3%

profile of v9, /device:TPU:1, one launch (start us, length us, event | category | flops | bytes accessed | tf_op | source)
XLA Modules:
  0.0 90.8 jit_solution(10646163045184400263)
XLA Ops:
  0.6 1.9 %project_theirs.1 = (f32[1056,128]{1,0:T(8,128)S(1)}, f32[32,128]{1,0:T(8,128)S(1)}, bf16[512,1024]{1,0:T(8,128)(2,1)S(1)}, bf16[1024,512]{1,0:T(8,128)(2,1)S(1)}) custom-call(bf16[512,1024]{1,0:T(8,128)(2,1)} %bitcast.22, bf16[1024,512]{1,0:T(8,128)(2,1)} %refs_1_.1), custom_call_target="tpu_custom_call" | custom-call | tf_op jit(solution)/shard_map/project_theirs/pallas_call | solution.py:54
  2.5 8.8 %collective-permute-start = (f32[1056,128]{1,0:T(8,128)S(1)}, f32[1056,128]{1,0:T(8,128)S(1)}, u32[]{:S(2)}, u32[]{:S(2)}) collective-permute-start(f32[1056,128]{1,0:T(8,128)S(1)} %get-tuple-element.18), channel_id=1, source_target_pairs={{0,1},{1,0},{2,3},{3,2},{4,5},{5,4},{6,7},{7,6},{8,9},{9,8},{10,11... | collective-permute-start | bytes 1622024 | tf_op jit(solution)/shard_map/ppermute | solution.py:476
  11.3 0.0 copy-start.2
  11.4 0.0 copy-start.3
  11.4 0.5 project_kept.1.a_ref
  11.9 1.0 %collective-permute-done.b_ref = f32[1056,128]{1,0:T(8,128)S(1)} collective-permute-done((f32[1056,128]{1,0:T(8,128)S(1)}, f32[1056,128]{1,0:T(8,128)S(1)}, u32[]{:S(2)}, u32[]{:S(2)}) %collective-permute-start) | collective-permute-done | bytes 540704 | tf_op jit(solution)/shard_map/ppermute | solution.py:476
  12.9 0.9 add.15
  13.7 4.6 %all-to-all-start = ((f32[4,264,128]{2,1,0:T(8,128)}), f32[4,264,128]{2,1,0:T(8,128)S(1)}, u32[]{:S(2)}, u32[]{:S(2)}) async-start(f32[4,264,128]{2,1,0:T(8,128)} %bitcast.1), calls=%async_computation | async-start | bytes 1081344 | tf_op jit(solution)/shard_map/all_to_all | solution.py:485
  18.4 0.0 copy-start.1
  19.1 0.1 pad.11.clone
  19.2 0.0 copy-done.2
  19.2 0.0 copy-done.3
  19.2 0.6 fusion.1.route_hbm
  19.8 2.2 %decode.1 = (f32[8,128]{1,0:T(8,128)S(1)}, f32[160,128]{1,0:T(8,128)S(1)}, bf16[128,128]{1,0:T(8,128)(2,1)S(1)}, bf16[128,128]{1,0:T(8,128)(2,1)S(1)}, f32[24,12...) custom-call(s32[4]{0:T(128)} %lens_hbm.1, bf16[4,256]{1,0:T(4,128)(2,1)} %q_hbm.1, ...), custom_call_target="tpu_custom_call" | custom-call | tf_op jit(solution)/shard_map/decode/pallas_call | solution.py:54
  22.1 8.6 %all-to-all-done = f32[4,264,128]{2,1,0:T(8,128)S(1)} async-done(((f32[4,264,128]{2,1,0:T(8,128)}), f32[4,264,128]{2,1,0:T(8,128)S(1)}, u32[]{:S(2)}, u32[]{:S(2)}) %all-to-all-start) | async-done | bytes 540704 | tf_op jit(solution)/shard_map/all_to_all | solution.py:485
  30.6 0.4 place.1
  31.0 30.0 %all_to_all.20.x_ref = bf16[192,8,128]{2,1,0:T(8,128)(2,1)S(1)} all-to-all(bf16[192,8,128]{2,1,0:T(8,128)(2,1)S(1)} %place.1), channel_id=1, replica_groups={{504,496,488,480,472,464,456,448,440,432,424,416,408,400,392,384,376,36..., dimensions={0} | all-to-all | bytes 786432 | tf_op jit(solution)/shard_map/all_to_all | solution.py:150
  61.0 0.0 copy-done
  61.0 0.0 copy-done.1
  61.0 1.2 %score.1 = f32[320,128]{1,0:T(8,128)S(1)} custom-call(bf16[192,8,128]{2,1,0:T(8,128)(2,1)S(1)} %all_to_all.20.x_ref, bf16[1024,128]{1,0:T(8,128)(2,1)S(1)} %bitcast.20, bf16[1024,128]{1,0:T(8,128)(2,1)S(1)} %bitcast.21, f32[24,128]{1,0:T(8,128)S(1)} %get-tuple-element.21.weight_ref, bf16[128,128]{1,0:T(8,128)(2,1)S(1)} %get-tuple-element.22.delta_ref), custom_call_target="tpu_custom_call" | custom-call | tf_op jit(solution)/shard_map/score/pallas_call | solution.py:54
  62.2 15.3 %all_to_all.21 = f32[64,1,640]{2,1,0:T(1,128)S(1)} all-to-all(f32[64,1,640]{2,1,0:T(1,128)S(1)} %bitcast.16), channel_id=1, replica_groups=mesh['wide'=64,'th'=4,'tc'=2] {'wide'}, dimensions={0} | all-to-all | bytes 327680 | tf_op jit(solution)/shard_map/all_to_all | solution.py:543
  77.6 0.2 merge.1
  77.8 12.4 %all_to_all.22 = f32[8,1,2304]{2,1,0:T(1,128)S(1)} all-to-all(f32[8,1,2304]{2,1,0:T(1,128)S(1)} %bitcast.19), channel_id=1, replica_groups=mesh['wide'=64,'th'=4,'tc'=2] {'th','tc'}, dimensions={0} | all-to-all | bytes 147456 | tf_op jit(solution)/shard_map/all_to_all | solution.py:554
  90.2 0.6 final.1
  (1 shorter events, 0.0 us)
Async XLA Ops:
  2.5 10.3 %collective-permute-start = (f32[1056,128]{1,0:T(8,128)S(1)}, f32[1056,128]{1,0:T(8,128)S(1)}, u32[]{:S(2)}, u32[]{:S(2)}) collective-permute-start(f32[1056,128]{1,0:T(8,128)S(1)} %get-tuple-element.18), channel_id=1, source_target_pairs={{0,1},{1,0},{2,3},{3,2},{4,5},{5,4},{6,7},{7,6},{8,9},{9,8},{10,11... | collective-permute-start | bytes 1622024 | tf_op jit(solution)/shard_map/ppermute | solution.py:476
  11.3 7.8 %copy-start.2 = (s32[64]{0:T(128)S(1)}, s32[64]{0:T(128)}, u32[]{:S(2)}) copy-start(s32[64]{0:T(128)} %param.26) | copy-start | bytes 772
  11.4 7.8 %copy-start.3 = (s32[64,1]{0,1:T(1,128)S(1)}, s32[64,1]{0,1:T(1,128)}, u32[]{:S(2)}) copy-start(s32[64,1]{0,1:T(1,128)} %param.25) | copy-start | bytes 772
  13.7 16.9 %all-to-all-start = ((f32[4,264,128]{2,1,0:T(8,128)}), f32[4,264,128]{2,1,0:T(8,128)S(1)}, u32[]{:S(2)}, u32[]{:S(2)}) async-start(f32[4,264,128]{2,1,0:T(8,128)} %bitcast.1), calls=%async_computation | async-start | bytes 1081344 | tf_op jit(solution)/shard_map/all_to_all | solution.py:485
  18.4 42.6 %copy-start = (bf16[1,1024,128]{2,1,0:T(8,128)(2,1)S(1)}, bf16[1,1024,128]{2,1,0:T(8,128)(2,1)}, u32[]{:S(2)}) copy-start(bf16[1,1024,128]{2,1,0:T(8,128)(2,1)} %param.29) | copy-start | bytes 786436
  18.4 42.6 %copy-start.1 = (bf16[1,1024,128]{2,1,0:T(8,128)(2,1)S(1)}, bf16[1,1024,128]{2,1,0:T(8,128)(2,1)}, u32[]{:S(2)}) copy-start(bf16[1,1024,128]{2,1,0:T(8,128)(2,1)} %param.30) | copy-start | bytes 786436

commit v10 on v9

--- a/solution.py
+++ b/solution.py
@@ -333,12 +333,11 @@
     for w in range(senders):
         came = jnp.where(core == 1, w, senders - 1 - w)
         for k in range(3):
-            in_order_ref[3 * w + k] = x_ref[3 * came + k]
+            in_order_ref[k, w * tile : (w + 1) * tile, :] = x_ref[3 * came + k].astype(F32)
     started = []
     for first in range(0, senders, at_once):
-        x = in_order_ref[3 * first : 3 * (first + at_once)].astype(F32)
-        x = x.reshape(at_once, 3, tile, HD)
-        flat = [x[:, k].reshape(at_once * tile, HD).astype(BF16) for k in range(3)]
+        span = slice(first * tile, (first + at_once) * tile)
+        flat = [in_order_ref[k, span, :].astype(BF16) for k in range(3)]
         scores = mm_t(jnp.concatenate(flat[:2], axis=1), keys2)
         started.append((first, scores, mm(flat[2], delta)))
     for first, scores, product in started:
@@ -538,7 +537,7 @@
             delta,
         ),
         [shape((wide_count * answer, HD), F32)],
-        [pltpu.VMEM((wide_count * tile, HD), F32), pltpu.VMEM(received.shape, BF16)],
+        [pltpu.VMEM((wide_count * tile, HD), F32), pltpu.VMEM((3, wide_count * tile, HD), F32)],
     )
     returned = lax.all_to_all(
         answers.reshape(wide_count, 1, answer * HD), "wide", split_axis=0, concat_axis=0, tiled=True

time: 91.2 us -> 91.2 us (level)
  no operation moved by 1% of the time
where the time goes in v10:
time: 91.2 us; the launch traced here: 90.8 us
  blocking collectives  57.7 us (63%)
  starting transfers between devices  13.4 us (15%)
  waiting for transfers between devices  9.59 us (11%)
  Pallas kernels  7.94 us (9%)
  between operations  1.41 us (2%)
    all_to_all x1, blocking collectives, exchange_both_ways(): lax.all_to_all(x, AXES, split_axis=0, concat_axis=0, axis_index_groups=gr...  30 us
    all_to_all x1, blocking collectives, per_device(): lax.all_to_all(answers.reshape(wide_count, 1, answer * HD), 'wide', split...  15.4 us
    all_to_all x1, blocking collectives, per_device(): lax.all_to_all(merged.reshape(tp_count, 1, share * HD), ('th', 'tc'), spl...  12.3 us
    ppermute x1, starting transfers between devices, per_device(): got = lax.ppermute(theirs, 'tc', [(0, 1), (1, 0)])  8.79 us
    all_to_all x1, waiting for transfers between devices, per_device(): lax.all_to_all(both.reshape(chips, message, HD), 'th', split_axis=0, conc...  8.56 us
    pallas_call x8, Pallas kernels, local_call(): pl.pallas_call(kernel, in_specs=[vmem] * kept + [hbm] * fetched, out_spec...  7.94 us
    all_to_all x1, starting transfers between devices, per_device(): lax.all_to_all(both.reshape(chips, message, HD), 'th', split_axis=0, conc...  4.65 us
  transfers between devices with their start and end apart: 2, of which 2 were waited for; matrix products, arithmetic and copies ran while one was open for 1% of the time, Pallas kernels for 3%

profile of v10, /device:TPU:1, one launch (start us, length us, event | category | flops | bytes accessed | tf_op | source)
XLA Modules:
  0.0 90.8 jit_solution(16411101574082969779)
XLA Ops:
  0.6 1.9 %project_theirs.1 = (f32[1056,128]{1,0:T(8,128)S(1)}, f32[32,128]{1,0:T(8,128)S(1)}, bf16[512,1024]{1,0:T(8,128)(2,1)S(1)}, bf16[1024,512]{1,0:T(8,128)(2,1)S(1)}) custom-call(bf16[512,1024]{1,0:T(8,128)(2,1)} %bitcast.22, bf16[1024,512]{1,0:T(8,128)(2,1)} %refs_1_.1), custom_call_target="tpu_custom_call" | custom-call | tf_op jit(solution)/shard_map/project_theirs/pallas_call | solution.py:54
  2.5 8.8 %collective-permute-start = (f32[1056,128]{1,0:T(8,128)S(1)}, f32[1056,128]{1,0:T(8,128)S(1)}, u32[]{:S(2)}, u32[]{:S(2)}) collective-permute-start(f32[1056,128]{1,0:T(8,128)S(1)} %get-tuple-element.18), channel_id=1, source_target_pairs={{0,1},{1,0},{2,3},{3,2},{4,5},{5,4},{6,7},{7,6},{8,9},{9,8},{10,11... | collective-permute-start | bytes 1622024 | tf_op jit(solution)/shard_map/ppermute | solution.py:475
  11.3 0.0 copy-start.2
  11.4 0.0 copy-start.3
  11.4 0.5 project_kept.1.a_ref
  11.9 1.0 %collective-permute-done.b_ref = f32[1056,128]{1,0:T(8,128)S(1)} collective-permute-done((f32[1056,128]{1,0:T(8,128)S(1)}, f32[1056,128]{1,0:T(8,128)S(1)}, u32[]{:S(2)}, u32[]{:S(2)}) %collective-permute-start) | collective-permute-done | bytes 540704 | tf_op jit(solution)/shard_map/ppermute | solution.py:475
  12.9 0.9 add.15
  13.7 4.6 %all-to-all-start = ((f32[4,264,128]{2,1,0:T(8,128)}), f32[4,264,128]{2,1,0:T(8,128)S(1)}, u32[]{:S(2)}, u32[]{:S(2)}) async-start(f32[4,264,128]{2,1,0:T(8,128)} %bitcast.1), calls=%async_computation | async-start | bytes 1081344 | tf_op jit(solution)/shard_map/all_to_all | solution.py:484
  18.4 0.0 copy-start.1
  19.1 0.1 pad.11.clone
  19.2 0.0 copy-done.2
  19.2 0.0 copy-done.3
  19.2 0.6 fusion.1.route_hbm
  19.8 2.2 %decode.1 = (f32[8,128]{1,0:T(8,128)S(1)}, f32[160,128]{1,0:T(8,128)S(1)}, bf16[128,128]{1,0:T(8,128)(2,1)S(1)}, bf16[128,128]{1,0:T(8,128)(2,1)S(1)}, f32[24,12...) custom-call(s32[4]{0:T(128)} %lens_hbm.1, bf16[4,256]{1,0:T(4,128)(2,1)} %q_hbm.1, ...), custom_call_target="tpu_custom_call" | custom-call | tf_op jit(solution)/shard_map/decode/pallas_call | solution.py:54
  22.1 8.6 %all-to-all-done = f32[4,264,128]{2,1,0:T(8,128)S(1)} async-done(((f32[4,264,128]{2,1,0:T(8,128)}), f32[4,264,128]{2,1,0:T(8,128)S(1)}, u32[]{:S(2)}, u32[]{:S(2)}) %all-to-all-start) | async-done | bytes 540704 | tf_op jit(solution)/shard_map/all_to_all | solution.py:484
  30.6 0.4 place.1
  31.0 30.0 %all_to_all.20.x_ref = bf16[192,8,128]{2,1,0:T(8,128)(2,1)S(1)} all-to-all(bf16[192,8,128]{2,1,0:T(8,128)(2,1)S(1)} %place.1), channel_id=1, replica_groups={{504,496,488,480,472,464,456,448,440,432,424,416,408,400,392,384,376,36..., dimensions={0} | all-to-all | bytes 786432 | tf_op jit(solution)/shard_map/all_to_all | solution.py:150
  61.0 0.0 copy-done
  61.0 0.0 copy-done.1
  61.0 1.2 %score.1 = f32[320,128]{1,0:T(8,128)S(1)} custom-call(bf16[192,8,128]{2,1,0:T(8,128)(2,1)S(1)} %all_to_all.20.x_ref, bf16[1024,128]{1,0:T(8,128)(2,1)S(1)} %bitcast.20, bf16[1024,128]{1,0:T(8,128)(2,1)S(1)} %bitcast.21, f32[24,128]{1,0:T(8,128)S(1)} %get-tuple-element.21.weight_ref, bf16[128,128]{1,0:T(8,128)(2,1)S(1)} %get-tuple-element.22.delta_ref), custom_call_target="tpu_custom_call" | custom-call | tf_op jit(solution)/shard_map/score/pallas_call | solution.py:54
  62.2 15.4 %all_to_all.21 = f32[64,1,640]{2,1,0:T(1,128)S(1)} all-to-all(f32[64,1,640]{2,1,0:T(1,128)S(1)} %bitcast.16), channel_id=1, replica_groups=mesh['wide'=64,'th'=4,'tc'=2] {'wide'}, dimensions={0} | all-to-all | bytes 327680 | tf_op jit(solution)/shard_map/all_to_all | solution.py:542
  77.6 0.2 merge.1
  77.8 12.3 %all_to_all.22 = f32[8,1,2304]{2,1,0:T(1,128)S(1)} all-to-all(f32[8,1,2304]{2,1,0:T(1,128)S(1)} %bitcast.19), channel_id=1, replica_groups=mesh['wide'=64,'th'=4,'tc'=2] {'th','tc'}, dimensions={0} | all-to-all | bytes 147456 | tf_op jit(solution)/shard_map/all_to_all | solution.py:553
  90.2 0.6 final.1
  (1 shorter events, 0.0 us)
Async XLA Ops:
  2.5 10.3 %collective-permute-start = (f32[1056,128]{1,0:T(8,128)S(1)}, f32[1056,128]{1,0:T(8,128)S(1)}, u32[]{:S(2)}, u32[]{:S(2)}) collective-permute-start(f32[1056,128]{1,0:T(8,128)S(1)} %get-tuple-element.18), channel_id=1, source_target_pairs={{0,1},{1,0},{2,3},{3,2},{4,5},{5,4},{6,7},{7,6},{8,9},{9,8},{10,11... | collective-permute-start | bytes 1622024 | tf_op jit(solution)/shard_map/ppermute | solution.py:475
  11.3 7.8 %copy-start.2 = (s32[64]{0:T(128)S(1)}, s32[64]{0:T(128)}, u32[]{:S(2)}) copy-start(s32[64]{0:T(128)} %param.26) | copy-start | bytes 772
  11.4 7.8 %copy-start.3 = (s32[64,1]{0,1:T(1,128)S(1)}, s32[64,1]{0,1:T(1,128)}, u32[]{:S(2)}) copy-start(s32[64,1]{0,1:T(1,128)} %param.25) | copy-start | bytes 772
  13.7 16.9 %all-to-all-start = ((f32[4,264,128]{2,1,0:T(8,128)}), f32[4,264,128]{2,1,0:T(8,128)S(1)}, u32[]{:S(2)}, u32[]{:S(2)}) async-start(f32[4,264,128]{2,1,0:T(8,128)} %bitcast.1), calls=%async_computation | async-start | bytes 1081344 | tf_op jit(solution)/shard_map/all_to_all | solution.py:484
  18.4 42.6 %copy-start = (bf16[1,1024,128]{2,1,0:T(8,128)(2,1)S(1)}, bf16[1,1024,128]{2,1,0:T(8,128)(2,1)}, u32[]{:S(2)}) copy-start(bf16[1,1024,128]{2,1,0:T(8,128)(2,1)} %param.29) | copy-start | bytes 786436
  18.4 42.6 %copy-start.1 = (bf16[1,1024,128]{2,1,0:T(8,128)(2,1)S(1)}, bf16[1,1024,128]{2,1,0:T(8,128)(2,1)}, u32[]{:S(2)}) copy-start(bf16[1,1024,128]{2,1,0:T(8,128)(2,1)} %param.30) | copy-start | bytes 786436
